TPU v7x, 32 devices: a whole 2x2x4 slice. The times are simulated.
32 devices in a mesh: seq: 16 (over z, y, core), ch: 2 (over x).
Axes of the slice: x: 2, y: 2, z: 4, core: 2. Of those that a mesh axis runs over, the one named last changes fastest.
Arguments:
- gate_in: bfloat16 [4096, 4096], P('seq', 'ch'), may hold values from -80 to 80
- key_in: bfloat16 [4096, 4096], P('seq', 'ch'), may hold values from -6 to 6
- value_in: bfloat16 [4096, 4096], P('seq', 'ch'), may hold values from -6 to 6
- long_filter: bfloat16 [4096, 4096], P('seq', 'ch'), may hold values from -2 to 2
- gate_short: float32 [3, 4096], P(None, 'ch'), may hold values from -3 to 3
- key_short: float32 [3, 4096], P(None, 'ch'), may hold values from -3 to 3
- value_short: float32 [3, 4096], P(None, 'ch'), may hold values from -3 to 3
- skip_gain: float32 [4096], P('ch'), may hold values from 0.5 to 1.5
- norm_gain: float32 [4096], P('ch'), may hold values from 0.5 to 1.5
Outputs:
- mixed: bfloat16 [4096, 4096], P('seq', 'ch')
All inputs are finite; a program needn't handle non-finite values.
Results may differ from a plain program's by a relative error of at most 0.0057.
Values may be sent and summed in bfloat16 or wider, within the bound.
No kernel may reach another device: no remote copies, remote signals or barrier semaphores. Data moves between devices by JAX's collectives and lax.ppermute only.
A program may use at most 128 MiB of HBM per device.

v0:
```python
import functools

import jax
import jax.numpy as jnp
from jax import lax
from jax.experimental import pallas as pl
from jax.experimental.pallas import tpu as pltpu
from jax.sharding import PartitionSpec as P

LANES = 128
FINE = 32
GROUP = 4
HALO = 16
WIDE = 512
PARTS = 2
NEAR = 4
VMEM_BYTES = 20 * 1024 * 1024
F32 = jnp.float32
BF16 = jnp.bfloat16


def passed_along(array, axis, by):
    size = lax.axis_size(axis)
    pairs = [(i, i + by) for i in range(size) if 0 <= i + by < size]
    return lax.ppermute(array, axis, pairs)


def short_conv(rows, prev, taps):
    last = prev[HALO - 1 : HALO]
    before = prev[HALO - 2 : HALO - 1]
    at = lax.broadcasted_iota(jnp.int32, rows.shape, 0)
    one = jnp.where(at == 0, last, pltpu.roll(rows, 1, 0))
    two = jnp.where(at == 0, before, jnp.where(at == 1, last, pltpu.roll(rows, 2, 0)))
    return taps[0:1] * rows + taps[1:2] * one + taps[2:3] * two


def send_out(held, outs, origin):
    for near, out_ref in enumerate(outs):
        for far in range(out_ref.shape[0]):
            out_ref[far] = held[origin ^ (far * len(outs) + near)]


def pack_kernel(wants, at_ref, *refs):
    refs, outs, held = refs[: -NEAR - 1], refs[-NEAR - 1 : -1], refs[-1]
    blocks, _, narrow, tok = held.shape
    count = WIDE // narrow
    step = pl.program_id(0)
    here = pl.ds(step * count, count)
    refs = list(refs)
    for at, want in enumerate(wants):
        if want == "filter":
            packed = refs.pop(0)[...].astype(F32)
        else:
            key, value, halo, key_taps, value_taps = [refs.pop(0)[...] for _ in range(5)]
            halo = halo.astype(F32)
            packed = short_conv(key.astype(F32), halo[:HALO], key_taps)
            packed *= short_conv(value.astype(F32), halo[HALO : 2 * HALO], value_taps)
        held[here, at] = packed.T.astype(BF16).reshape(count, narrow, tok)

    @pl.when(step == pl.num_programs(0) - 1)
    def _():
        for near, out_ref in enumerate(outs):
            for far in range(blocks // NEAR):
                out_ref[far] = held[at_ref[0] ^ (far * NEAR + near)]


def packed(wants, arrays, part, position):
    start, narrow, blocks = part
    tok = arrays[0].shape[0]
    first = start // WIDE
    shape = (blocks // NEAR, len(wants), narrow, tok)
    return pl.pallas_call(
        functools.partial(pack_kernel, wants),
        grid_spec=pltpu.PrefetchScalarGridSpec(
            num_scalar_prefetch=1,
            grid=(blocks * narrow // WIDE,),
            in_specs=[
                pl.BlockSpec((array.shape[0], WIDE), lambda i, at: (0, first + i))
                for array in arrays
            ],
            out_specs=[pl.BlockSpec(shape, lambda i, at: (0, 0, 0, 0))] * NEAR,
            scratch_shapes=[pltpu.VMEM((blocks,) + shape[1:], BF16)],
        ),
        out_shape=[jax.ShapeDtypeStruct(shape, BF16)] * NEAR,
        compiler_params=pltpu.CompilerParams(vmem_limit_bytes=VMEM_BYTES),
        cost_estimate=pl.CostEstimate(
            flops=8 * len(arrays) * tok * blocks * narrow,
            bytes_accessed=4 * len(arrays) * tok * blocks * narrow,
            transcendentals=0,
        ),
        name="pack_" + "_".join(wants),
    )(position, *arrays)


def swapped(rows, by):
    size = lax.axis_size("seq")
    return lax.ppermute(rows, "seq", [(i, i ^ by) for i in range(size)])


def swap_near(parts):
    parts = [parts[0]] + [swapped(parts[i], i) for i in range(1, len(parts))]
    return [jnp.stack([part[j] for part in parts]) for j in range(parts[0].shape[0])]


def swap_far(lines):
    return [lines[0]] + [swapped(lines[j], NEAR * j) for j in range(1, len(lines))]


def swap_back(lines):
    lines = swap_far(lines)
    parts = [jnp.stack([line[i] for line in lines]) for i in range(NEAR)]
    return [parts[0]] + [swapped(parts[i], i) for i in range(1, NEAR)]


def delayed(rows, by):
    at = lax.broadcasted_iota(jnp.int32, rows.shape, 1)
    return jnp.where(at < by, 0.0, pltpu.roll(rows, by, 1))


def halves(first, second, upper):
    return (
        jnp.where(upper, first, pltpu.roll(second, 4, second.ndim - 2)),
        jnp.where(upper, pltpu.roll(first, 4, first.ndim - 2), second),
    )


def left_rows(pairs, turns):
    tok = pairs.shape[1]
    lane_of = lax.broadcasted_iota(jnp.int32, (turns * 8, LANES), 1) // FINE
    own = lane_of == lax.broadcasted_iota(jnp.int32, (turns * 8, LANES), 0) % GROUP
    columns = []
    for a in range(tok // LANES):
        piece = pairs[:, a * LANES : (a + 1) * LANES]
        moved = [piece] + [pltpu.roll(piece, FINE * d, 1) for d in range(1, 4)]
        picked = []
        for e in range(LANES // FINE):
            spread = moved[(3 - e) % 4]
            for c in range(3):
                spread = jnp.where(lane_of == c, moved[(c - e) % 4], spread)
            picked.append(jnp.where(own, spread, 0.0).reshape(turns, 1, 8, LANES))
        columns.append(jnp.concatenate(picked, axis=1).reshape(turns * 32, LANES).astype(BF16))
    return jnp.concatenate(columns, axis=1)


def conv_kernel(at_ref, skip_ref, *refs):
    refs, (filt, prod, base, left, total, held) = refs[:-6], refs[-6:]
    blocks, lanes, tok = prod.shape
    far = blocks // NEAR
    in_refs, out_refs = refs[:-far], refs[-far:]
    length = blocks * tok
    turns = blocks // 2
    units = lanes // 16

    merged = in_refs[0].shape[1] == 2
    for j in range(far):
        for i in range(NEAR):
            block = at_ref[0] ^ (NEAR * j + i)
            lags = pl.ds(pl.multiple_of(block * tok, tok), tok)
            filt[:, lags] = in_refs[j][i, 0].astype(F32)
            prod[block] = (in_refs[j][i, 1] if merged else in_refs[far + j][i, 0]).astype(F32)
    base[:, :, :LANES] = jnp.zeros((2, GROUP * FINE, LANES), BF16)

    def pairs_of(row, side):
        rows = prod[:, pl.ds(pl.multiple_of(row, 8), 8), :].reshape(turns, 2, 8, tok)
        upper = lax.broadcasted_iota(jnp.int32, (turns, 8, tok), 1) < 4
        return halves(rows[:, 0], rows[:, 1], upper)[side].reshape(turns * 8, tok)

    def build_left(row, side):
        left[side] = left_rows(pairs_of(row, side), turns)

    def build_base(row, side, c, pair):
        line = jnp.broadcast_to(filt[pl.ds(row + side * GROUP + c, 1), :], (8, length))
        steps = []
        for a in (2 * pair, 2 * pair + 1):
            shifted = pltpu.roll(line, 8 * a, 1, stride=1, stride_axis=0)
            late = lax.broadcasted_iota(
                jnp.int32, (8, LANES), 1
            ) >= 8 * a + lax.broadcasted_iota(jnp.int32, (8, LANES), 0)
            steps.append(
                jnp.concatenate(
                    [jnp.where(late, shifted[:, :LANES], 0.0), shifted[:, LANES:]], axis=1
                )
            )
        at = c * FINE + 16 * pair
        base[side, at : at + 16, LANES:] = jnp.concatenate(steps, axis=0).astype(BF16)

    jobs = [(c, pair) for c in range(GROUP) for pair in range(FINE // 16)]

    def multiply(side, k):
        start = k * tok
        right = jnp.concatenate(
            [
                base[side, :, LANES + start : LANES + start + tok],
                base[side, :, start : start + tok],
            ],
            axis=0,
        )
        count = turns - k // 2
        out = jnp.dot(left[side, : 32 * count], right, preferred_element_type=F32)
        for m in range(count):
            at = slice(start + 2 * tok * m, start + 2 * tok * m + tok)
            piece = out[32 * m : 32 * m + 32]
            if k < 2:
                total[side, :, at] = piece
            else:
                total[side, :, at] += piece

    def summed(side):
        run = total[side, 24:32]
        for e in (2, 1, 0):
            run = total[side, 8 * e : 8 * e + 8] + delayed(run, FINE)
        return run

    build_left(0, 0)
    for job in jobs:
        build_base(0, 0, *job)

    def unit(index, carry):
        done = []
        for part in range(2):
            row = index * 16 + 8 * part
            sums = []
            for side in range(2):
                if side == 0:
                    after = row
                elif part == 0:
                    after = row + 8
                else:
                    after = jnp.minimum(row + 8, lanes - 8)
                build_left(after, 1 - side)
                for k in range(blocks):
                    for at, job in enumerate(jobs):
                        if at * blocks // len(jobs) == k:
                            build_base(after, 1 - side, *job)
                    multiply(side, k)
                sums.append(summed(side))
            upper = lax.broadcasted_iota(jnp.int32, (8, length), 0) < 4
            even, odd = halves(sums[0], sums[1], upper)
            conv = even + jnp.concatenate(
                [jnp.zeros((8, tok), F32), odd[:, : length - tok]], axis=1
            )
            here = pl.ds(pl.multiple_of(row, 8), 8)
            skip = jnp.concatenate([skip_ref[here, :]] * (tok // LANES), axis=1)
            done.append(
                [conv[:, h * tok : (h + 1) * tok] + skip * prod[h, here, :] for h in range(blocks)]
            )
        for h in range(blocks):
            held[h, pl.ds(pl.multiple_of(index * 16, 16), 16), :] = jnp.concatenate(
                [done[0][h], done[1][h]], axis=0
            ).astype(BF16)
        return carry

    lax.fori_loop(0, units, unit, 0)
    for j in range(far):
        for i in range(NEAR):
            out_refs[j][i] = held[at_ref[0] ^ (NEAR * j + i)]


def long_conv(arrays, skip_rows, blocks, position):
    near, _, lanes, tok = arrays[0].shape
    far = blocks // near
    length = blocks * tok
    whole = lambda array: pl.BlockSpec(array.shape, lambda i, at: (0,) * array.ndim)
    operands = [skip_rows, *arrays]
    out_shape = [jax.ShapeDtypeStruct((near, lanes, tok), BF16)] * far
    return pl.pallas_call(
        conv_kernel,
        grid_spec=pltpu.PrefetchScalarGridSpec(
            num_scalar_prefetch=1,
            grid=(1,),
            in_specs=[whole(array) for array in operands],
            out_specs=[whole(array) for array in out_shape],
            scratch_shapes=[
                pltpu.VMEM((lanes, length), F32),
                pltpu.VMEM((blocks, lanes, tok), F32),
                pltpu.VMEM((2, GROUP * FINE, LANES + length), BF16),
                pltpu.VMEM((2, 16 * blocks, 2 * LANES), BF16),
                pltpu.VMEM((2, 32, length), F32),
                pltpu.VMEM((blocks, lanes, tok), BF16),
            ],
        ),
        out_shape=out_shape,
        compiler_params=pltpu.CompilerParams(vmem_limit_bytes=VMEM_BYTES),
        cost_estimate=pl.CostEstimate(
            flops=64 * lanes * length * 256, bytes_accessed=6 * lanes * length, transcendentals=0
        ),
        name="long_conv",
    )(position, *operands)


def gated_kernel(at_ref, gate_ref, halo_ref, taps_ref, *refs):
    mixed_refs, refs, held = refs[:NEAR], refs[NEAR:-1], refs[-1]
    gated_ref, squares_ref = refs[-2:]
    _, narrow, tok = held.shape
    count = WIDE // narrow
    step = pl.program_id(0)

    @pl.when(step == 0)
    def _():
        for i, mixed_ref in enumerate(mixed_refs):
            for j in range(mixed_ref.shape[0]):
                held[at_ref[0] ^ (NEAR * j + i)] = mixed_ref[j]

    halo = halo_ref[...].astype(F32)
    gate = short_conv(gate_ref[...].astype(F32), halo[2 * HALO :], taps_ref[...])
    mixed = held[pl.ds(step * count, count)].reshape(WIDE, tok)
    gated = gate * mixed.astype(F32).T
    gated_ref[...] = gated
    squares = gated * gated
    part = squares[:, :LANES]
    for at in range(LANES, WIDE, LANES):
        part = part + squares[:, at : at + LANES]
    turned = jnp.sum(part.T.reshape(LANES // 8, 8, part.shape[0]), axis=0)

    @pl.when(step == 0)
    def _():
        squares_ref[...] = refs[0][...] + turned if len(refs) > 2 else turned

    @pl.when(step > 0)
    def _():
        squares_ref[...] += turned


def gated_of(gate_in, halo, gate_short, mixed, start, before, position):
    tok, full = gate_in.shape
    far, narrow, _ = mixed[0].shape
    width = NEAR * far * narrow
    first = start // WIDE
    column = lambda rows: pl.BlockSpec((rows, WIDE), lambda i, at: (0, first + i))
    sums = pl.BlockSpec((8, tok), lambda i, at: (0, 0))
    more = [] if before is None else [sums, pl.BlockSpec(memory_space=pl.ANY)]
    return pl.pallas_call(
        gated_kernel,
        grid_spec=pltpu.PrefetchScalarGridSpec(
            num_scalar_prefetch=1,
            grid=(width // WIDE,),
            in_specs=[column(tok), column(3 * HALO), column(3)]
            + [pl.BlockSpec(mixed[0].shape, lambda i, at: (0, 0, 0))] * NEAR
            + more,
            out_specs=[column(tok), sums],
            scratch_shapes=[pltpu.VMEM((NEAR * far, narrow, tok), BF16)],
        ),
        out_shape=[
            jax.ShapeDtypeStruct((tok, full), F32),
            jax.ShapeDtypeStruct((8, tok), F32),
        ],
        input_output_aliases={5 + NEAR: 0} if more else {},
        compiler_params=pltpu.CompilerParams(vmem_limit_bytes=VMEM_BYTES),
        cost_estimate=pl.CostEstimate(
            flops=10 * tok * width, bytes_accessed=8 * tok * width, transcendentals=0
        ),
        name="gated_squares",
    )(
        position,
        gate_in,
        halo,
        gate_short,
        *mixed,
        *(() if before is None else (before[1], before[0])),
    )


def norm_kernel(channels, gated_ref, gain_ref, *refs):
    sums, out_ref = refs[:-1], refs[-1]
    total = sums[0][...]
    for other in sums[1:]:
        total = total + other[...]
    total = jnp.sum(total, axis=0, keepdims=True)
    scale = lax.rsqrt(total / channels + 1e-06)
    scale = jnp.broadcast_to(scale, (LANES, scale.shape[1])).T
    scale = jnp.concatenate([scale] * (WIDE // LANES), axis=1)
    out_ref[...] = (gated_ref[...] * gain_ref[...] * scale).astype(BF16)


def normed(gated, squares, norm_gain, channels):
    tok, width = gated.shape
    column = lambda rows: pl.BlockSpec((rows, WIDE), lambda i: (0, i))
    return pl.pallas_call(
        functools.partial(norm_kernel, channels),
        grid=(width // WIDE,),
        in_specs=[column(tok), column(1)]
        + [pl.BlockSpec((8, tok), lambda i: (0, 0))] * len(squares),
        out_specs=column(tok),
        out_shape=jax.ShapeDtypeStruct((tok, width), BF16),
        compiler_params=pltpu.CompilerParams(vmem_limit_bytes=VMEM_BYTES),
        cost_estimate=pl.CostEstimate(
            flops=4 * tok * width, bytes_accessed=6 * tok * width, transcendentals=tok
        ),
        name="normed",
    )(gated, norm_gain, *squares)


def local(
    gate_in, key_in, value_in, long_filter, gate_short, key_short, value_short, skip_gain, norm_gain
):
    tok, width = value_in.shape
    blocks = lax.axis_size("seq")
    groups = lax.axis_size("ch")
    place = lax.axis_index("seq")
    position = jnp.full((1,), place, jnp.int32)
    halo = passed_along(
        jnp.concatenate([a[tok - HALO :] for a in (key_in, value_in, gate_in)], axis=0), "seq", 1
    )
    narrow = width // blocks // PARTS
    starts = [at * narrow * blocks for at in range(PARTS)]
    pack = lambda wants, start: packed(
        wants,
        ([long_filter] if "filter" in wants else [])
        + ([key_in, value_in, halo, key_short, value_short] if "product" in wants else []),
        (start, narrow, blocks),
        position,
    )
    far = blocks // NEAR
    sent = [pack(("filter",), starts[0]), pack(("product",), starts[0])]
    arrived = [[]]
    for parts in sent:
        arrived[0] += swap_far(swap_near(parts))
    for start in starts[1:]:
        parts = pack(("filter", "product"), start)
        arrived[0][:far], parts = lax.optimization_barrier((arrived[0][:far], parts))
        arrived[-1], lines = lax.optimization_barrier((arrived[-1], swap_near(parts)))
        arrived.append(swap_far(lines))
    mixed = []
    for start, arrays in zip(starts, arrived):
        skip = lax.dynamic_slice_in_dim(skip_gain, start + place * narrow, narrow, 0)
        skip = jnp.broadcast_to(skip[:, None], (narrow, LANES))
        mixed.append(swap_back(long_conv(arrays, skip, blocks, position)))
    gated = None
    for start, part in zip(starts, mixed):
        gated = gated_of(gate_in, halo, gate_short, part, start, gated, position)
    gated, squares = gated
    sums = [squares]
    for by in range(1, groups):
        sums.append(lax.ppermute(squares, "ch", [(i, (i + by) % groups) for i in range(groups)]))
    return normed(gated, sums, norm_gain[None, :], width * groups)


def solution(mesh):
    return jax.shard_map(
        local,
        mesh=mesh,
        in_specs=(
            P("seq", "ch"),
            P("seq", "ch"),
            P("seq", "ch"),
            P("seq", "ch"),
            P(None, "ch"),
            P(None, "ch"),
            P(None, "ch"),
            P("ch"),
            P("ch"),
        ),
        out_specs=P("seq", "ch"),
        check_vma=False,
    )
```

profile of v0, /device:TPU:0, one launch (start us, length us, event | category | flops | bytes accessed | tf_op | source)
XLA Modules:
  0.0 129.7 jit_solution(3655276862386027593)
XLA Ops:
  0.0 1.0 slice.251
  1.0 0.8 slice.249
  1.8 0.8 slice.250
  2.7 2.4 %collective-permute-start = (bf16[48,2048]{1,0:T(8,128)(2,1)S(1)}, bf16[48,2048]{1,0:T(8,128)(2,1)S(1)}, u32[]{:S(2)}, u32[]{:S(2)}) collective-permute-start(bf16[48,2048]{1,0:T(8,128)(2,1)S(1)} %pad_maximum_fusion.4), channel_id=1, source_target_pairs={{0,2},{2,4},{4,6},{6,8},{8,10},{10,12},{12,14},{14,16},{16,18},{18... | collective-permute-start | bytes 589832 | tf_op jit(solution)/shard_map/ppermute | solution.py:25
  5.1 0.0 copy-start.3
  5.1 1.2 copy-done.3
  6.3 0.4 pack_filter.1
  6.7 2.7 %collective-permute-start.1 = (bf16[4,1,64,256]{3,2,1,0:T(8,128)(2,1)S(1)}, bf16[4,1,64,256]{3,2,1,0:T(8,128)(2,1)S(1)}, u32[]{:S(2)}, u32[]{:S(2)}) collective-permute-start(bf16[4,1,64,256]{3,2,1,0:T(8,128)(2,1)S(1)} %get-tuple-element.50), channel_id=1, source_target_pairs={{0,2},{2,0},{4,6},{6,4},{8,10},{10,8},{12,14},{14,12},{16,18},{18,... | collective-permute-start | bytes 393224 | tf_op jit(solution)/shard_map/ppermute | solution.py:97
  9.4 1.5 %collective-permute-start.2 = (bf16[4,1,64,256]{3,2,1,0:T(8,128)(2,1)S(1)}, bf16[4,1,64,256]{3,2,1,0:T(8,128)(2,1)S(1)}, u32[]{:S(2)}, u32[]{:S(2)}) collective-permute-start(bf16[4,1,64,256]{3,2,1,0:T(8,128)(2,1)S(1)} %get-tuple-element.51), channel_id=1, source_target_pairs={{0,4},{2,6},{4,0},{6,2},{8,12},{10,14},{12,8},{14,10},{16,20},{18,... | collective-permute-start | bytes 393224 | tf_op jit(solution)/shard_map/ppermute | solution.py:97
  10.9 0.8 fusion.20
  11.7 4.0 %collective-permute-done.2 = bf16[4,1,64,256]{3,2,1,0:T(8,128)(2,1)S(1)} collective-permute-done((bf16[4,1,64,256]{3,2,1,0:T(8,128)(2,1)S(1)}, bf16[4,1,64,256]{3,2,1,0:T(8,128)(2,1)S(1)}, u32[]{:S(2)}, u32[]{:S(2)}) %collective-permute-start.2) | collective-permute-done | bytes 131104 | tf_op jit(solution)/shard_map/ppermute | solution.py:97
  15.8 1.0 collective-permute-done.3
  16.9 1.6 %collective-permute-start.4 = (bf16[4,1,64,256]{3,2,1,0:T(8,128)(2,1)S(1)}, bf16[4,1,64,256]{3,2,1,0:T(8,128)(2,1)S(1)}, u32[]{:S(2)}, u32[]{:S(2)}) collective-permute-start(bf16[4,1,64,256]{3,2,1,0:T(8,128)(2,1)S(1)} %pad_maximum_fusion.6), channel_id=1, source_target_pairs={{0,8},{2,10},{4,12},{6,14},{8,0},{10,2},{12,4},{14,6},{16,24},{18,... | collective-permute-start | bytes 393224 | tf_op jit(solution)/shard_map/ppermute | solution.py:97
  18.5 2.7 %collective-permute-start.5 = (bf16[4,1,64,256]{3,2,1,0:T(8,128)(2,1)S(1)}, bf16[4,1,64,256]{3,2,1,0:T(8,128)(2,1)S(1)}, u32[]{:S(2)}, u32[]{:S(2)}) collective-permute-start(bf16[4,1,64,256]{3,2,1,0:T(8,128)(2,1)S(1)} %pad_maximum_fusion.7), channel_id=1, source_target_pairs={{0,16},{2,18},{4,20},{6,22},{8,24},{10,26},{12,28},{14,30},{16,0},... | collective-permute-start | bytes 393224 | tf_op jit(solution)/shard_map/ppermute | solution.py:97
  21.2 0.3 collective-permute-start.6
  21.6 1.2 pack_product.1
  22.7 0.1 collective-permute-start.7
  22.8 1.6 %collective-permute-start.8 = (bf16[4,1,64,256]{3,2,1,0:T(8,128)(2,1)S(1)}, bf16[4,1,64,256]{3,2,1,0:T(8,128)(2,1)S(1)}, u32[]{:S(2)}, u32[]{:S(2)}) collective-permute-start(bf16[4,1,64,256]{3,2,1,0:T(8,128)(2,1)S(1)} %get-tuple-element.63), channel_id=1, source_target_pairs={{0,4},{2,6},{4,0},{6,2},{8,12},{10,14},{12,8},{14,10},{16,20},{18,... | collective-permute-start | bytes 393224 | tf_op jit(solution)/shard_map/ppermute | solution.py:97
  24.4 1.3 %pack_filter_product.1 = (bf16[4,2,64,256]{3,2,1,0:T(8,128)(2,1)S(1)}, bf16[4,2,64,256]{3,2,1,0:T(8,128)(2,1)S(1)}, bf16[4,2,64,256]{3,2,1,0:T(8,128)(2,1)S(1)}, bf16[4,2,64,256]{3,2,1,0:T(8,128)(2,1)S(1)}) custom-call(s32[1]{0:T(128)} %bitcast.at_ref, bf16[256,2048]{1,0:T(8,128)(2,1)S(1)} %copy-done.4, bf16[256,2048]{1,0:T(8,128)(2,1)S(1)} %copy-done.1, ...), custom_call_target="tpu_custom_call" | custom-call | flops 12582912 | bytes 6291456 | tf_op jit(solution)/shard_map/pack_filter_product/pallas_call | solution.py:72
  25.8 0.6 collective-permute-start.9
  26.4 5.1 %collective-permute-done.5.refs_2_ = bf16[4,1,64,256]{3,2,1,0:T(8,128)(2,1)S(1)} collective-permute-done((bf16[4,1,64,256]{3,2,1,0:T(8,128)(2,1)S(1)}, bf16[4,1,64,256]{3,2,1,0:T(8,128)(2,1)S(1)}, u32[]{:S(2)}, u32[]{:S(2)}) %collective-permute-start.5) | collective-permute-done | bytes 131104 | tf_op jit(solution)/shard_map/ppermute | solution.py:97
  31.5 1.5 %collective-permute-start.14 = (bf16[4,2,64,256]{3,2,1,0:T(8,128)(2,1)S(1)}, bf16[4,2,64,256]{3,2,1,0:T(8,128)(2,1)S(1)}, u32[]{:S(2)}, u32[]{:S(2)}) collective-permute-start(bf16[4,2,64,256]{3,2,1,0:T(8,128)(2,1)S(1)} %get-tuple-element.67), channel_id=1, source_target_pairs={{0,4},{2,6},{4,0},{6,2},{8,12},{10,14},{12,8},{14,10},{16,20},{18,... | collective-permute-start | bytes 786440 | tf_op jit(solution)/shard_map/ppermute | solution.py:97
  33.0 0.4 collective-permute-start.15
  33.5 3.0 %collective-permute-start.10 = (bf16[4,1,64,256]{3,2,1,0:T(8,128)(2,1)S(1)}, bf16[4,1,64,256]{3,2,1,0:T(8,128)(2,1)S(1)}, u32[]{:S(2)}, u32[]{:S(2)}) collective-permute-start(bf16[4,1,64,256]{3,2,1,0:T(8,128)(2,1)S(1)} %pad_maximum_fusion.10), channel_id=1, source_target_pairs={{0,8},{2,10},{4,12},{6,14},{8,0},{10,2},{12,4},{14,6},{16,24},{18,... | collective-permute-start | bytes 393224 | tf_op jit(solution)/shard_map/ppermute | solution.py:97
  36.5 1.1 collective-permute-start.11
  37.7 1.5 %collective-permute-start.12 = (bf16[4,1,64,256]{3,2,1,0:T(8,128)(2,1)S(1)}, bf16[4,1,64,256]{3,2,1,0:T(8,128)(2,1)S(1)}, u32[]{:S(2)}, u32[]{:S(2)}) collective-permute-start(bf16[4,1,64,256]{3,2,1,0:T(8,128)(2,1)S(1)} %pad_maximum_fusion.12), channel_id=1, source_target_pairs={{0,24},{2,26},{4,28},{6,30},{8,16},{10,18},{12,20},{14,22},{16,8},... | collective-permute-start | bytes 393224 | tf_op jit(solution)/shard_map/ppermute | solution.py:97
  39.2 1.3 %collective-permute-done.14 = bf16[4,2,64,256]{3,2,1,0:T(8,128)(2,1)S(1)} collective-permute-done((bf16[4,2,64,256]{3,2,1,0:T(8,128)(2,1)S(1)}, bf16[4,2,64,256]{3,2,1,0:T(8,128)(2,1)S(1)}, u32[]{:S(2)}, u32[]{:S(2)}) %collective-permute-start.14) | collective-permute-done | bytes 262176 | tf_op jit(solution)/shard_map/ppermute | solution.py:97
  40.6 4.8 %collective-permute-done.15 = bf16[4,2,64,256]{3,2,1,0:T(8,128)(2,1)S(1)} collective-permute-done((bf16[4,2,64,256]{3,2,1,0:T(8,128)(2,1)S(1)}, bf16[4,2,64,256]{3,2,1,0:T(8,128)(2,1)S(1)}, u32[]{:S(2)}, u32[]{:S(2)}) %collective-permute-start.15) | collective-permute-done | bytes 262176 | tf_op jit(solution)/shard_map/ppermute | solution.py:97
  45.4 0.1 pad_maximum_fusion.2
  45.5 0.1 pad_maximum_fusion
  45.6 3.9 %collective-permute-done.11.refs_6_ = bf16[4,1,64,256]{3,2,1,0:T(8,128)(2,1)S(1)} collective-permute-done((bf16[4,1,64,256]{3,2,1,0:T(8,128)(2,1)S(1)}, bf16[4,1,64,256]{3,2,1,0:T(8,128)(2,1)S(1)}, u32[]{:S(2)}, u32[]{:S(2)}) %collective-permute-start.11) | collective-permute-done | bytes 131104 | tf_op jit(solution)/shard_map/ppermute | solution.py:97
  49.5 2.4 %collective-permute-start.16 = (bf16[4,2,64,256]{3,2,1,0:T(8,128)(2,1)S(1)}, bf16[4,2,64,256]{3,2,1,0:T(8,128)(2,1)S(1)}, u32[]{:S(2)}, u32[]{:S(2)}) collective-permute-start(bf16[4,2,64,256]{3,2,1,0:T(8,128)(2,1)S(1)} %get-tuple-element.70), channel_id=1, source_target_pairs={{0,8},{2,10},{4,12},{6,14},{8,0},{10,2},{12,4},{14,6},{16,24},{18,... | collective-permute-start | bytes 786440 | tf_op jit(solution)/shard_map/ppermute | solution.py:97
  51.9 1.0 collective-permute-start.17
  52.9 1.5 %collective-permute-start.18 = (bf16[4,2,64,256]{3,2,1,0:T(8,128)(2,1)S(1)}, bf16[4,2,64,256]{3,2,1,0:T(8,128)(2,1)S(1)}, u32[]{:S(2)}, u32[]{:S(2)}) collective-permute-start(bf16[4,2,64,256]{3,2,1,0:T(8,128)(2,1)S(1)} %get-tuple-element.72), channel_id=1, source_target_pairs={{0,24},{2,26},{4,28},{6,30},{8,16},{10,18},{12,20},{14,22},{16,8},... | collective-permute-start | bytes 786440 | tf_op jit(solution)/shard_map/ppermute | solution.py:97
  54.3 0.1 broadcast_in_dim.20.skip_ref
  54.4 10.3 %long_conv.3 = (bf16[4,64,256]{2,1,0:T(8,128)(2,1)S(1)}, bf16[4,64,256]{2,1,0:T(8,128)(2,1)S(1)}, bf16[4,64,256]{2,1,0:T(8,128)(2,1)S(1)}, bf16[4,64,256]{2,1,0:T(8,128)(2,1)S(1)}) custom-call(s32[1]{0:T(128)} %bitcast.at_ref, f32[64,128]{1,0:T(8,128)S(1)} %broadcast_in_dim.20.skip_ref, bf16[4,1,64,256]{3,2,1,0:T(8,128)(2,1)S(1)} %pad_maximum_fusion.5.refs_0_, ...), custom_call_target="tpu_custom_call" | custom-call | flops 4294967296 | bytes 1572864 | tf_op jit(solution)/shard_map/long_conv/pallas_call | solution.py:266
  64.8 1.1 collective-permute-start.25
  65.9 1.9 %collective-permute-start.26 = (bf16[4,64,256]{2,1,0:T(8,128)(2,1)S(1)}, bf16[4,64,256]{2,1,0:T(8,128)(2,1)S(1)}, u32[]{:S(2)}, u32[]{:S(2)}) collective-permute-start(bf16[4,64,256]{2,1,0:T(8,128)(2,1)S(1)} %get-tuple-element.87), channel_id=1, source_target_pairs={{0,16},{2,18},{4,20},{6,22},{8,24},{10,26},{12,28},{14,30},{16,0},... | collective-permute-start | bytes 393224 | tf_op jit(solution)/shard_map/ppermute | solution.py:97
  67.8 6.6 %collective-permute-done.25 = bf16[4,64,256]{2,1,0:T(8,128)(2,1)S(1)} collective-permute-done((bf16[4,64,256]{2,1,0:T(8,128)(2,1)S(1)}, bf16[4,64,256]{2,1,0:T(8,128)(2,1)S(1)}, u32[]{:S(2)}, u32[]{:S(2)}) %collective-permute-start.25) | collective-permute-done | bytes 131104 | tf_op jit(solution)/shard_map/ppermute | solution.py:97
  74.4 2.0 %collective-permute-start.27 = (bf16[4,64,256]{2,1,0:T(8,128)(2,1)S(1)}, bf16[4,64,256]{2,1,0:T(8,128)(2,1)S(1)}, u32[]{:S(2)}, u32[]{:S(2)}) collective-permute-start(bf16[4,64,256]{2,1,0:T(8,128)(2,1)S(1)} %get-tuple-element.88), channel_id=1, source_target_pairs={{0,24},{2,26},{4,28},{6,30},{8,16},{10,18},{12,20},{14,22},{16,8},... | collective-permute-start | bytes 393224 | tf_op jit(solution)/shard_map/ppermute | solution.py:97
  76.4 10.3 %collective-permute-done.26 = bf16[4,64,256]{2,1,0:T(8,128)(2,1)S(1)} collective-permute-done((bf16[4,64,256]{2,1,0:T(8,128)(2,1)S(1)}, bf16[4,64,256]{2,1,0:T(8,128)(2,1)S(1)}, u32[]{:S(2)}, u32[]{:S(2)}) %collective-permute-start.26) | collective-permute-done | bytes 131104 | tf_op jit(solution)/shard_map/ppermute | solution.py:97
  86.7 0.1 collective-permute-start.28
  86.8 1.6 %collective-permute-start.29 = (bf16[4,64,256]{2,1,0:T(8,128)(2,1)S(1)}, bf16[4,64,256]{2,1,0:T(8,128)(2,1)S(1)}, u32[]{:S(2)}, u32[]{:S(2)}) collective-permute-start(bf16[4,64,256]{2,1,0:T(8,128)(2,1)S(1)} %pad_maximum_fusion.19), channel_id=1, source_target_pairs={{0,4},{2,6},{4,0},{6,2},{8,12},{10,14},{12,8},{14,10},{16,20},{18,... | collective-permute-start | bytes 393224 | tf_op jit(solution)/shard_map/ppermute | solution.py:97
  88.5 0.4 collective-permute-start.30
  88.9 0.1 broadcast_in_dim.9.skip_ref
  88.9 10.3 %long_conv.2 = (bf16[4,64,256]{2,1,0:T(8,128)(2,1)S(1)}, bf16[4,64,256]{2,1,0:T(8,128)(2,1)S(1)}, bf16[4,64,256]{2,1,0:T(8,128)(2,1)S(1)}, bf16[4,64,256]{2,1,0:T(8,128)(2,1)S(1)}) custom-call(s32[1]{0:T(128)} %bitcast.at_ref, f32[64,128]{1,0:T(8,128)S(1)} %broadcast_in_dim.9.skip_ref, bf16[4,2,64,256]{3,2,1,0:T(8,128)(2,1)S(1)} %get-tuple-element.69.refs_0_, ...), custom_call_target="tpu_custom_call" | custom-call | flops 4294967296 | bytes 1572864 | tf_op jit(solution)/shard_map/long_conv/pallas_call | solution.py:266
  99.3 0.0 copy-start.2
  99.3 0.0 copy-start.7
  99.3 2.0 %collective-permute-start.19 = (bf16[4,64,256]{2,1,0:T(8,128)(2,1)S(1)}, bf16[4,64,256]{2,1,0:T(8,128)(2,1)S(1)}, u32[]{:S(2)}, u32[]{:S(2)}) collective-permute-start(bf16[4,64,256]{2,1,0:T(8,128)(2,1)S(1)} %get-tuple-element.74), channel_id=1, source_target_pairs={{0,8},{2,10},{4,12},{6,14},{8,0},{10,2},{12,4},{14,6},{16,24},{18,... | collective-permute-start | bytes 393224 | tf_op jit(solution)/shard_map/ppermute | solution.py:97
  101.3 1.2 collective-permute-start.20
  102.5 5.2 %collective-permute-done.19 = bf16[4,64,256]{2,1,0:T(8,128)(2,1)S(1)} collective-permute-done((bf16[4,64,256]{2,1,0:T(8,128)(2,1)S(1)}, bf16[4,64,256]{2,1,0:T(8,128)(2,1)S(1)}, u32[]{:S(2)}, u32[]{:S(2)}) %collective-permute-start.19) | collective-permute-done | bytes 131104 | tf_op jit(solution)/shard_map/ppermute | solution.py:97
  107.7 1.4 %collective-permute-start.21 = (bf16[4,64,256]{2,1,0:T(8,128)(2,1)S(1)}, bf16[4,64,256]{2,1,0:T(8,128)(2,1)S(1)}, u32[]{:S(2)}, u32[]{:S(2)}) collective-permute-start(bf16[4,64,256]{2,1,0:T(8,128)(2,1)S(1)} %get-tuple-element.76), channel_id=1, source_target_pairs={{0,24},{2,26},{4,28},{6,30},{8,16},{10,18},{12,20},{14,22},{16,8},... | collective-permute-start | bytes 393224 | tf_op jit(solution)/shard_map/ppermute | solution.py:97
  109.1 2.8 %collective-permute-done.20 = bf16[4,64,256]{2,1,0:T(8,128)(2,1)S(1)} collective-permute-done((bf16[4,64,256]{2,1,0:T(8,128)(2,1)S(1)}, bf16[4,64,256]{2,1,0:T(8,128)(2,1)S(1)}, u32[]{:S(2)}, u32[]{:S(2)}) %collective-permute-start.20) | collective-permute-done | bytes 131104 | tf_op jit(solution)/shard_map/ppermute | solution.py:97
  111.9 2.7 %collective-permute-done.21 = bf16[4,64,256]{2,1,0:T(8,128)(2,1)S(1)} collective-permute-done((bf16[4,64,256]{2,1,0:T(8,128)(2,1)S(1)}, bf16[4,64,256]{2,1,0:T(8,128)(2,1)S(1)}, u32[]{:S(2)}, u32[]{:S(2)}) %collective-permute-start.21) | collective-permute-done | bytes 131104 | tf_op jit(solution)/shard_map/ppermute | solution.py:97
  114.6 0.1 collective-permute-start.22
  114.7 1.6 %collective-permute-start.23 = (bf16[4,64,256]{2,1,0:T(8,128)(2,1)S(1)}, bf16[4,64,256]{2,1,0:T(8,128)(2,1)S(1)}, u32[]{:S(2)}, u32[]{:S(2)}) collective-permute-start(bf16[4,64,256]{2,1,0:T(8,128)(2,1)S(1)} %pad_maximum_fusion.15), channel_id=1, source_target_pairs={{0,4},{2,6},{4,0},{6,2},{8,12},{10,14},{12,8},{14,10},{16,20},{18,... | collective-permute-start | bytes 393224 | tf_op jit(solution)/shard_map/ppermute | solution.py:97
  116.3 0.4 collective-permute-start.24
  116.8 1.0 gated_squares.2
  117.8 3.3 %collective-permute-done.23.refs_2_ = bf16[4,64,256]{2,1,0:T(8,128)(2,1)S(1)} collective-permute-done((bf16[4,64,256]{2,1,0:T(8,128)(2,1)S(1)}, bf16[4,64,256]{2,1,0:T(8,128)(2,1)S(1)}, u32[]{:S(2)}, u32[]{:S(2)}) %collective-permute-start.23) | collective-permute-done | bytes 131104 | tf_op jit(solution)/shard_map/ppermute | solution.py:97
  121.1 2.0 %collective-permute-done.24.refs_3_ = bf16[4,64,256]{2,1,0:T(8,128)(2,1)S(1)} collective-permute-done((bf16[4,64,256]{2,1,0:T(8,128)(2,1)S(1)}, bf16[4,64,256]{2,1,0:T(8,128)(2,1)S(1)}, u32[]{:S(2)}, u32[]{:S(2)}) %collective-permute-start.24) | collective-permute-done | bytes 131104 | tf_op jit(solution)/shard_map/ppermute | solution.py:97
  123.1 1.0 gated_squares.3
  124.0 1.5 %collective-permute-start.31 = (f32[8,256]{1,0:T(8,128)S(1)}, f32[8,256]{1,0:T(8,128)S(1)}, u32[]{:S(2)}, u32[]{:S(2)}) collective-permute-start(f32[8,256]{1,0:T(8,128)S(1)} %get-tuple-element.92.refs_0_), channel_id=1, source_target_pairs={{0,1},{1,0},{2,3},{3,2},{4,5},{5,4},{6,7},{7,6},{8,9},{9,8},{10,11... | collective-permute-start | bytes 24584 | tf_op jit(solution)/shard_map/ppermute | solution.py:434
  125.6 2.2 %collective-permute-done.31.refs_1_ = f32[8,256]{1,0:T(8,128)S(1)} collective-permute-done((f32[8,256]{1,0:T(8,128)S(1)}, f32[8,256]{1,0:T(8,128)S(1)}, u32[]{:S(2)}, u32[]{:S(2)}) %collective-permute-start.31) | collective-permute-done | bytes 8224 | tf_op jit(solution)/shard_map/ppermute | solution.py:434
  127.8 1.9 %normed.1 = bf16[256,2048]{1,0:T(8,128)(2,1)} custom-call(f32[256,2048]{1,0:T(8,128)S(1)} %get-tuple-element.91.gated_ref, f32[1,2048]{1,0:T(1,128)S(1)} %bitcast.2, f32[8,256]{1,0:T(8,128)S(1)} %get-tuple-element.92.refs_0_, f32[8,256]{1,0:T(8,128)S(1)} %collective-permute-done.31.refs_1_), custom_call_target="tpu_custom_call" | custom-call | flops 2097152 | bytes 3145728 | tf_op jit(solution)/shard_map/normed/pallas_call | solution.py:378
  (71 shorter events, 0.6 us)
Async XLA Ops:
  0.0 21.5 %copy-start.1 = (bf16[256,2048]{1,0:T(8,128)(2,1)S(1)}, bf16[256,2048]{1,0:T(8,128)(2,1)}, u32[]{:S(2)}) copy-start(bf16[256,2048]{1,0:T(8,128)(2,1)} %refs_0_.5) | copy-start | bytes 3145732
  0.0 21.5 %copy-start = (bf16[256,2048]{1,0:T(8,128)(2,1)S(1)}, bf16[256,2048]{1,0:T(8,128)(2,1)}, u32[]{:S(2)}) copy-start(bf16[256,2048]{1,0:T(8,128)(2,1)} %refs_1_.3) | copy-start | bytes 3145732
  2.7 18.8 %collective-permute-start = (bf16[48,2048]{1,0:T(8,128)(2,1)S(1)}, bf16[48,2048]{1,0:T(8,128)(2,1)S(1)}, u32[]{:S(2)}, u32[]{:S(2)}) collective-permute-start(bf16[48,2048]{1,0:T(8,128)(2,1)S(1)} %pad_maximum_fusion.4), channel_id=1, source_target_pairs={{0,2},{2,4},{4,6},{6,8},{8,10},{10,12},{12,14},{14,16},{16,18},{18... | collective-permute-start | bytes 589832 | tf_op jit(solution)/shard_map/ppermute | solution.py:25
  5.1 1.2 copy-start.3
  6.3 15.2 %copy-start.5 = (f32[3,2048]{1,0:T(4,128)S(1)}, f32[3,2048]{1,0:T(4,128)}, u32[]{:S(2)}) copy-start(f32[3,2048]{1,0:T(4,128)} %refs_3_.1) | copy-start | bytes 73732
  6.3 15.2 %copy-start.6 = (f32[3,2048]{1,0:T(4,128)S(1)}, f32[3,2048]{1,0:T(4,128)}, u32[]{:S(2)}) copy-start(f32[3,2048]{1,0:T(4,128)} %refs_4_.3) | copy-start | bytes 73732
  6.7 5.0 %collective-permute-start.1 = (bf16[4,1,64,256]{3,2,1,0:T(8,128)(2,1)S(1)}, bf16[4,1,64,256]{3,2,1,0:T(8,128)(2,1)S(1)}, u32[]{:S(2)}, u32[]{:S(2)}) collective-permute-start(bf16[4,1,64,256]{3,2,1,0:T(8,128)(2,1)S(1)} %get-tuple-element.50), channel_id=1, source_target_pairs={{0,2},{2,0},{4,6},{6,4},{8,10},{10,8},{12,14},{14,12},{16,18},{18,... | collective-permute-start | bytes 393224 | tf_op jit(solution)/shard_map/ppermute | solution.py:97
  9.4 6.4 %collective-permute-start.2 = (bf16[4,1,64,256]{3,2,1,0:T(8,128)(2,1)S(1)}, bf16[4,1,64,256]{3,2,1,0:T(8,128)(2,1)S(1)}, u32[]{:S(2)}, u32[]{:S(2)}) collective-permute-start(bf16[4,1,64,256]{3,2,1,0:T(8,128)(2,1)S(1)} %get-tuple-element.51), channel_id=1, source_target_pairs={{0,4},{2,6},{4,0},{6,2},{8,12},{10,14},{12,8},{14,10},{16,20},{18,... | collective-permute-start | bytes 393224 | tf_op jit(solution)/shard_map/ppermute | solution.py:97
  10.9 5.9 %collective-permute-start.3 = (bf16[4,1,64,256]{3,2,1,0:T(8,128)(2,1)S(1)}, bf16[4,1,64,256]{3,2,1,0:T(8,128)(2,1)S(1)}, u32[]{:S(2)}, u32[]{:S(2)}) collective-permute-start(bf16[4,1,64,256]{3,2,1,0:T(8,128)(2,1)S(1)} %get-tuple-element.52), channel_id=1, source_target_pairs={{0,6},{2,4},{4,2},{6,0},{8,14},{10,12},{12,10},{14,8},{16,22},{18,... | collective-permute-start | bytes 393224 | tf_op jit(solution)/shard_map/ppermute | solution.py:97
  11.7 12.7 %copy-start.4 = (bf16[256,2048]{1,0:T(8,128)(2,1)S(1)}, bf16[256,2048]{1,0:T(8,128)(2,1)}, u32[]{:S(2)}) copy-start(bf16[256,2048]{1,0:T(8,128)(2,1)} %refs_0_.4) | copy-start | bytes 3145732
  16.9 8.9 %collective-permute-start.4 = (bf16[4,1,64,256]{3,2,1,0:T(8,128)(2,1)S(1)}, bf16[4,1,64,256]{3,2,1,0:T(8,128)(2,1)S(1)}, u32[]{:S(2)}, u32[]{:S(2)}) collective-permute-start(bf16[4,1,64,256]{3,2,1,0:T(8,128)(2,1)S(1)} %pad_maximum_fusion.6), channel_id=1, source_target_pairs={{0,8},{2,10},{4,12},{6,14},{8,0},{10,2},{12,4},{14,6},{16,24},{18,... | collective-permute-start | bytes 393224 | tf_op jit(solution)/shard_map/ppermute | solution.py:97
  18.5 12.9 %collective-permute-start.5 = (bf16[4,1,64,256]{3,2,1,0:T(8,128)(2,1)S(1)}, bf16[4,1,64,256]{3,2,1,0:T(8,128)(2,1)S(1)}, u32[]{:S(2)}, u32[]{:S(2)}) collective-permute-start(bf16[4,1,64,256]{3,2,1,0:T(8,128)(2,1)S(1)} %pad_maximum_fusion.7), channel_id=1, source_target_pairs={{0,16},{2,18},{4,20},{6,22},{8,24},{10,26},{12,28},{14,30},{16,0},... | collective-permute-start | bytes 393224 | tf_op jit(solution)/shard_map/ppermute | solution.py:97
  21.2 10.3 %collective-permute-start.6 = (bf16[4,1,64,256]{3,2,1,0:T(8,128)(2,1)S(1)}, bf16[4,1,64,256]{3,2,1,0:T(8,128)(2,1)S(1)}, u32[]{:S(2)}, u32[]{:S(2)}) collective-permute-start(bf16[4,1,64,256]{3,2,1,0:T(8,128)(2,1)S(1)} %pad_maximum_fusion.8), channel_id=1, source_target_pairs={{0,24},{2,26},{4,28},{6,30},{8,16},{10,18},{12,20},{14,22},{16,8},... | collective-permute-start | bytes 393224 | tf_op jit(solution)/shard_map/ppermute | solution.py:97
  22.7 10.3 %collective-permute-start.7 = (bf16[4,1,64,256]{3,2,1,0:T(8,128)(2,1)S(1)}, bf16[4,1,64,256]{3,2,1,0:T(8,128)(2,1)S(1)}, u32[]{:S(2)}, u32[]{:S(2)}) collective-permute-start(bf16[4,1,64,256]{3,2,1,0:T(8,128)(2,1)S(1)} %get-tuple-element.62), channel_id=1, source_target_pairs={{0,2},{2,0},{4,6},{6,4},{8,10},{10,8},{12,14},{14,12},{16,18},{18,... | collective-permute-start | bytes 393224 | tf_op jit(solution)/shard_map/ppermute | solution.py:97
  22.8 10.6 %collective-permute-start.8 = (bf16[4,1,64,256]{3,2,1,0:T(8,128)(2,1)S(1)}, bf16[4,1,64,256]{3,2,1,0:T(8,128)(2,1)S(1)}, u32[]{:S(2)}, u32[]{:S(2)}) collective-permute-start(bf16[4,1,64,256]{3,2,1,0:T(8,128)(2,1)S(1)} %get-tuple-element.63), channel_id=1, source_target_pairs={{0,4},{2,6},{4,0},{6,2},{8,12},{10,14},{12,8},{14,10},{16,20},{18,... | collective-permute-start | bytes 393224 | tf_op jit(solution)/shard_map/ppermute | solution.py:97
  25.8 7.7 %collective-permute-start.9 = (bf16[4,1,64,256]{3,2,1,0:T(8,128)(2,1)S(1)}, bf16[4,1,64,256]{3,2,1,0:T(8,128)(2,1)S(1)}, u32[]{:S(2)}, u32[]{:S(2)}) collective-permute-start(bf16[4,1,64,256]{3,2,1,0:T(8,128)(2,1)S(1)} %get-tuple-element.64), channel_id=1, source_target_pairs={{0,6},{2,4},{4,2},{6,0},{8,14},{10,12},{12,10},{14,8},{16,22},{18,... | collective-permute-start | bytes 393224 | tf_op jit(solution)/shard_map/ppermute | solution.py:97
  31.5 6.2 %collective-permute-start.13 = (bf16[4,2,64,256]{3,2,1,0:T(8,128)(2,1)S(1)}, bf16[4,2,64,256]{3,2,1,0:T(8,128)(2,1)S(1)}, u32[]{:S(2)}, u32[]{:S(2)}) collective-permute-start(bf16[4,2,64,256]{3,2,1,0:T(8,128)(2,1)S(1)} %get-tuple-element.66), channel_id=1, source_target_pairs={{0,2},{2,0},{4,6},{6,4},{8,10},{10,8},{12,14},{14,12},{16,18},{18,... | collective-permute-start | bytes 786440 | tf_op jit(solution)/shard_map/ppermute | solution.py:97
  31.5 9.1 %collective-permute-start.14 = (bf16[4,2,64,256]{3,2,1,0:T(8,128)(2,1)S(1)}, bf16[4,2,64,256]{3,2,1,0:T(8,128)(2,1)S(1)}, u32[]{:S(2)}, u32[]{:S(2)}) collective-permute-start(bf16[4,2,64,256]{3,2,1,0:T(8,128)(2,1)S(1)} %get-tuple-element.67), channel_id=1, source_target_pairs={{0,4},{2,6},{4,0},{6,2},{8,12},{10,14},{12,8},{14,10},{16,20},{18,... | collective-permute-start | bytes 786440 | tf_op jit(solution)/shard_map/ppermute | solution.py:97
  33.0 12.4 %collective-permute-start.15 = (bf16[4,2,64,256]{3,2,1,0:T(8,128)(2,1)S(1)}, bf16[4,2,64,256]{3,2,1,0:T(8,128)(2,1)S(1)}, u32[]{:S(2)}, u32[]{:S(2)}) collective-permute-start(bf16[4,2,64,256]{3,2,1,0:T(8,128)(2,1)S(1)} %get-tuple-element.68), channel_id=1, source_target_pairs={{0,6},{2,4},{4,2},{6,0},{8,14},{10,12},{12,10},{14,8},{16,22},{18,... | collective-permute-start | bytes 786440 | tf_op jit(solution)/shard_map/ppermute | solution.py:97
  33.5 12.1 %collective-permute-start.10 = (bf16[4,1,64,256]{3,2,1,0:T(8,128)(2,1)S(1)}, bf16[4,1,64,256]{3,2,1,0:T(8,128)(2,1)S(1)}, u32[]{:S(2)}, u32[]{:S(2)}) collective-permute-start(bf16[4,1,64,256]{3,2,1,0:T(8,128)(2,1)S(1)} %pad_maximum_fusion.10), channel_id=1, source_target_pairs={{0,8},{2,10},{4,12},{6,14},{8,0},{10,2},{12,4},{14,6},{16,24},{18,... | collective-permute-start | bytes 393224 | tf_op jit(solution)/shard_map/ppermute | solution.py:97
  36.5 13.0 %collective-permute-start.11 = (bf16[4,1,64,256]{3,2,1,0:T(8,128)(2,1)S(1)}, bf16[4,1,64,256]{3,2,1,0:T(8,128)(2,1)S(1)}, u32[]{:S(2)}, u32[]{:S(2)}) collective-permute-start(bf16[4,1,64,256]{3,2,1,0:T(8,128)(2,1)S(1)} %pad_maximum_fusion.11), channel_id=1, source_target_pairs={{0,16},{2,18},{4,20},{6,22},{8,24},{10,26},{12,28},{14,30},{16,0},... | collective-permute-start | bytes 393224 | tf_op jit(solution)/shard_map/ppermute | solution.py:97
  37.7 11.8 %collective-permute-start.12 = (bf16[4,1,64,256]{3,2,1,0:T(8,128)(2,1)S(1)}, bf16[4,1,64,256]{3,2,1,0:T(8,128)(2,1)S(1)}, u32[]{:S(2)}, u32[]{:S(2)}) collective-permute-start(bf16[4,1,64,256]{3,2,1,0:T(8,128)(2,1)S(1)} %pad_maximum_fusion.12), channel_id=1, source_target_pairs={{0,24},{2,26},{4,28},{6,30},{8,16},{10,18},{12,20},{14,22},{16,8},... | collective-permute-start | bytes 393224 | tf_op jit(solution)/shard_map/ppermute | solution.py:97
  49.5 39.0 %collective-permute-start.16 = (bf16[4,2,64,256]{3,2,1,0:T(8,128)(2,1)S(1)}, bf16[4,2,64,256]{3,2,1,0:T(8,128)(2,1)S(1)}, u32[]{:S(2)}, u32[]{:S(2)}) collective-permute-start(bf16[4,2,64,256]{3,2,1,0:T(8,128)(2,1)S(1)} %get-tuple-element.70), channel_id=1, source_target_pairs={{0,8},{2,10},{4,12},{6,14},{8,0},{10,2},{12,4},{14,6},{16,24},{18,... | collective-permute-start | bytes 786440 | tf_op jit(solution)/shard_map/ppermute | solution.py:97
  51.9 36.9 %collective-permute-start.17 = (bf16[4,2,64,256]{3,2,1,0:T(8,128)(2,1)S(1)}, bf16[4,2,64,256]{3,2,1,0:T(8,128)(2,1)S(1)}, u32[]{:S(2)}, u32[]{:S(2)}) collective-permute-start(bf16[4,2,64,256]{3,2,1,0:T(8,128)(2,1)S(1)} %get-tuple-element.71), channel_id=1, source_target_pairs={{0,16},{2,18},{4,20},{6,22},{8,24},{10,26},{12,28},{14,30},{16,0},... | collective-permute-start | bytes 786440 | tf_op jit(solution)/shard_map/ppermute | solution.py:97
  52.9 36.0 %collective-permute-start.18 = (bf16[4,2,64,256]{3,2,1,0:T(8,128)(2,1)S(1)}, bf16[4,2,64,256]{3,2,1,0:T(8,128)(2,1)S(1)}, u32[]{:S(2)}, u32[]{:S(2)}) collective-permute-start(bf16[4,2,64,256]{3,2,1,0:T(8,128)(2,1)S(1)} %get-tuple-element.72), channel_id=1, source_target_pairs={{0,24},{2,26},{4,28},{6,30},{8,16},{10,18},{12,20},{14,22},{16,8},... | collective-permute-start | bytes 786440 | tf_op jit(solution)/shard_map/ppermute | solution.py:97
  64.8 9.6 %collective-permute-start.25 = (bf16[4,64,256]{2,1,0:T(8,128)(2,1)S(1)}, bf16[4,64,256]{2,1,0:T(8,128)(2,1)S(1)}, u32[]{:S(2)}, u32[]{:S(2)}) collective-permute-start(bf16[4,64,256]{2,1,0:T(8,128)(2,1)S(1)} %get-tuple-element.86), channel_id=1, source_target_pairs={{0,8},{2,10},{4,12},{6,14},{8,0},{10,2},{12,4},{14,6},{16,24},{18,... | collective-permute-start | bytes 393224 | tf_op jit(solution)/shard_map/ppermute | solution.py:97
  65.9 20.8 %collective-permute-start.26 = (bf16[4,64,256]{2,1,0:T(8,128)(2,1)S(1)}, bf16[4,64,256]{2,1,0:T(8,128)(2,1)S(1)}, u32[]{:S(2)}, u32[]{:S(2)}) collective-permute-start(bf16[4,64,256]{2,1,0:T(8,128)(2,1)S(1)} %get-tuple-element.87), channel_id=1, source_target_pairs={{0,16},{2,18},{4,20},{6,22},{8,24},{10,26},{12,28},{14,30},{16,0},... | collective-permute-start | bytes 393224 | tf_op jit(solution)/shard_map/ppermute | solution.py:97
  74.4 12.3 %collective-permute-start.27 = (bf16[4,64,256]{2,1,0:T(8,128)(2,1)S(1)}, bf16[4,64,256]{2,1,0:T(8,128)(2,1)S(1)}, u32[]{:S(2)}, u32[]{:S(2)}) collective-permute-start(bf16[4,64,256]{2,1,0:T(8,128)(2,1)S(1)} %get-tuple-element.88), channel_id=1, source_target_pairs={{0,24},{2,26},{4,28},{6,30},{8,16},{10,18},{12,20},{14,22},{16,8},... | collective-permute-start | bytes 393224 | tf_op jit(solution)/shard_map/ppermute | solution.py:97
  86.7 29.6 %collective-permute-start.28 = (bf16[4,64,256]{2,1,0:T(8,128)(2,1)S(1)}, bf16[4,64,256]{2,1,0:T(8,128)(2,1)S(1)}, u32[]{:S(2)}, u32[]{:S(2)}) collective-permute-start(bf16[4,64,256]{2,1,0:T(8,128)(2,1)S(1)} %pad_maximum_fusion.18), channel_id=1, source_target_pairs={{0,2},{2,0},{4,6},{6,4},{8,10},{10,8},{12,14},{14,12},{16,18},{18,... | collective-permute-start | bytes 393224 | tf_op jit(solution)/shard_map/ppermute | solution.py:97
  86.8 29.9 %collective-permute-start.29 = (bf16[4,64,256]{2,1,0:T(8,128)(2,1)S(1)}, bf16[4,64,256]{2,1,0:T(8,128)(2,1)S(1)}, u32[]{:S(2)}, u32[]{:S(2)}) collective-permute-start(bf16[4,64,256]{2,1,0:T(8,128)(2,1)S(1)} %pad_maximum_fusion.19), channel_id=1, source_target_pairs={{0,4},{2,6},{4,0},{6,2},{8,12},{10,14},{12,8},{14,10},{16,20},{18,... | collective-permute-start | bytes 393224 | tf_op jit(solution)/shard_map/ppermute | solution.py:97
  88.5 28.3 %collective-permute-start.30 = (bf16[4,64,256]{2,1,0:T(8,128)(2,1)S(1)}, bf16[4,64,256]{2,1,0:T(8,128)(2,1)S(1)}, u32[]{:S(2)}, u32[]{:S(2)}) collective-permute-start(bf16[4,64,256]{2,1,0:T(8,128)(2,1)S(1)} %pad_maximum_fusion.20), channel_id=1, source_target_pairs={{0,6},{2,4},{4,2},{6,0},{8,14},{10,12},{12,10},{14,8},{16,22},{18,... | collective-permute-start | bytes 393224 | tf_op jit(solution)/shard_map/ppermute | solution.py:97
  99.3 17.5 %copy-start.2 = (bf16[256,2048]{1,0:T(8,128)(2,1)S(1)}, bf16[256,2048]{1,0:T(8,128)(2,1)}, u32[]{:S(2)}) copy-start(bf16[256,2048]{1,0:T(8,128)(2,1)} %gate_ref.3) | copy-start | bytes 3145732
  99.3 17.5 %copy-start.7 = (f32[3,2048]{1,0:T(4,128)S(1)}, f32[3,2048]{1,0:T(4,128)}, u32[]{:S(2)}) copy-start(f32[3,2048]{1,0:T(4,128)} %taps_ref.3) | copy-start | bytes 73732
  99.3 8.4 %collective-permute-start.19 = (bf16[4,64,256]{2,1,0:T(8,128)(2,1)S(1)}, bf16[4,64,256]{2,1,0:T(8,128)(2,1)S(1)}, u32[]{:S(2)}, u32[]{:S(2)}) collective-permute-start(bf16[4,64,256]{2,1,0:T(8,128)(2,1)S(1)} %get-tuple-element.74), channel_id=1, source_target_pairs={{0,8},{2,10},{4,12},{6,14},{8,0},{10,2},{12,4},{14,6},{16,24},{18,... | collective-permute-start | bytes 393224 | tf_op jit(solution)/shard_map/ppermute | solution.py:97
  101.3 10.6 %collective-permute-start.20 = (bf16[4,64,256]{2,1,0:T(8,128)(2,1)S(1)}, bf16[4,64,256]{2,1,0:T(8,128)(2,1)S(1)}, u32[]{:S(2)}, u32[]{:S(2)}) collective-permute-start(bf16[4,64,256]{2,1,0:T(8,128)(2,1)S(1)} %get-tuple-element.75), channel_id=1, source_target_pairs={{0,16},{2,18},{4,20},{6,22},{8,24},{10,26},{12,28},{14,30},{16,0},... | collective-permute-start | bytes 393224 | tf_op jit(solution)/shard_map/ppermute | solution.py:97
  107.7 6.9 %collective-permute-start.21 = (bf16[4,64,256]{2,1,0:T(8,128)(2,1)S(1)}, bf16[4,64,256]{2,1,0:T(8,128)(2,1)S(1)}, u32[]{:S(2)}, u32[]{:S(2)}) collective-permute-start(bf16[4,64,256]{2,1,0:T(8,128)(2,1)S(1)} %get-tuple-element.76), channel_id=1, source_target_pairs={{0,24},{2,26},{4,28},{6,30},{8,16},{10,18},{12,20},{14,22},{16,8},... | collective-permute-start | bytes 393224 | tf_op jit(solution)/shard_map/ppermute | solution.py:97
  114.6 3.2 %collective-permute-start.22 = (bf16[4,64,256]{2,1,0:T(8,128)(2,1)S(1)}, bf16[4,64,256]{2,1,0:T(8,128)(2,1)S(1)}, u32[]{:S(2)}, u32[]{:S(2)}) collective-permute-start(bf16[4,64,256]{2,1,0:T(8,128)(2,1)S(1)} %pad_maximum_fusion.14), channel_id=1, source_target_pairs={{0,2},{2,0},{4,6},{6,4},{8,10},{10,8},{12,14},{14,12},{16,18},{18,... | collective-permute-start | bytes 393224 | tf_op jit(solution)/shard_map/ppermute | solution.py:97
  114.7 6.4 %collective-permute-start.23 = (bf16[4,64,256]{2,1,0:T(8,128)(2,1)S(1)}, bf16[4,64,256]{2,1,0:T(8,128)(2,1)S(1)}, u32[]{:S(2)}, u32[]{:S(2)}) collective-permute-start(bf16[4,64,256]{2,1,0:T(8,128)(2,1)S(1)} %pad_maximum_fusion.15), channel_id=1, source_target_pairs={{0,4},{2,6},{4,0},{6,2},{8,12},{10,14},{12,8},{14,10},{16,20},{18,... | collective-permute-start | bytes 393224 | tf_op jit(solution)/shard_map/ppermute | solution.py:97
  116.3 6.8 %collective-permute-start.24 = (bf16[4,64,256]{2,1,0:T(8,128)(2,1)S(1)}, bf16[4,64,256]{2,1,0:T(8,128)(2,1)S(1)}, u32[]{:S(2)}, u32[]{:S(2)}) collective-permute-start(bf16[4,64,256]{2,1,0:T(8,128)(2,1)S(1)} %pad_maximum_fusion.16), channel_id=1, source_target_pairs={{0,6},{2,4},{4,2},{6,0},{8,14},{10,12},{12,10},{14,8},{16,22},{18,... | collective-permute-start | bytes 393224 | tf_op jit(solution)/shard_map/ppermute | solution.py:97
  117.8 10.0 %copy-start.8 = (f32[2048]{0:T(1024)S(1)}, f32[2048]{0:T(1024)}, u32[]{:S(2)}) copy-start(f32[2048]{0:T(1024)} %param.17) | copy-start | bytes 24580
  124.0 3.7 %collective-permute-start.31 = (f32[8,256]{1,0:T(8,128)S(1)}, f32[8,256]{1,0:T(8,128)S(1)}, u32[]{:S(2)}, u32[]{:S(2)}) collective-permute-start(f32[8,256]{1,0:T(8,128)S(1)} %get-tuple-element.92.refs_0_), channel_id=1, source_target_pairs={{0,1},{1,0},{2,3},{3,2},{4,5},{5,4},{6,7},{7,6},{8,9},{9,8},{10,11... | collective-permute-start | bytes 24584 | tf_op jit(solution)/shard_map/ppermute | solution.py:434
where the time goes:
time: 130 us
  waiting for transfers between devices  55.3 us (43%)
  starting transfers between devices  40.9 us (31%)
  Pallas kernels  27.4 us (21%)
  local copies, waits for them, and re-layouts  5.09 us (4%)
    ppermute x30, waiting for transfers between devices, swapped(): return lax.ppermute(rows, 'seq', [(i, i ^ by) for i in range(size)])  53.1 us
    ppermute x30, starting transfers between devices, swapped(): return lax.ppermute(rows, 'seq', [(i, i ^ by) for i in range(size)])  37 us
    pallas_call x2, Pallas kernels, long_conv(): pl.pallas_call(conv_kernel, grid_spec=pltpu.PrefetchScalarGridSpec(num_sc...  20.7 us
    pallas_call x3, Pallas kernels, packed(): pl.pallas_call(functools.partial(pack_kernel, wants), grid_spec=pltpu.Pre...  2.89 us
    slice x3, local copies, waits for them, and re-layouts, local(): a[tok - HALO:]  2.68 us
  transfers between devices with their start and end apart: 32, of which 14 were waited for; matrix products, arithmetic and copies ran while one was open for 1% of the time, Pallas kernels for 19%

commit v1 on v0

--- a/solution.py
+++ b/solution.py
@@ -15,6 +15,7 @@
 PARTS = 2
 NEAR = 4
 VMEM_BYTES = 20 * 1024 * 1024
+BRIEF = pl.CostEstimate(flops=1000, bytes_accessed=1000, transcendentals=0)
 F32 = jnp.float32
 BF16 = jnp.bfloat16
 
@@ -34,41 +35,35 @@
     return taps[0:1] * rows + taps[1:2] * one + taps[2:3] * two
 
 
-def send_out(held, outs, origin):
-    for near, out_ref in enumerate(outs):
-        for far in range(out_ref.shape[0]):
-            out_ref[far] = held[origin ^ (far * len(outs) + near)]
-
-
 def pack_kernel(wants, at_ref, *refs):
-    refs, outs, held = refs[: -NEAR - 1], refs[-NEAR - 1 : -1], refs[-1]
-    blocks, _, narrow, tok = held.shape
+    arrays = len(wants) + 4 * ("product" in wants)
+    refs, outs, held = list(refs[:arrays]), refs[arrays:-1], refs[-1]
+    _, _, narrow, tok = held.shape
+    near = outs[0].shape[0]
     count = WIDE // narrow
     step = pl.program_id(0)
-    here = pl.ds(step * count, count)
-    refs = list(refs)
     for at, want in enumerate(wants):
         if want == "filter":
-            packed = refs.pop(0)[...].astype(F32)
+            rows = refs.pop(0)[...].astype(F32)
         else:
             key, value, halo, key_taps, value_taps = [refs.pop(0)[...] for _ in range(5)]
             halo = halo.astype(F32)
-            packed = short_conv(key.astype(F32), halo[:HALO], key_taps)
-            packed *= short_conv(value.astype(F32), halo[HALO : 2 * HALO], value_taps)
-        held[here, at] = packed.T.astype(BF16).reshape(count, narrow, tok)
+            rows = short_conv(key.astype(F32), halo[:HALO], key_taps)
+            rows *= short_conv(value.astype(F32), halo[HALO : 2 * HALO], value_taps)
+        held[pl.ds(step * count, count), at] = rows.T.astype(BF16).reshape(count, narrow, tok)
 
     @pl.when(step == pl.num_programs(0) - 1)
     def _():
-        for near, out_ref in enumerate(outs):
-            for far in range(blocks // NEAR):
-                out_ref[far] = held[at_ref[0] ^ (far * NEAR + near)]
-
-
-def packed(wants, arrays, part, position):
+        for j, out_ref in enumerate(outs):
+            for i in range(near):
+                out_ref[i] = held[at_ref[0] ^ (near * j + i)]
+
+
+def packed(wants, arrays, part, near, position):
     start, narrow, blocks = part
     tok = arrays[0].shape[0]
     first = start // WIDE
-    shape = (blocks // NEAR, len(wants), narrow, tok)
+    shape = (near, len(wants), narrow, tok)
     return pl.pallas_call(
         functools.partial(pack_kernel, wants),
         grid_spec=pltpu.PrefetchScalarGridSpec(
@@ -78,18 +73,31 @@
                 pl.BlockSpec((array.shape[0], WIDE), lambda i, at: (0, first + i))
                 for array in arrays
             ],
-            out_specs=[pl.BlockSpec(shape, lambda i, at: (0, 0, 0, 0))] * NEAR,
+            out_specs=[pl.BlockSpec(shape, lambda i, at: (0, 0, 0, 0))] * (blocks // near),
             scratch_shapes=[pltpu.VMEM((blocks,) + shape[1:], BF16)],
         ),
-        out_shape=[jax.ShapeDtypeStruct(shape, BF16)] * NEAR,
+        out_shape=[jax.ShapeDtypeStruct(shape, BF16)] * (blocks // near),
         compiler_params=pltpu.CompilerParams(vmem_limit_bytes=VMEM_BYTES),
-        cost_estimate=pl.CostEstimate(
-            flops=8 * len(arrays) * tok * blocks * narrow,
-            bytes_accessed=4 * len(arrays) * tok * blocks * narrow,
-            transcendentals=0,
-        ),
+        cost_estimate=BRIEF,
         name="pack_" + "_".join(wants),
     )(position, *arrays)
+
+
+def tails_kernel(*refs):
+    for at, ref in enumerate(refs[:-1]):
+        refs[-1][at * HALO : (at + 1) * HALO, :] = ref[...]
+
+
+def tails(arrays):
+    tok, width = arrays[0].shape
+    return pl.pallas_call(
+        tails_kernel,
+        grid=(1,),
+        in_specs=[pl.BlockSpec((HALO, width), lambda i: (tok // HALO - 1, 0))] * len(arrays),
+        out_specs=pl.BlockSpec((HALO * len(arrays), width), lambda i: (0, 0)),
+        out_shape=jax.ShapeDtypeStruct((HALO * len(arrays), width), BF16),
+        name="tails",
+    )(*arrays)
 
 
 def swapped(rows, by):
@@ -97,19 +105,20 @@
     return lax.ppermute(rows, "seq", [(i, i ^ by) for i in range(size)])
 
 
-def swap_near(parts):
-    parts = [parts[0]] + [swapped(parts[i], i) for i in range(1, len(parts))]
-    return [jnp.stack([part[j] for part in parts]) for j in range(parts[0].shape[0])]
-
-
 def swap_far(lines):
-    return [lines[0]] + [swapped(lines[j], NEAR * j) for j in range(1, len(lines))]
-
-
-def swap_back(lines):
-    lines = swap_far(lines)
+    order = sorted(range(1, len(lines)), key=lambda j: j == 1)
+    came = {j: swapped(lines[j], NEAR * j) for j in order}
+    return [lines[0]] + [came[j] for j in range(1, len(lines))]
+
+
+def swap_near(lines):
     parts = [jnp.stack([line[i] for line in lines]) for i in range(NEAR)]
     return [parts[0]] + [swapped(parts[i], i) for i in range(1, NEAR)]
+
+
+def after(arrays, *others):
+    tokens = [other[(slice(0, 1),) * other.ndim] for other in others]
+    return lax.optimization_barrier((arrays, tokens))[0]
 
 
 def delayed(rows, by):
@@ -145,19 +154,21 @@
 def conv_kernel(at_ref, skip_ref, *refs):
     refs, (filt, prod, base, left, total, held) = refs[:-6], refs[-6:]
     blocks, lanes, tok = prod.shape
-    far = blocks // NEAR
-    in_refs, out_refs = refs[:-far], refs[-far:]
+    near = next(at for at, ref in enumerate(refs) if len(ref.shape) == 3)
+    in_refs, out_refs = refs[:near], refs[near:]
+    merged = in_refs[0].shape[1] == 2
+    count = near if merged else near // 2
+    filt_refs, prod_refs = in_refs[:count], in_refs[-count:]
     length = blocks * tok
     turns = blocks // 2
     units = lanes // 16
 
-    merged = in_refs[0].shape[1] == 2
-    for j in range(far):
-        for i in range(NEAR):
-            block = at_ref[0] ^ (NEAR * j + i)
+    for i, (filt_ref, prod_ref) in enumerate(zip(filt_refs, prod_refs)):
+        for j in range(filt_ref.shape[0]):
+            block = at_ref[0] ^ (len(filt_refs) * j + i)
             lags = pl.ds(pl.multiple_of(block * tok, tok), tok)
-            filt[:, lags] = in_refs[j][i, 0].astype(F32)
-            prod[block] = (in_refs[j][i, 1] if merged else in_refs[far + j][i, 0]).astype(F32)
+            filt[:, lags] = filt_ref[j, 0].astype(F32)
+            prod[block] = prod_ref[j, int(merged)].astype(F32)
     base[:, :, :LANES] = jnp.zeros((2, GROUP * FINE, LANES), BF16)
 
     def pairs_of(row, side):
@@ -251,24 +262,22 @@
         return carry
 
     lax.fori_loop(0, units, unit, 0)
-    for j in range(far):
-        for i in range(NEAR):
-            out_refs[j][i] = held[at_ref[0] ^ (NEAR * j + i)]
-
-
-def long_conv(arrays, skip_rows, blocks, position):
-    near, _, lanes, tok = arrays[0].shape
-    far = blocks // near
+    for j, out_ref in enumerate(out_refs):
+        for i in range(out_ref.shape[0]):
+            out_ref[i] = held[at_ref[0] ^ (out_ref.shape[0] * j + i)]
+
+
+def long_conv(arrays, skip_rows, blocks, near, position, cost=BRIEF):
+    _, _, lanes, tok = arrays[0].shape
     length = blocks * tok
-    whole = lambda array: pl.BlockSpec(array.shape, lambda i, at: (0,) * array.ndim)
-    operands = [skip_rows, *arrays]
-    out_shape = [jax.ShapeDtypeStruct((near, lanes, tok), BF16)] * far
+    whole = lambda array: pl.BlockSpec(array.shape, lambda i, at: (0,) * len(array.shape))
+    out_shape = [jax.ShapeDtypeStruct((near, lanes, tok), BF16)] * (blocks // near)
     return pl.pallas_call(
         conv_kernel,
         grid_spec=pltpu.PrefetchScalarGridSpec(
             num_scalar_prefetch=1,
             grid=(1,),
-            in_specs=[whole(array) for array in operands],
+            in_specs=[whole(array) for array in (skip_rows, *arrays)],
             out_specs=[whole(array) for array in out_shape],
             scratch_shapes=[
                 pltpu.VMEM((lanes, length), F32),
@@ -281,17 +290,17 @@
         ),
         out_shape=out_shape,
         compiler_params=pltpu.CompilerParams(vmem_limit_bytes=VMEM_BYTES),
-        cost_estimate=pl.CostEstimate(
-            flops=64 * lanes * length * 256, bytes_accessed=6 * lanes * length, transcendentals=0
-        ),
+        cost_estimate=cost,
         name="long_conv",
-    )(position, *operands)
+    )(position, skip_rows, *arrays)
 
 
 def gated_kernel(at_ref, gate_ref, halo_ref, taps_ref, *refs):
-    mixed_refs, refs, held = refs[:NEAR], refs[NEAR:-1], refs[-1]
+    held = refs[-1]
+    blocks, narrow, tok = held.shape
+    near = blocks // refs[0].shape[0]
+    mixed_refs, refs = refs[:near], refs[near:-1]
     gated_ref, squares_ref = refs[-2:]
-    _, narrow, tok = held.shape
     count = WIDE // narrow
     step = pl.program_id(0)
 
@@ -299,7 +308,7 @@
     def _():
         for i, mixed_ref in enumerate(mixed_refs):
             for j in range(mixed_ref.shape[0]):
-                held[at_ref[0] ^ (NEAR * j + i)] = mixed_ref[j]
+                held[at_ref[0] ^ (near * j + i)] = mixed_ref[j]
 
     halo = halo_ref[...].astype(F32)
     gate = short_conv(gate_ref[...].astype(F32), halo[2 * HALO :], taps_ref[...])
@@ -324,7 +333,8 @@
 def gated_of(gate_in, halo, gate_short, mixed, start, before, position):
     tok, full = gate_in.shape
     far, narrow, _ = mixed[0].shape
-    width = NEAR * far * narrow
+    near = len(mixed)
+    width = near * far * narrow
     first = start // WIDE
     column = lambda rows: pl.BlockSpec((rows, WIDE), lambda i, at: (0, first + i))
     sums = pl.BlockSpec((8, tok), lambda i, at: (0, 0))
@@ -335,20 +345,18 @@
             num_scalar_prefetch=1,
             grid=(width // WIDE,),
             in_specs=[column(tok), column(3 * HALO), column(3)]
-            + [pl.BlockSpec(mixed[0].shape, lambda i, at: (0, 0, 0))] * NEAR
+            + [pl.BlockSpec(mixed[0].shape, lambda i, at: (0, 0, 0))] * near
             + more,
             out_specs=[column(tok), sums],
-            scratch_shapes=[pltpu.VMEM((NEAR * far, narrow, tok), BF16)],
+            scratch_shapes=[pltpu.VMEM((near * far, narrow, tok), BF16)],
         ),
         out_shape=[
             jax.ShapeDtypeStruct((tok, full), F32),
             jax.ShapeDtypeStruct((8, tok), F32),
         ],
-        input_output_aliases={5 + NEAR: 0} if more else {},
+        input_output_aliases={5 + near: 0} if more else {},
         compiler_params=pltpu.CompilerParams(vmem_limit_bytes=VMEM_BYTES),
-        cost_estimate=pl.CostEstimate(
-            flops=10 * tok * width, bytes_accessed=8 * tok * width, transcendentals=0
-        ),
+        cost_estimate=BRIEF,
         name="gated_squares",
     )(
         position,
@@ -383,9 +391,7 @@
         out_specs=column(tok),
         out_shape=jax.ShapeDtypeStruct((tok, width), BF16),
         compiler_params=pltpu.CompilerParams(vmem_limit_bytes=VMEM_BYTES),
-        cost_estimate=pl.CostEstimate(
-            flops=4 * tok * width, bytes_accessed=6 * tok * width, transcendentals=tok
-        ),
+        cost_estimate=BRIEF,
         name="normed",
     )(gated, norm_gain, *squares)
 
@@ -398,36 +404,40 @@
     groups = lax.axis_size("ch")
     place = lax.axis_index("seq")
     position = jnp.full((1,), place, jnp.int32)
-    halo = passed_along(
-        jnp.concatenate([a[tok - HALO :] for a in (key_in, value_in, gate_in)], axis=0), "seq", 1
-    )
     narrow = width // blocks // PARTS
     starts = [at * narrow * blocks for at in range(PARTS)]
-    pack = lambda wants, start: packed(
+    exchange = lambda rows: lax.all_to_all(rows, "seq", split_axis=0, concat_axis=0, tiled=True)
+    natural = jnp.zeros((1,), jnp.int32)
+    pack = lambda wants, start, near, origin: packed(
         wants,
         ([long_filter] if "filter" in wants else [])
         + ([key_in, value_in, halo, key_short, value_short] if "product" in wants else []),
         (start, narrow, blocks),
-        position,
+        near,
+        origin,
     )
-    far = blocks // NEAR
-    sent = [pack(("filter",), starts[0]), pack(("product",), starts[0])]
-    arrived = [[]]
-    for parts in sent:
-        arrived[0] += swap_far(swap_near(parts))
-    for start in starts[1:]:
-        parts = pack(("filter", "product"), start)
-        arrived[0][:far], parts = lax.optimization_barrier((arrived[0][:far], parts))
-        arrived[-1], lines = lax.optimization_barrier((arrived[-1], swap_near(parts)))
-        arrived.append(swap_far(lines))
-    mixed = []
-    for start, arrays in zip(starts, arrived):
+
+    def skip_of(start):
         skip = lax.dynamic_slice_in_dim(skip_gain, start + place * narrow, narrow, 0)
-        skip = jnp.broadcast_to(skip[:, None], (narrow, LANES))
-        mixed.append(swap_back(long_conv(arrays, skip, blocks, position)))
-    gated = None
-    for start, part in zip(starts, mixed):
-        gated = gated_of(gate_in, halo, gate_short, part, start, gated, position)
+        return jnp.broadcast_to(skip[:, None], (narrow, LANES))
+
+    lines = pack(("filter",), starts[0], NEAR, position)
+    halo = passed_along(tails((key_in, value_in, gate_in)), "seq", 1)
+    came = swap_far(pack(("product",), starts[0], NEAR, position))
+    filters = swap_near(after(swap_far(lines), came[2]))
+    products = swap_near(came)
+    second = pack(("filter", "product"), starts[1], blocks, natural)[0]
+    second = exchange(after(second, came[2]))
+    lines = long_conv(filters + products, skip_of(starts[0]), blocks, NEAR, position)
+    lines = swap_far(after(lines, second))
+    cost = pl.CostEstimate(
+        flops=2 * width * tok * tok * blocks, bytes_accessed=6 * tok * width, transcendentals=0
+    )
+    last = long_conv([second], skip_of(starts[1]), blocks, blocks, natural, cost)[0]
+    lines, last = lax.optimization_barrier((lines, last))
+    last = exchange(last)
+    gated = gated_of(gate_in, halo, gate_short, swap_near(lines), starts[0], None, position)
+    gated = gated_of(gate_in, halo, gate_short, [last], starts[1], gated, natural)
     gated, squares = gated
     sums = [squares]
     for by in range(1, groups):

time: 130 us -> 115 us (0.88)
  waiting for transfers between devices: 55.3 us -> 40.6 us
  starting transfers between devices: 40.9 us -> 35.5 us
  Pallas kernels: 27.4 us -> 32.3 us
    ppermute x30 -> x18, waiting for transfers between devices: 53.1 us -> 37.6 us  [swapped(): return lax.ppermute(rows, 'seq', [(i, i ^ by) for i in range(size)])]
    ppermute x30 -> x18, starting transfers between devices: 37 us -> 23 us  [swapped(): return lax.ppermute(rows, 'seq', [(i, i ^ by) for i in range(size)])]
    all_to_all x0 -> x2, starting transfers between devices: none -> 8.58 us  [local(): lax.all_to_all(rows, 'seq', split_axis=0, concat_axis=0, tiled=True)]
    pallas_call x0 -> x1, Pallas kernels: none -> 1.76 us  [tails(): pl.pallas_call(tails_kernel, grid=(1,), in_specs=[pl.BlockSpec((HALO, wid...]
    pallas_call x3, Pallas kernels: 2.89 us -> 4.33 us  [packed(): pl.pallas_call(functools.partial(pack_kernel, wants), grid_spec=pltpu.Pre...]
    slice x23 -> x10, local copies, waits for them, and re-layouts: 2.91 us -> 2.62 us  [swap_near(): parts = [jnp.stack([line[i] for line in lines]) for i in range(NEAR)]]
  transfers between devices with their start and end apart: 32 -> 22, of which waited for: 14 -> 10; matrix products, arithmetic and copies ran while one was open for 1% -> 3% of each run, Pallas kernels for 19% -> 23%
where the time goes in v1:
time: 115 us; the launch traced here: 114 us
  waiting for transfers between devices  40.6 us (35%)
  starting transfers between devices  35.5 us (31%)
  Pallas kernels  32.3 us (28%)
  local copies, waits for them, and re-layouts  5.18 us (5%)
    ppermute x18, waiting for transfers between devices, swapped(): return lax.ppermute(rows, 'seq', [(i, i ^ by) for i in range(size)])  37.6 us
    ppermute x18, starting transfers between devices, swapped(): return lax.ppermute(rows, 'seq', [(i, i ^ by) for i in range(size)])  23 us
    pallas_call x2, Pallas kernels, long_conv(): pl.pallas_call(conv_kernel, grid_spec=pltpu.PrefetchScalarGridSpec(num_sc...  21.5 us
    all_to_all x2, starting transfers between devices, local(): lax.all_to_all(rows, 'seq', split_axis=0, concat_axis=0, tiled=True)  8.58 us
    pallas_call x3, Pallas kernels, packed(): pl.pallas_call(functools.partial(pack_kernel, wants), grid_spec=pltpu.Pre...  4.33 us
    pallas_call x2, Pallas kernels, gated_of(): pl.pallas_call(gated_kernel, grid_spec=pltpu.PrefetchScalarGridSpec(num_s...  2.9 us
    slice x10, local copies, waits for them, and re-layouts, swap_near(): parts = [jnp.stack([line[i] for line in lines]) for i in range(NEAR)]  2.62 us
    ppermute x1, starting transfers between devices, passed_along(): return lax.ppermute(array, axis, pairs)  2.37 us
  transfers between devices with their start and end apart: 22, of which 10 were waited for; matrix products, arithmetic and copies ran while one was open for 3% of the time, Pallas kernels for 23%

profile of v1, /device:TPU:0, one launch (start us, length us, event | category | flops | bytes accessed | tf_op | source)
XLA Modules:
  0.0 114.2 jit_solution(8838358430953879207)
XLA Ops:
  0.0 1.8 %tails.1 = bf16[48,2048]{1,0:T(8,128)(2,1)} custom-call(bf16[256,2048]{1,0:T(8,128)(2,1)} %refs_1_.5, bf16[256,2048]{1,0:T(8,128)(2,1)} %refs_2_.3, bf16[256,2048]{1,0:T(8,128)(2,1)} %gate_ref.3), custom_call_target="tpu_custom_call" | custom-call | tf_op jit(solution)/shard_map/tails/pallas_call | solution.py:93
  1.8 2.4 %collective-permute-start = (bf16[48,2048]{1,0:T(8,128)(2,1)}, bf16[48,2048]{1,0:T(8,128)(2,1)S(1)}, u32[]{:S(2)}, u32[]{:S(2)}) collective-permute-start(bf16[48,2048]{1,0:T(8,128)(2,1)} %tails.1), channel_id=1, source_target_pairs={{0,2},{2,4},{4,6},{6,8},{8,10},{10,12},{12,14},{14,16},{16,18},{18... | collective-permute-start | bytes 589832 | tf_op jit(solution)/shard_map/ppermute | solution.py:26
  4.2 1.1 pack_filter.1
  5.3 2.6 %collective-permute-start.1 = (bf16[4,1,64,256]{3,2,1,0:T(8,128)(2,1)}, bf16[4,1,64,256]{3,2,1,0:T(8,128)(2,1)}, u32[]{:S(2)}, u32[]{:S(2)}) collective-permute-start(bf16[4,1,64,256]{3,2,1,0:T(8,128)(2,1)} %get-tuple-element.32), channel_id=1, source_target_pairs={{0,8},{2,10},{4,12},{6,14},{8,0},{10,2},{12,4},{14,6},{16,24},{18,... | collective-permute-start | bytes 393224 | tf_op jit(solution)/shard_map/ppermute | solution.py:105
  7.9 2.6 %collective-permute-start.2 = (bf16[4,1,64,256]{3,2,1,0:T(8,128)(2,1)}, bf16[4,1,64,256]{3,2,1,0:T(8,128)(2,1)}, u32[]{:S(2)}, u32[]{:S(2)}) collective-permute-start(bf16[4,1,64,256]{3,2,1,0:T(8,128)(2,1)} %get-tuple-element.33), channel_id=1, source_target_pairs={{0,16},{2,18},{4,20},{6,22},{8,24},{10,26},{12,28},{14,30},{16,0},... | collective-permute-start | bytes 393224 | tf_op jit(solution)/shard_map/ppermute | solution.py:105
  10.5 0.0 collective-permute-start.3
  10.5 0.8 fusion.12
  11.3 0.0 collective-permute-done.refs_2_.refs_3_.halo_ref
  11.3 1.9 %pack_product.1 = (bf16[4,1,64,256]{3,2,1,0:T(8,128)(2,1)S(1)}, bf16[4,1,64,256]{3,2,1,0:T(8,128)(2,1)}, bf16[4,1,64,256]{3,2,1,0:T(8,128)(2,1)S(1)}, bf16[4,1,64,256]{3,2,1,0:T(8,128)(2,1)}) custom-call(s32[1]{0:T(128)} %bitcast.at_ref, bf16[256,2048]{1,0:T(8,128)(2,1)S(1)} %copy-done, bf16[256,2048]{1,0:T(8,128)(2,1)S(1)} %copy-done.1, ...), custom_call_target="tpu_custom_call" | custom-call | flops 1000 | bytes 1000 | tf_op jit(solution)/shard_map/pack_product/pallas_call | solution.py:67
  13.1 2.6 %collective-permute-start.4 = (bf16[4,1,64,256]{3,2,1,0:T(8,128)(2,1)S(1)}, bf16[4,1,64,256]{3,2,1,0:T(8,128)(2,1)S(1)}, u32[]{:S(2)}, u32[]{:S(2)}) collective-permute-start(bf16[4,1,64,256]{3,2,1,0:T(8,128)(2,1)S(1)} %get-tuple-element.35), channel_id=1, source_target_pairs={{0,16},{2,18},{4,20},{6,22},{8,24},{10,26},{12,28},{14,30},{16,0},... | collective-permute-start | bytes 393224 | tf_op jit(solution)/shard_map/ppermute | solution.py:105
  15.8 1.8 %collective-permute-start.8 = (bf16[4,1,64,256]{3,2,1,0:T(8,128)(2,1)}, bf16[4,1,64,256]{3,2,1,0:T(8,128)(2,1)}, u32[]{:S(2)}, u32[]{:S(2)}) collective-permute-start(bf16[4,1,64,256]{3,2,1,0:T(8,128)(2,1)} %get-tuple-element.41), channel_id=1, source_target_pairs={{0,8},{2,10},{4,12},{6,14},{8,0},{10,2},{12,4},{14,6},{16,24},{18,... | collective-permute-start | bytes 393224 | tf_op jit(solution)/shard_map/ppermute | solution.py:105
  17.6 1.3 %pack_filter_product.1 = bf16[16,2,64,256]{3,2,1,0:T(8,128)(2,1)S(1)} custom-call(s32[1]{0:T(128)} %constant.3.clone.1.at_ref, bf16[256,2048]{1,0:T(8,128)(2,1)S(1)} %copy-done.3, bf16[256,2048]{1,0:T(8,128)(2,1)S(1)} %copy-done, bf16[256,2048]{1,0:T(8,128)(2,1)S(1)} %copy-done.1, bf16[48,2048]{1,0:T(8,128)(2,1)S(1)} %collective-permute-done.refs_2_.refs_3_.halo_ref, ...), custom_call_target="tpu_custom_call" | custom-call | flops 1000 | bytes 1000 | tf_op jit(solution)/shard_map/pack_filter_product/pallas_call | solution.py:67
  18.9 0.0 copy-start.4
  18.9 1.0 copy-done.4
  19.9 9.2 %collective-permute-done.4 = bf16[4,1,64,256]{3,2,1,0:T(8,128)(2,1)S(1)} collective-permute-done((bf16[4,1,64,256]{3,2,1,0:T(8,128)(2,1)S(1)}, bf16[4,1,64,256]{3,2,1,0:T(8,128)(2,1)S(1)}, u32[]{:S(2)}, u32[]{:S(2)}) %collective-permute-start.4) | collective-permute-done | bytes 131104 | tf_op jit(solution)/shard_map/ppermute | solution.py:105
  29.1 0.6 copy-done.9
  29.8 2.5 %collective-permute-start.9 = (bf16[4,1,64,256]{3,2,1,0:T(8,128)(2,1)}, bf16[4,1,64,256]{3,2,1,0:T(8,128)(2,1)S(1)}, u32[]{:S(2)}, u32[]{:S(2)}) collective-permute-start(bf16[4,1,64,256]{3,2,1,0:T(8,128)(2,1)} %get-tuple-element.42), channel_id=1, source_target_pairs={{0,24},{2,26},{4,28},{6,30},{8,16},{10,18},{12,20},{14,22},{16,8},... | collective-permute-start | bytes 393224 | tf_op jit(solution)/shard_map/ppermute | solution.py:105
  32.3 3.7 %all-to-all-start = ((bf16[16,2,64,256]{3,2,1,0:T(8,128)(2,1)}), bf16[16,2,64,256]{3,2,1,0:T(8,128)(2,1)S(1)}, u32[]{:S(2)}, u32[]{:S(2)}) async-start(bf16[16,2,64,256]{3,2,1,0:T(8,128)(2,1)} %copy-done.4), calls=%async_computation | async-start | bytes 2097152 | tf_op jit(solution)/shard_map/all_to_all | solution.py:409
  36.1 0.0 collective-permute-done.8
  36.1 0.8 fusion.5
  36.9 0.5 collective-permute-done.9
  37.4 0.1 collective-permute-start.10
  37.6 1.7 %collective-permute-start.11 = (bf16[4,1,64,256]{3,2,1,0:T(8,128)(2,1)S(1)}, bf16[4,1,64,256]{3,2,1,0:T(8,128)(2,1)S(1)}, u32[]{:S(2)}, u32[]{:S(2)}) collective-permute-start(bf16[4,1,64,256]{3,2,1,0:T(8,128)(2,1)S(1)} %pad_maximum_fusion.6), channel_id=1, source_target_pairs={{0,4},{2,6},{4,0},{6,2},{8,12},{10,14},{12,8},{14,10},{16,20},{18,... | collective-permute-start | bytes 393224 | tf_op jit(solution)/shard_map/ppermute | solution.py:105
  39.3 0.0 collective-permute-done.1
  39.3 0.3 collective-permute-start.12
  39.6 0.0 collective-permute-done.2
  39.6 0.0 collective-permute-done.3
  39.6 0.8 fusion.8
  40.4 0.9 fusion.10
  41.3 0.4 collective-permute-start.5
  41.7 1.7 %collective-permute-start.6 = (bf16[4,1,64,256]{3,2,1,0:T(8,128)(2,1)S(1)}, bf16[4,1,64,256]{3,2,1,0:T(8,128)(2,1)S(1)}, u32[]{:S(2)}, u32[]{:S(2)}) collective-permute-start(bf16[4,1,64,256]{3,2,1,0:T(8,128)(2,1)S(1)} %pad_maximum_fusion.2), channel_id=1, source_target_pairs={{0,4},{2,6},{4,0},{6,2},{8,12},{10,14},{12,8},{14,10},{16,20},{18,... | collective-permute-start | bytes 393224 | tf_op jit(solution)/shard_map/ppermute | solution.py:105
  43.4 0.0 collective-permute-done.10.refs_5_
  43.4 0.1 collective-permute-start.7
  43.6 7.1 %collective-permute-done.11.refs_6_ = bf16[4,1,64,256]{3,2,1,0:T(8,128)(2,1)S(1)} collective-permute-done((bf16[4,1,64,256]{3,2,1,0:T(8,128)(2,1)S(1)}, bf16[4,1,64,256]{3,2,1,0:T(8,128)(2,1)S(1)}, u32[]{:S(2)}, u32[]{:S(2)}) %collective-permute-start.11) | collective-permute-done | bytes 131104 | tf_op jit(solution)/shard_map/ppermute | solution.py:105
  50.7 2.0 %collective-permute-done.12.refs_7_ = bf16[4,1,64,256]{3,2,1,0:T(8,128)(2,1)S(1)} collective-permute-done((bf16[4,1,64,256]{3,2,1,0:T(8,128)(2,1)S(1)}, bf16[4,1,64,256]{3,2,1,0:T(8,128)(2,1)S(1)}, u32[]{:S(2)}, u32[]{:S(2)}) %collective-permute-start.12) | collective-permute-done | bytes 131104 | tf_op jit(solution)/shard_map/ppermute | solution.py:105
  52.7 0.0 collective-permute-done.5.refs_1_
  52.7 4.2 %collective-permute-done.6.refs_2_ = bf16[4,1,64,256]{3,2,1,0:T(8,128)(2,1)S(1)} collective-permute-done((bf16[4,1,64,256]{3,2,1,0:T(8,128)(2,1)S(1)}, bf16[4,1,64,256]{3,2,1,0:T(8,128)(2,1)S(1)}, u32[]{:S(2)}, u32[]{:S(2)}) %collective-permute-start.6) | collective-permute-done | bytes 131104 | tf_op jit(solution)/shard_map/ppermute | solution.py:105
  57.0 4.2 %collective-permute-done.7.refs_3_ = bf16[4,1,64,256]{3,2,1,0:T(8,128)(2,1)S(1)} collective-permute-done((bf16[4,1,64,256]{3,2,1,0:T(8,128)(2,1)S(1)}, bf16[4,1,64,256]{3,2,1,0:T(8,128)(2,1)S(1)}, u32[]{:S(2)}, u32[]{:S(2)}) %collective-permute-start.7) | collective-permute-done | bytes 131104 | tf_op jit(solution)/shard_map/ppermute | solution.py:105
  61.2 0.1 broadcast_in_dim.9.skip_ref
  61.2 10.3 %long_conv.2 = (bf16[4,64,256]{2,1,0:T(8,128)(2,1)S(1)}, bf16[4,64,256]{2,1,0:T(8,128)(2,1)S(1)}, bf16[4,64,256]{2,1,0:T(8,128)(2,1)S(1)}, bf16[4,64,256]{2,1,0:T(8,128)(2,1)S(1)}) custom-call(s32[1]{0:T(128)} %bitcast.at_ref, f32[64,128]{1,0:T(8,128)S(1)} %broadcast_in_dim.9.skip_ref, bf16[4,1,64,256]{3,2,1,0:T(8,128)(2,1)S(1)} %pad_maximum_fusion.refs_0_, ...), custom_call_target="tpu_custom_call" | custom-call | flops 1000 | bytes 1000 | tf_op jit(solution)/shard_map/long_conv/pallas_call | solution.py:275
  71.6 0.5 collective-permute-start.13
  72.1 3.3 %collective-permute-start.14 = (bf16[4,64,256]{2,1,0:T(8,128)(2,1)S(1)}, bf16[4,64,256]{2,1,0:T(8,128)(2,1)S(1)}, u32[]{:S(2)}, u32[]{:S(2)}) collective-permute-start(bf16[4,64,256]{2,1,0:T(8,128)(2,1)S(1)} %get-tuple-element.45), channel_id=1, source_target_pairs={{0,16},{2,18},{4,20},{6,22},{8,24},{10,26},{12,28},{14,30},{16,0},... | collective-permute-start | bytes 393224 | tf_op jit(solution)/shard_map/ppermute | solution.py:105
  75.5 0.6 collective-permute-start.15
  76.0 0.0 all-to-all-done.refs_0_
  76.0 0.1 broadcast_in_dim.20.skip_ref
  76.1 11.1 %long_conv.3 = bf16[16,64,256]{2,1,0:T(8,128)(2,1)} custom-call(s32[1]{0:T(128)} %constant.3.clone.1.at_ref, f32[64,128]{1,0:T(8,128)S(1)} %broadcast_in_dim.20.skip_ref, bf16[16,2,64,256]{3,2,1,0:T(8,128)(2,1)S(1)} %all-to-all-done.refs_0_), custom_call_target="tpu_custom_call" | custom-call | flops 4294967296 | bytes 3145728 | tf_op jit(solution)/shard_map/long_conv/pallas_call | solution.py:275
  87.2 0.0 collective-permute-done.13
  87.2 0.0 collective-permute-done.14
  87.2 0.0 collective-permute-done.15
  87.2 4.8 %all-to-all-start.1 = ((bf16[16,64,256]{2,1,0:T(8,128)(2,1)}), bf16[16,64,256]{2,1,0:T(8,128)(2,1)}, u32[]{:S(2)}, u32[]{:S(2)}) async-start(bf16[16,64,256]{2,1,0:T(8,128)(2,1)} %long_conv.3), calls=%async_computation.1 | async-start | bytes 1048576 | tf_op jit(solution)/shard_map/all_to_all | solution.py:409
  92.2 0.4 collective-permute-start.16
  92.6 1.7 %collective-permute-start.17 = (bf16[4,64,256]{2,1,0:T(8,128)(2,1)S(1)}, bf16[4,64,256]{2,1,0:T(8,128)(2,1)S(1)}, u32[]{:S(2)}, u32[]{:S(2)}) collective-permute-start(bf16[4,64,256]{2,1,0:T(8,128)(2,1)S(1)} %pad_maximum_fusion.10), channel_id=1, source_target_pairs={{0,4},{2,6},{4,0},{6,2},{8,12},{10,14},{12,8},{14,10},{16,20},{18,... | collective-permute-start | bytes 393224 | tf_op jit(solution)/shard_map/ppermute | solution.py:105
  94.4 0.1 collective-permute-start.18
  94.5 0.0 collective-permute-done.16.refs_1_
  94.5 8.2 %collective-permute-done.17.refs_2_ = bf16[4,64,256]{2,1,0:T(8,128)(2,1)S(1)} collective-permute-done((bf16[4,64,256]{2,1,0:T(8,128)(2,1)S(1)}, bf16[4,64,256]{2,1,0:T(8,128)(2,1)S(1)}, u32[]{:S(2)}, u32[]{:S(2)}) %collective-permute-start.17) | collective-permute-done | bytes 131104 | tf_op jit(solution)/shard_map/ppermute | solution.py:105
  102.7 2.1 %collective-permute-done.18.refs_3_ = bf16[4,64,256]{2,1,0:T(8,128)(2,1)S(1)} collective-permute-done((bf16[4,64,256]{2,1,0:T(8,128)(2,1)S(1)}, bf16[4,64,256]{2,1,0:T(8,128)(2,1)S(1)}, u32[]{:S(2)}, u32[]{:S(2)}) %collective-permute-start.18) | collective-permute-done | bytes 131104 | tf_op jit(solution)/shard_map/ppermute | solution.py:105
  104.8 0.0 copy-done.2
  104.8 0.9 gated_squares.2
  105.8 0.0 copy-start.8
  105.8 0.8 all-to-all-done.1.refs_0_
  106.6 1.9 %gated_squares.3 = (f32[256,2048]{1,0:T(8,128)S(1)}, f32[8,256]{1,0:T(8,128)S(1)}) custom-call(s32[1]{0:T(128)} %constant.3.clone.1.at_ref, bf16[256,2048]{1,0:T(8,128)(2,1)S(1)} %copy-done.2, bf16[48,2048]{1,0:T(8,128)(2,1)S(1)} %collective-permute-done.refs_2_.refs_3_.halo_ref, f32[3,2048]{1,0:T(4,128)S(1)} %copy-done.7, ...), custom_call_target="tpu_custom_call", output_to_operand_aliasing={{0}: (6, {})} | custom-call | flops 1000 | bytes 1000 | tf_op jit(solution)/shard_map/gated_squares/pallas_call | solution.py:342
  108.6 1.5 %collective-permute-start.19 = (f32[8,256]{1,0:T(8,128)S(1)}, f32[8,256]{1,0:T(8,128)S(1)}, u32[]{:S(2)}, u32[]{:S(2)}) collective-permute-start(f32[8,256]{1,0:T(8,128)S(1)} %get-tuple-element.56.refs_0_), channel_id=1, source_target_pairs={{0,1},{1,0},{2,3},{3,2},{4,5},{5,4},{6,7},{7,6},{8,9},{9,8},{10,11... | collective-permute-start | bytes 24584 | tf_op jit(solution)/shard_map/ppermute | solution.py:444
  110.1 2.2 %collective-permute-done.19.refs_1_ = f32[8,256]{1,0:T(8,128)S(1)} collective-permute-done((f32[8,256]{1,0:T(8,128)S(1)}, f32[8,256]{1,0:T(8,128)S(1)}, u32[]{:S(2)}, u32[]{:S(2)}) %collective-permute-start.19) | collective-permute-done | bytes 8224 | tf_op jit(solution)/shard_map/ppermute | solution.py:444
  112.3 1.9 %normed.1 = bf16[256,2048]{1,0:T(8,128)(2,1)} custom-call(f32[256,2048]{1,0:T(8,128)S(1)} %get-tuple-element.55.gated_ref, f32[1,2048]{1,0:T(1,128)S(1)} %bitcast.2, f32[8,256]{1,0:T(8,128)S(1)} %get-tuple-element.56.refs_0_, f32[8,256]{1,0:T(8,128)S(1)} %collective-permute-done.19.refs_1_), custom_call_target="tpu_custom_call" | custom-call | flops 1000 | bytes 1000 | tf_op jit(solution)/shard_map/normed/pallas_call | solution.py:386
  (36 shorter events, 0.3 us)
Async XLA Ops:
  0.0 11.3 %copy-start.1 = (bf16[256,2048]{1,0:T(8,128)(2,1)S(1)}, bf16[256,2048]{1,0:T(8,128)(2,1)}, u32[]{:S(2)}) copy-start(bf16[256,2048]{1,0:T(8,128)(2,1)} %refs_2_.3) | copy-start | bytes 3145732
  0.0 11.3 %copy-start = (bf16[256,2048]{1,0:T(8,128)(2,1)S(1)}, bf16[256,2048]{1,0:T(8,128)(2,1)}, u32[]{:S(2)}) copy-start(bf16[256,2048]{1,0:T(8,128)(2,1)} %refs_1_.5) | copy-start | bytes 3145732
  0.0 4.2 %copy-start.3 = (bf16[256,2048]{1,0:T(8,128)(2,1)S(1)}, bf16[256,2048]{1,0:T(8,128)(2,1)}, u32[]{:S(2)}) copy-start(bf16[256,2048]{1,0:T(8,128)(2,1)} %refs_0_.7) | copy-start | bytes 3145732
  0.0 11.3 %copy-start.6 = (f32[3,2048]{1,0:T(4,128)S(1)}, f32[3,2048]{1,0:T(4,128)}, u32[]{:S(2)}) copy-start(f32[3,2048]{1,0:T(4,128)} %refs_5_.1) | copy-start | bytes 73732
  0.0 11.3 %copy-start.5 = (f32[3,2048]{1,0:T(4,128)S(1)}, f32[3,2048]{1,0:T(4,128)}, u32[]{:S(2)}) copy-start(f32[3,2048]{1,0:T(4,128)} %refs_4_.3) | copy-start | bytes 73732
  1.8 9.5 %collective-permute-start = (bf16[48,2048]{1,0:T(8,128)(2,1)}, bf16[48,2048]{1,0:T(8,128)(2,1)S(1)}, u32[]{:S(2)}, u32[]{:S(2)}) collective-permute-start(bf16[48,2048]{1,0:T(8,128)(2,1)} %tails.1), channel_id=1, source_target_pairs={{0,2},{2,4},{4,6},{6,8},{8,10},{10,12},{12,14},{14,16},{16,18},{18... | collective-permute-start | bytes 589832 | tf_op jit(solution)/shard_map/ppermute | solution.py:26
  5.3 33.9 %collective-permute-start.1 = (bf16[4,1,64,256]{3,2,1,0:T(8,128)(2,1)}, bf16[4,1,64,256]{3,2,1,0:T(8,128)(2,1)}, u32[]{:S(2)}, u32[]{:S(2)}) collective-permute-start(bf16[4,1,64,256]{3,2,1,0:T(8,128)(2,1)} %get-tuple-element.32), channel_id=1, source_target_pairs={{0,8},{2,10},{4,12},{6,14},{8,0},{10,2},{12,4},{14,6},{16,24},{18,... | collective-permute-start | bytes 393224 | tf_op jit(solution)/shard_map/ppermute | solution.py:105
  7.9 31.7 %collective-permute-start.2 = (bf16[4,1,64,256]{3,2,1,0:T(8,128)(2,1)}, bf16[4,1,64,256]{3,2,1,0:T(8,128)(2,1)}, u32[]{:S(2)}, u32[]{:S(2)}) collective-permute-start(bf16[4,1,64,256]{3,2,1,0:T(8,128)(2,1)} %get-tuple-element.33), channel_id=1, source_target_pairs={{0,16},{2,18},{4,20},{6,22},{8,24},{10,26},{12,28},{14,30},{16,0},... | collective-permute-start | bytes 393224 | tf_op jit(solution)/shard_map/ppermute | solution.py:105
  10.5 29.1 %collective-permute-start.3 = (bf16[4,1,64,256]{3,2,1,0:T(8,128)(2,1)}, bf16[4,1,64,256]{3,2,1,0:T(8,128)(2,1)}, u32[]{:S(2)}, u32[]{:S(2)}) collective-permute-start(bf16[4,1,64,256]{3,2,1,0:T(8,128)(2,1)} %get-tuple-element.34), channel_id=1, source_target_pairs={{0,24},{2,26},{4,28},{6,30},{8,16},{10,18},{12,20},{14,22},{16,8},... | collective-permute-start | bytes 393224 | tf_op jit(solution)/shard_map/ppermute | solution.py:105
  13.1 16.0 %collective-permute-start.4 = (bf16[4,1,64,256]{3,2,1,0:T(8,128)(2,1)S(1)}, bf16[4,1,64,256]{3,2,1,0:T(8,128)(2,1)S(1)}, u32[]{:S(2)}, u32[]{:S(2)}) collective-permute-start(bf16[4,1,64,256]{3,2,1,0:T(8,128)(2,1)S(1)} %get-tuple-element.35), channel_id=1, source_target_pairs={{0,16},{2,18},{4,20},{6,22},{8,24},{10,26},{12,28},{14,30},{16,0},... | collective-permute-start | bytes 393224 | tf_op jit(solution)/shard_map/ppermute | solution.py:105
  15.8 20.3 %collective-permute-start.8 = (bf16[4,1,64,256]{3,2,1,0:T(8,128)(2,1)}, bf16[4,1,64,256]{3,2,1,0:T(8,128)(2,1)}, u32[]{:S(2)}, u32[]{:S(2)}) collective-permute-start(bf16[4,1,64,256]{3,2,1,0:T(8,128)(2,1)} %get-tuple-element.41), channel_id=1, source_target_pairs={{0,8},{2,10},{4,12},{6,14},{8,0},{10,2},{12,4},{14,6},{16,24},{18,... | collective-permute-start | bytes 393224 | tf_op jit(solution)/shard_map/ppermute | solution.py:105
  18.9 1.0 copy-start.4
  29.1 0.6 copy-start.9
  29.8 6.3 %copy-start.10 = (bf16[4,1,64,256]{3,2,1,0:T(8,128)(2,1)S(1)}, bf16[4,1,64,256]{3,2,1,0:T(8,128)(2,1)}, u32[]{:S(2)}) copy-start(bf16[4,1,64,256]{3,2,1,0:T(8,128)(2,1)} %copy-done.9) | copy-start | bytes 393220
  29.8 7.6 %collective-permute-start.9 = (bf16[4,1,64,256]{3,2,1,0:T(8,128)(2,1)}, bf16[4,1,64,256]{3,2,1,0:T(8,128)(2,1)S(1)}, u32[]{:S(2)}, u32[]{:S(2)}) collective-permute-start(bf16[4,1,64,256]{3,2,1,0:T(8,128)(2,1)} %get-tuple-element.42), channel_id=1, source_target_pairs={{0,24},{2,26},{4,28},{6,30},{8,16},{10,18},{12,20},{14,22},{16,8},... | collective-permute-start | bytes 393224 | tf_op jit(solution)/shard_map/ppermute | solution.py:105
  32.3 43.7 %all-to-all-start = ((bf16[16,2,64,256]{3,2,1,0:T(8,128)(2,1)}), bf16[16,2,64,256]{3,2,1,0:T(8,128)(2,1)S(1)}, u32[]{:S(2)}, u32[]{:S(2)}) async-start(bf16[16,2,64,256]{3,2,1,0:T(8,128)(2,1)} %copy-done.4), calls=%async_computation | async-start | bytes 2097152 | tf_op jit(solution)/shard_map/all_to_all | solution.py:409
  37.4 6.0 %collective-permute-start.10 = (bf16[4,1,64,256]{3,2,1,0:T(8,128)(2,1)S(1)}, bf16[4,1,64,256]{3,2,1,0:T(8,128)(2,1)S(1)}, u32[]{:S(2)}, u32[]{:S(2)}) collective-permute-start(bf16[4,1,64,256]{3,2,1,0:T(8,128)(2,1)S(1)} %pad_maximum_fusion.5), channel_id=1, source_target_pairs={{0,2},{2,0},{4,6},{6,4},{8,10},{10,8},{12,14},{14,12},{16,18},{18,... | collective-permute-start | bytes 393224 | tf_op jit(solution)/shard_map/ppermute | solution.py:105
  37.6 13.2 %collective-permute-start.11 = (bf16[4,1,64,256]{3,2,1,0:T(8,128)(2,1)S(1)}, bf16[4,1,64,256]{3,2,1,0:T(8,128)(2,1)S(1)}, u32[]{:S(2)}, u32[]{:S(2)}) collective-permute-start(bf16[4,1,64,256]{3,2,1,0:T(8,128)(2,1)S(1)} %pad_maximum_fusion.6), channel_id=1, source_target_pairs={{0,4},{2,6},{4,0},{6,2},{8,12},{10,14},{12,8},{14,10},{16,20},{18,... | collective-permute-start | bytes 393224 | tf_op jit(solution)/shard_map/ppermute | solution.py:105
  39.3 13.5 %collective-permute-start.12 = (bf16[4,1,64,256]{3,2,1,0:T(8,128)(2,1)S(1)}, bf16[4,1,64,256]{3,2,1,0:T(8,128)(2,1)S(1)}, u32[]{:S(2)}, u32[]{:S(2)}) collective-permute-start(bf16[4,1,64,256]{3,2,1,0:T(8,128)(2,1)S(1)} %pad_maximum_fusion.7), channel_id=1, source_target_pairs={{0,6},{2,4},{4,2},{6,0},{8,14},{10,12},{12,10},{14,8},{16,22},{18,... | collective-permute-start | bytes 393224 | tf_op jit(solution)/shard_map/ppermute | solution.py:105
  41.3 11.4 %collective-permute-start.5 = (bf16[4,1,64,256]{3,2,1,0:T(8,128)(2,1)S(1)}, bf16[4,1,64,256]{3,2,1,0:T(8,128)(2,1)S(1)}, u32[]{:S(2)}, u32[]{:S(2)}) collective-permute-start(bf16[4,1,64,256]{3,2,1,0:T(8,128)(2,1)S(1)} %pad_maximum_fusion.1), channel_id=1, source_target_pairs={{0,2},{2,0},{4,6},{6,4},{8,10},{10,8},{12,14},{14,12},{16,18},{18,... | collective-permute-start | bytes 393224 | tf_op jit(solution)/shard_map/ppermute | solution.py:105
  41.7 15.3 %collective-permute-start.6 = (bf16[4,1,64,256]{3,2,1,0:T(8,128)(2,1)S(1)}, bf16[4,1,64,256]{3,2,1,0:T(8,128)(2,1)S(1)}, u32[]{:S(2)}, u32[]{:S(2)}) collective-permute-start(bf16[4,1,64,256]{3,2,1,0:T(8,128)(2,1)S(1)} %pad_maximum_fusion.2), channel_id=1, source_target_pairs={{0,4},{2,6},{4,0},{6,2},{8,12},{10,14},{12,8},{14,10},{16,20},{18,... | collective-permute-start | bytes 393224 | tf_op jit(solution)/shard_map/ppermute | solution.py:105
  43.4 17.7 %collective-permute-start.7 = (bf16[4,1,64,256]{3,2,1,0:T(8,128)(2,1)S(1)}, bf16[4,1,64,256]{3,2,1,0:T(8,128)(2,1)S(1)}, u32[]{:S(2)}, u32[]{:S(2)}) collective-permute-start(bf16[4,1,64,256]{3,2,1,0:T(8,128)(2,1)S(1)} %pad_maximum_fusion.3), channel_id=1, source_target_pairs={{0,6},{2,4},{4,2},{6,0},{8,14},{10,12},{12,10},{14,8},{16,22},{18,... | collective-permute-start | bytes 393224 | tf_op jit(solution)/shard_map/ppermute | solution.py:105
  71.6 15.7 %collective-permute-start.13 = (bf16[4,64,256]{2,1,0:T(8,128)(2,1)S(1)}, bf16[4,64,256]{2,1,0:T(8,128)(2,1)S(1)}, u32[]{:S(2)}, u32[]{:S(2)}) collective-permute-start(bf16[4,64,256]{2,1,0:T(8,128)(2,1)S(1)} %get-tuple-element.44), channel_id=1, source_target_pairs={{0,8},{2,10},{4,12},{6,14},{8,0},{10,2},{12,4},{14,6},{16,24},{18,... | collective-permute-start | bytes 393224 | tf_op jit(solution)/shard_map/ppermute | solution.py:105
  72.1 15.1 %collective-permute-start.14 = (bf16[4,64,256]{2,1,0:T(8,128)(2,1)S(1)}, bf16[4,64,256]{2,1,0:T(8,128)(2,1)S(1)}, u32[]{:S(2)}, u32[]{:S(2)}) collective-permute-start(bf16[4,64,256]{2,1,0:T(8,128)(2,1)S(1)} %get-tuple-element.45), channel_id=1, source_target_pairs={{0,16},{2,18},{4,20},{6,22},{8,24},{10,26},{12,28},{14,30},{16,0},... | collective-permute-start | bytes 393224 | tf_op jit(solution)/shard_map/ppermute | solution.py:105
  75.5 11.8 %collective-permute-start.15 = (bf16[4,64,256]{2,1,0:T(8,128)(2,1)S(1)}, bf16[4,64,256]{2,1,0:T(8,128)(2,1)S(1)}, u32[]{:S(2)}, u32[]{:S(2)}) collective-permute-start(bf16[4,64,256]{2,1,0:T(8,128)(2,1)S(1)} %get-tuple-element.46), channel_id=1, source_target_pairs={{0,24},{2,26},{4,28},{6,30},{8,16},{10,18},{12,20},{14,22},{16,8},... | collective-permute-start | bytes 393224 | tf_op jit(solution)/shard_map/ppermute | solution.py:105
  87.2 17.6 %copy-start.2 = (bf16[256,2048]{1,0:T(8,128)(2,1)S(1)}, bf16[256,2048]{1,0:T(8,128)(2,1)}, u32[]{:S(2)}) copy-start(bf16[256,2048]{1,0:T(8,128)(2,1)} %gate_ref.3) | copy-start | bytes 3145732
  87.2 17.6 %copy-start.7 = (f32[3,2048]{1,0:T(4,128)S(1)}, f32[3,2048]{1,0:T(4,128)}, u32[]{:S(2)}) copy-start(f32[3,2048]{1,0:T(4,128)} %taps_ref.3) | copy-start | bytes 73732
  87.2 19.4 %all-to-all-start.1 = ((bf16[16,64,256]{2,1,0:T(8,128)(2,1)}), bf16[16,64,256]{2,1,0:T(8,128)(2,1)}, u32[]{:S(2)}, u32[]{:S(2)}) async-start(bf16[16,64,256]{2,1,0:T(8,128)(2,1)} %long_conv.3), calls=%async_computation.1 | async-start | bytes 1048576 | tf_op jit(solution)/shard_map/all_to_all | solution.py:409
  92.2 2.3 %collective-permute-start.16 = (bf16[4,64,256]{2,1,0:T(8,128)(2,1)S(1)}, bf16[4,64,256]{2,1,0:T(8,128)(2,1)S(1)}, u32[]{:S(2)}, u32[]{:S(2)}) collective-permute-start(bf16[4,64,256]{2,1,0:T(8,128)(2,1)S(1)} %pad_maximum_fusion.9), channel_id=1, source_target_pairs={{0,2},{2,0},{4,6},{6,4},{8,10},{10,8},{12,14},{14,12},{16,18},{18,... | collective-permute-start | bytes 393224 | tf_op jit(solution)/shard_map/ppermute | solution.py:105
  92.6 10.1 %collective-permute-start.17 = (bf16[4,64,256]{2,1,0:T(8,128)(2,1)S(1)}, bf16[4,64,256]{2,1,0:T(8,128)(2,1)S(1)}, u32[]{:S(2)}, u32[]{:S(2)}) collective-permute-start(bf16[4,64,256]{2,1,0:T(8,128)(2,1)S(1)} %pad_maximum_fusion.10), channel_id=1, source_target_pairs={{0,4},{2,6},{4,0},{6,2},{8,12},{10,14},{12,8},{14,10},{16,20},{18,... | collective-permute-start | bytes 393224 | tf_op jit(solution)/shard_map/ppermute | solution.py:105
  94.4 10.4 %collective-permute-start.18 = (bf16[4,64,256]{2,1,0:T(8,128)(2,1)S(1)}, bf16[4,64,256]{2,1,0:T(8,128)(2,1)S(1)}, u32[]{:S(2)}, u32[]{:S(2)}) collective-permute-start(bf16[4,64,256]{2,1,0:T(8,128)(2,1)S(1)} %pad_maximum_fusion.11), channel_id=1, source_target_pairs={{0,6},{2,4},{4,2},{6,0},{8,14},{10,12},{12,10},{14,8},{16,22},{18,... | collective-permute-start | bytes 393224 | tf_op jit(solution)/shard_map/ppermute | solution.py:105
  105.8 6.5 %copy-start.8 = (f32[2048]{0:T(1024)S(1)}, f32[2048]{0:T(1024)}, u32[]{:S(2)}) copy-start(f32[2048]{0:T(1024)} %param.17) | copy-start | bytes 24580
  108.6 3.7 %collective-permute-start.19 = (f32[8,256]{1,0:T(8,128)S(1)}, f32[8,256]{1,0:T(8,128)S(1)}, u32[]{:S(2)}, u32[]{:S(2)}) collective-permute-start(f32[8,256]{1,0:T(8,128)S(1)} %get-tuple-element.56.refs_0_), channel_id=1, source_target_pairs={{0,1},{1,0},{2,3},{3,2},{4,5},{5,4},{6,7},{7,6},{8,9},{9,8},{10,11... | collective-permute-start | bytes 24584 | tf_op jit(solution)/shard_map/ppermute | solution.py:444

commit v2 on v1

--- a/solution.py
+++ b/solution.py
@@ -16,8 +16,14 @@
 NEAR = 4
 VMEM_BYTES = 20 * 1024 * 1024
 BRIEF = pl.CostEstimate(flops=1000, bytes_accessed=1000, transcendentals=0)
+DONE = jax.ShapeDtypeStruct((8, 128), jnp.float32)
 F32 = jnp.float32
 BF16 = jnp.bfloat16
+
+
+def corner(array):
+    block = (1,) * (len(array.shape) - 2) + (8 if array.dtype == F32 else 16, LANES)
+    return pl.BlockSpec(block, lambda *at: (0,) * len(block))
 
 
 def passed_along(array, axis, by):
@@ -35,11 +41,11 @@
     return taps[0:1] * rows + taps[1:2] * one + taps[2:3] * two
 
 
-def pack_kernel(wants, at_ref, *refs):
+def pack_kernel(wants, waits, at_ref, *refs):
     arrays = len(wants) + 4 * ("product" in wants)
-    refs, outs, held = list(refs[:arrays]), refs[arrays:-1], refs[-1]
+    refs, outs, done_ref, held = list(refs[:arrays]), refs[arrays + waits : -2], refs[-2], refs[-1]
+    done_ref[...] = jnp.zeros_like(done_ref)
     _, _, narrow, tok = held.shape
-    near = outs[0].shape[0]
     count = WIDE // narrow
     step = pl.program_id(0)
     for at, want in enumerate(wants):
@@ -54,33 +60,35 @@
 
     @pl.when(step == pl.num_programs(0) - 1)
     def _():
-        for j, out_ref in enumerate(outs):
-            for i in range(near):
-                out_ref[i] = held[at_ref[0] ^ (near * j + i)]
-
-
-def packed(wants, arrays, part, near, position):
+        for i, out_ref in enumerate(outs):
+            for j in range(out_ref.shape[0]):
+                out_ref[j] = held[at_ref[0] ^ (len(outs) * j + i)]
+
+
+def packed(wants, arrays, later, part, near, position):
     start, narrow, blocks = part
     tok = arrays[0].shape[0]
     first = start // WIDE
-    shape = (near, len(wants), narrow, tok)
-    return pl.pallas_call(
-        functools.partial(pack_kernel, wants),
+    shape = (blocks // near, len(wants), narrow, tok)
+    return pl.pallas_call(
+        functools.partial(pack_kernel, wants, len(later)),
         grid_spec=pltpu.PrefetchScalarGridSpec(
             num_scalar_prefetch=1,
             grid=(blocks * narrow // WIDE,),
             in_specs=[
                 pl.BlockSpec((array.shape[0], WIDE), lambda i, at: (0, first + i))
                 for array in arrays
-            ],
-            out_specs=[pl.BlockSpec(shape, lambda i, at: (0, 0, 0, 0))] * (blocks // near),
+            ]
+            + [corner(array) for array in later],
+            out_specs=[pl.BlockSpec(shape, lambda i, at: (0, 0, 0, 0))] * near
+            + [pl.BlockSpec(DONE.shape, lambda i, at: (0, 0))],
             scratch_shapes=[pltpu.VMEM((blocks,) + shape[1:], BF16)],
         ),
-        out_shape=[jax.ShapeDtypeStruct(shape, BF16)] * (blocks // near),
+        out_shape=[jax.ShapeDtypeStruct(shape, BF16)] * near + [DONE],
         compiler_params=pltpu.CompilerParams(vmem_limit_bytes=VMEM_BYTES),
         cost_estimate=BRIEF,
         name="pack_" + "_".join(wants),
-    )(position, *arrays)
+    )(position, *arrays, *later)
 
 
 def tails_kernel(*refs):
@@ -111,14 +119,34 @@
     return [lines[0]] + [came[j] for j in range(1, len(lines))]
 
 
-def swap_near(lines):
-    parts = [jnp.stack([line[i] for line in lines]) for i in range(NEAR)]
+def plane_first(parts):
     return [parts[0]] + [swapped(parts[i], i) for i in range(1, NEAR)]
 
 
-def after(arrays, *others):
-    tokens = [other[(slice(0, 1),) * other.ndim] for other in others]
-    return lax.optimization_barrier((arrays, tokens))[0]
+def regroup_kernel(count, *refs):
+    for i, out_ref in enumerate(refs[-count:]):
+        for j in range(out_ref.shape[0]):
+            out_ref[j] = refs[j][i]
+
+
+def regroup(lines, later):
+    whole = lambda array: pl.BlockSpec(array.shape, lambda i: (0,) * len(array.shape))
+    count = lines[0].shape[0]
+    out_shape = [jax.ShapeDtypeStruct((len(lines),) + lines[0].shape[1:], BF16)] * count
+    return pl.pallas_call(
+        functools.partial(regroup_kernel, count),
+        grid=(1,),
+        in_specs=[whole(line) for line in lines] + [corner(array) for array in later],
+        out_specs=[whole(array) for array in out_shape],
+        out_shape=out_shape,
+        compiler_params=pltpu.CompilerParams(vmem_limit_bytes=VMEM_BYTES),
+        cost_estimate=BRIEF,
+        name="regroup",
+    )(*lines, *later)
+
+
+def swap_near(lines, later):
+    return plane_first(regroup(lines, later))
 
 
 def delayed(rows, by):
@@ -151,8 +179,9 @@
     return jnp.concatenate(columns, axis=1)
 
 
-def conv_kernel(at_ref, skip_ref, *refs):
-    refs, (filt, prod, base, left, total, held) = refs[:-6], refs[-6:]
+def conv_kernel(at_ref, skip_ref, later_ref, *refs):
+    refs, (done_ref, filt, prod, base, left, total, held) = refs[:-7], refs[-7:]
+    done_ref[...] = jnp.zeros_like(done_ref)
     blocks, lanes, tok = prod.shape
     near = next(at for at, ref in enumerate(refs) if len(ref.shape) == 3)
     in_refs, out_refs = refs[:near], refs[near:]
@@ -163,12 +192,12 @@
     turns = blocks // 2
     units = lanes // 16
 
-    for i, (filt_ref, prod_ref) in enumerate(zip(filt_refs, prod_refs)):
-        for j in range(filt_ref.shape[0]):
-            block = at_ref[0] ^ (len(filt_refs) * j + i)
+    for j, (filt_ref, prod_ref) in enumerate(zip(filt_refs, prod_refs)):
+        for i in range(filt_ref.shape[0]):
+            block = at_ref[0] ^ (filt_ref.shape[0] * j + i)
             lags = pl.ds(pl.multiple_of(block * tok, tok), tok)
-            filt[:, lags] = filt_ref[j, 0].astype(F32)
-            prod[block] = prod_ref[j, int(merged)].astype(F32)
+            filt[:, lags] = filt_ref[i, 0].astype(F32)
+            prod[block] = prod_ref[i, int(merged)].astype(F32)
     base[:, :, :LANES] = jnp.zeros((2, GROUP * FINE, LANES), BF16)
 
     def pairs_of(row, side):
@@ -267,17 +296,17 @@
             out_ref[i] = held[at_ref[0] ^ (out_ref.shape[0] * j + i)]
 
 
-def long_conv(arrays, skip_rows, blocks, near, position, cost=BRIEF):
+def long_conv(arrays, skip_rows, later, blocks, near, position, cost=BRIEF):
     _, _, lanes, tok = arrays[0].shape
     length = blocks * tok
     whole = lambda array: pl.BlockSpec(array.shape, lambda i, at: (0,) * len(array.shape))
-    out_shape = [jax.ShapeDtypeStruct((near, lanes, tok), BF16)] * (blocks // near)
+    out_shape = [jax.ShapeDtypeStruct((near, lanes, tok), BF16)] * (blocks // near) + [DONE]
     return pl.pallas_call(
         conv_kernel,
         grid_spec=pltpu.PrefetchScalarGridSpec(
             num_scalar_prefetch=1,
             grid=(1,),
-            in_specs=[whole(array) for array in (skip_rows, *arrays)],
+            in_specs=[whole(skip_rows), corner(later)] + [whole(array) for array in arrays],
             out_specs=[whole(array) for array in out_shape],
             scratch_shapes=[
                 pltpu.VMEM((lanes, length), F32),
@@ -292,7 +321,7 @@
         compiler_params=pltpu.CompilerParams(vmem_limit_bytes=VMEM_BYTES),
         cost_estimate=cost,
         name="long_conv",
-    )(position, skip_rows, *arrays)
+    )(position, skip_rows, later, *arrays)
 
 
 def gated_kernel(at_ref, gate_ref, halo_ref, taps_ref, *refs):
@@ -408,10 +437,11 @@
     starts = [at * narrow * blocks for at in range(PARTS)]
     exchange = lambda rows: lax.all_to_all(rows, "seq", split_axis=0, concat_axis=0, tiled=True)
     natural = jnp.zeros((1,), jnp.int32)
-    pack = lambda wants, start, near, origin: packed(
+    pack = lambda wants, start, near, origin, later: packed(
         wants,
         ([long_filter] if "filter" in wants else [])
         + ([key_in, value_in, halo, key_short, value_short] if "product" in wants else []),
+        later,
         (start, narrow, blocks),
         near,
         origin,
@@ -421,22 +451,25 @@
         skip = lax.dynamic_slice_in_dim(skip_gain, start + place * narrow, narrow, 0)
         return jnp.broadcast_to(skip[:, None], (narrow, LANES))
 
-    lines = pack(("filter",), starts[0], NEAR, position)
     halo = passed_along(tails((key_in, value_in, gate_in)), "seq", 1)
-    came = swap_far(pack(("product",), starts[0], NEAR, position))
-    filters = swap_near(after(swap_far(lines), came[2]))
-    products = swap_near(came)
-    second = pack(("filter", "product"), starts[1], blocks, natural)[0]
-    second = exchange(after(second, came[2]))
-    lines = long_conv(filters + products, skip_of(starts[0]), blocks, NEAR, position)
-    lines = swap_far(after(lines, second))
+    *lines, _ = pack(("filter",), starts[0], NEAR, position, [])
+    filters = swap_far(regroup(plane_first(lines), []))
+    *product, _ = pack(("product",), starts[0], NEAR, position, [])
+    product = plane_first(product)
+    products = swap_far(regroup(product, filters[1:]))
+    second, done = pack(("filter", "product"), starts[1], 1, natural, filters[1:2] + products[1:])
+    second = exchange(second)
+    *lines, ended = long_conv(filters + products, skip_of(starts[0]), done, blocks, NEAR, position)
+    lines, second = lax.optimization_barrier((lines, second))
+    lines = swap_far(lines)
     cost = pl.CostEstimate(
         flops=2 * width * tok * tok * blocks, bytes_accessed=6 * tok * width, transcendentals=0
     )
-    last = long_conv([second], skip_of(starts[1]), blocks, blocks, natural, cost)[0]
-    lines, last = lax.optimization_barrier((lines, last))
+    last, done = long_conv([second], skip_of(starts[1]), ended, blocks, blocks, natural, cost)
+    lines, last, done = lax.optimization_barrier((lines, last, done))
+    first = swap_near(lines, [done])
     last = exchange(last)
-    gated = gated_of(gate_in, halo, gate_short, swap_near(lines), starts[0], None, position)
+    gated = gated_of(gate_in, halo, gate_short, first, starts[0], None, position)
     gated = gated_of(gate_in, halo, gate_short, [last], starts[1], gated, natural)
     gated, squares = gated
     sums = [squares]

time: 115 us -> 117 us (1.017)
  waiting for transfers between devices: 40.6 us -> 44.5 us
  local copies, waits for them, and re-layouts: 5.18 us -> 2.18 us
  starting transfers between devices: 35.5 us -> 37 us
    all_to_all x2, waiting for transfers between devices: 0.84 us -> 12.6 us  [local(): lax.all_to_all(rows, 'seq', split_axis=0, concat_axis=0, tiled=True)]
    ppermute x18, waiting for transfers between devices: 37.6 us -> 29.7 us  [swapped(): return lax.ppermute(rows, 'seq', [(i, i ^ by) for i in range(size)])]
    slice x10 -> x0, local copies, waits for them, and re-layouts: 2.62 us -> none  [swap_near(): parts = [jnp.stack([line[i] for line in lines]) for i in range(NEAR)]]
    all_to_all x2, starting transfers between devices: 8.58 us -> 10.3 us  [local(): lax.all_to_all(rows, 'seq', split_axis=0, concat_axis=0, tiled=True)]
    pallas_call x3 -> x6, Pallas kernels: 4.33 us -> 5.12 us  [the longest x3 5.01 us: packed(): pl.pallas_call(functools.partial(pack_kernel, wants, len(later)), grid_sp...]
  transfers between devices with their start and end apart: 22 -> 22, of which waited for: 10 -> 10; matrix products, arithmetic and copies ran while one was open for 3% -> 1% of each run, Pallas kernels for 23% -> 22%
where the time goes in v2:
time: 117 us
  waiting for transfers between devices  44.5 us (38%)
  starting transfers between devices  37 us (32%)
  Pallas kernels  33 us (28%)
  local copies, waits for them, and re-layouts  2.18 us (2%)
    ppermute x18, waiting for transfers between devices, swapped(): return lax.ppermute(rows, 'seq', [(i, i ^ by) for i in range(size)])  29.7 us
    ppermute x18, starting transfers between devices, swapped(): return lax.ppermute(rows, 'seq', [(i, i ^ by) for i in range(size)])  23.1 us
    pallas_call x2, Pallas kernels, long_conv(): pl.pallas_call(conv_kernel, grid_spec=pltpu.PrefetchScalarGridSpec(num_sc...  21.5 us
    all_to_all x2, waiting for transfers between devices, local(): lax.all_to_all(rows, 'seq', split_axis=0, concat_axis=0, tiled=True)  12.6 us
    all_to_all x2, starting transfers between devices, local(): lax.all_to_all(rows, 'seq', split_axis=0, concat_axis=0, tiled=True)  10.3 us
    pallas_call x3, Pallas kernels, packed(): pl.pallas_call(functools.partial(pack_kernel, wants, len(later)), grid_sp...  5.01 us
    pallas_call x2, Pallas kernels, gated_of(): pl.pallas_call(gated_kernel, grid_spec=pltpu.PrefetchScalarGridSpec(num_s...  2.9 us
  transfers between devices with their start and end apart: 22, of which 10 were waited for; matrix products, arithmetic and copies ran while one was open for 1% of the time, Pallas kernels for 22%

profile of v2, /device:TPU:0, one launch (start us, length us, event | category | flops | bytes accessed | tf_op | source)
XLA Modules:
  0.0 116.8 jit_solution(11260236285943289497)
XLA Ops:
  0.0 1.2 %copy-done.3 = bf16[256,2048]{1,0:T(8,128)(2,1)S(1)} copy-done((bf16[256,2048]{1,0:T(8,128)(2,1)S(1)}, bf16[256,2048]{1,0:T(8,128)(2,1)}, u32[]{:S(2)}) %copy-start.3) | copy-done | bytes 1048600
  1.2 1.0 pack_filter.1
  2.2 0.5 collective-permute-start.1
  2.7 2.6 %collective-permute-start.2 = (bf16[4,1,64,256]{3,2,1,0:T(8,128)(2,1)S(1)}, bf16[4,1,64,256]{3,2,1,0:T(8,128)(2,1)S(1)}, u32[]{:S(2)}, u32[]{:S(2)}) collective-permute-start(bf16[4,1,64,256]{3,2,1,0:T(8,128)(2,1)S(1)} %get-tuple-element.51), channel_id=1, source_target_pairs={{0,4},{2,6},{4,0},{6,2},{8,12},{10,14},{12,8},{14,10},{16,20},{18,... | collective-permute-start | bytes 393224 | tf_op jit(solution)/shard_map/ppermute | solution.py:113
  5.3 0.1 collective-permute-start.3
  5.4 1.6 %tails.1 = bf16[48,2048]{1,0:T(8,128)(2,1)} custom-call(bf16[256,2048]{1,0:T(8,128)(2,1)} %refs_1_.5, bf16[256,2048]{1,0:T(8,128)(2,1)} %refs_2_.3, bf16[256,2048]{1,0:T(8,128)(2,1)} %gate_ref.3), custom_call_target="tpu_custom_call" | custom-call | tf_op jit(solution)/shard_map/tails/pallas_call | solution.py:101
  7.0 2.2 %collective-permute-start = (bf16[48,2048]{1,0:T(8,128)(2,1)}, bf16[48,2048]{1,0:T(8,128)(2,1)S(1)}, u32[]{:S(2)}, u32[]{:S(2)}) collective-permute-start(bf16[48,2048]{1,0:T(8,128)(2,1)} %tails.1), channel_id=1, source_target_pairs={{0,2},{2,4},{4,6},{6,8},{8,10},{10,12},{12,14},{14,16},{16,18},{18... | collective-permute-start | bytes 589832 | tf_op jit(solution)/shard_map/ppermute | solution.py:32
  9.2 0.0 collective-permute-done.1.refs_1_
  9.2 0.5 collective-permute-done.2.refs_2_
  9.7 2.3 %collective-permute-done.3.refs_3_ = bf16[4,1,64,256]{3,2,1,0:T(8,128)(2,1)S(1)} collective-permute-done((bf16[4,1,64,256]{3,2,1,0:T(8,128)(2,1)S(1)}, bf16[4,1,64,256]{3,2,1,0:T(8,128)(2,1)S(1)}, u32[]{:S(2)}, u32[]{:S(2)}) %collective-permute-start.3) | collective-permute-done | bytes 131104 | tf_op jit(solution)/shard_map/ppermute | solution.py:113
  12.0 1.7 %collective-permute-start.4 = (bf16[4,1,64,256]{3,2,1,0:T(8,128)(2,1)S(1)}, bf16[4,1,64,256]{3,2,1,0:T(8,128)(2,1)S(1)}, u32[]{:S(2)}, u32[]{:S(2)}) collective-permute-start(bf16[4,1,64,256]{3,2,1,0:T(8,128)(2,1)S(1)} %get-tuple-element.53), channel_id=1, source_target_pairs={{0,8},{2,10},{4,12},{6,14},{8,0},{10,2},{12,4},{14,6},{16,24},{18,... | collective-permute-start | bytes 393224 | tf_op jit(solution)/shard_map/ppermute | solution.py:113
  13.7 2.6 %collective-permute-start.8 = (bf16[4,1,64,256]{3,2,1,0:T(8,128)(2,1)S(1)}, bf16[4,1,64,256]{3,2,1,0:T(8,128)(2,1)S(1)}, u32[]{:S(2)}, u32[]{:S(2)}) collective-permute-start(bf16[4,1,64,256]{3,2,1,0:T(8,128)(2,1)S(1)} %get-tuple-element.58), channel_id=1, source_target_pairs={{0,16},{2,18},{4,20},{6,22},{8,24},{10,26},{12,28},{14,30},{16,0},... | collective-permute-start | bytes 393224 | tf_op jit(solution)/shard_map/ppermute | solution.py:113
  16.3 0.2 collective-permute-start.9
  16.4 0.0 collective-permute-done.refs_2_.refs_3_.halo_ref
  16.4 0.0 copy-done
  16.4 0.0 copy-done.1
  16.5 0.0 copy-done.5
  16.5 0.0 copy-done.6
  16.5 1.7 %pack_product.1 = (bf16[4,1,64,256]{3,2,1,0:T(8,128)(2,1)S(1)}, bf16[4,1,64,256]{3,2,1,0:T(8,128)(2,1)S(1)}, bf16[4,1,64,256]{3,2,1,0:T(8,128)(2,1)S(1)}, bf16[4,1,64,256]{3,2,1,0:T(8,128)(2,1)S(1)}, f32[8,128]{1,0:T(8,128)}) custom-call(s32[1]{0:T(128)} %bitcast.at_ref, bf16[256,2048]{1,0:T(8,128)(2,1)S(1)} %copy-done, bf16[256,2048]{1,0:T(8,128)(2,1)S(1)} %copy-done.1, ...), custom_call_target="tpu_custom_call" | custom-call | flops 1000 | bytes 1000 | tf_op jit(solution)/shard_map/pack_product/pallas_call | solution.py:73
  18.2 0.0 collective-permute-start.5
  18.2 1.6 %collective-permute-start.6 = (bf16[4,1,64,256]{3,2,1,0:T(8,128)(2,1)S(1)}, bf16[4,1,64,256]{3,2,1,0:T(8,128)(2,1)S(1)}, u32[]{:S(2)}, u32[]{:S(2)}) collective-permute-start(bf16[4,1,64,256]{3,2,1,0:T(8,128)(2,1)S(1)} %get-tuple-element.56), channel_id=1, source_target_pairs={{0,4},{2,6},{4,0},{6,2},{8,12},{10,14},{12,8},{14,10},{16,20},{18,... | collective-permute-start | bytes 393224 | tf_op jit(solution)/shard_map/ppermute | solution.py:113
  19.8 0.0 collective-permute-done.4.refs_4_.refs_6_.refs_1_
  19.8 0.3 collective-permute-start.7
  20.1 6.5 %collective-permute-done.8.refs_5_.refs_2_ = bf16[4,1,64,256]{3,2,1,0:T(8,128)(2,1)S(1)} collective-permute-done((bf16[4,1,64,256]{3,2,1,0:T(8,128)(2,1)S(1)}, bf16[4,1,64,256]{3,2,1,0:T(8,128)(2,1)S(1)}, u32[]{:S(2)}, u32[]{:S(2)}) %collective-permute-start.8) | collective-permute-done | bytes 131104 | tf_op jit(solution)/shard_map/ppermute | solution.py:113
  26.6 0.0 collective-permute-done.9.refs_6_.refs_3_
  26.6 0.0 collective-permute-done.5.refs_1_
  26.6 0.0 collective-permute-done.6.refs_2_
  26.6 0.0 collective-permute-done.7.refs_3_
  26.7 2.5 %collective-permute-start.10 = (bf16[4,1,64,256]{3,2,1,0:T(8,128)(2,1)S(1)}, bf16[4,1,64,256]{3,2,1,0:T(8,128)(2,1)S(1)}, u32[]{:S(2)}, u32[]{:S(2)}) collective-permute-start(bf16[4,1,64,256]{3,2,1,0:T(8,128)(2,1)S(1)} %get-tuple-element.60), channel_id=1, source_target_pairs={{0,8},{2,10},{4,12},{6,14},{8,0},{10,2},{12,4},{14,6},{16,24},{18,... | collective-permute-start | bytes 393224 | tf_op jit(solution)/shard_map/ppermute | solution.py:113
  29.1 1.7 %collective-permute-start.11 = (bf16[4,1,64,256]{3,2,1,0:T(8,128)(2,1)S(1)}, bf16[4,1,64,256]{3,2,1,0:T(8,128)(2,1)S(1)}, u32[]{:S(2)}, u32[]{:S(2)}) collective-permute-start(bf16[4,1,64,256]{3,2,1,0:T(8,128)(2,1)S(1)} %get-tuple-element.61), channel_id=1, source_target_pairs={{0,16},{2,18},{4,20},{6,22},{8,24},{10,26},{12,28},{14,30},{16,0},... | collective-permute-start | bytes 393224 | tf_op jit(solution)/shard_map/ppermute | solution.py:113
  30.9 0.7 collective-permute-start.12
  31.6 1.9 %collective-permute-done.10.refs_7_.refs_5_ = bf16[4,1,64,256]{3,2,1,0:T(8,128)(2,1)S(1)} collective-permute-done((bf16[4,1,64,256]{3,2,1,0:T(8,128)(2,1)S(1)}, bf16[4,1,64,256]{3,2,1,0:T(8,128)(2,1)S(1)}, u32[]{:S(2)}, u32[]{:S(2)}) %collective-permute-start.10) | collective-permute-done | bytes 131104 | tf_op jit(solution)/shard_map/ppermute | solution.py:113
  33.5 8.0 %collective-permute-done.11.refs_8_.refs_6_ = bf16[4,1,64,256]{3,2,1,0:T(8,128)(2,1)S(1)} collective-permute-done((bf16[4,1,64,256]{3,2,1,0:T(8,128)(2,1)S(1)}, bf16[4,1,64,256]{3,2,1,0:T(8,128)(2,1)S(1)}, u32[]{:S(2)}, u32[]{:S(2)}) %collective-permute-start.11) | collective-permute-done | bytes 131104 | tf_op jit(solution)/shard_map/ppermute | solution.py:113
  41.5 0.0 collective-permute-done.12.refs_9_.refs_7_
  41.5 0.0 copy-done.4
  41.5 2.3 %pack_filter_product.1 = (bf16[16,2,64,256]{3,2,1,0:T(8,128)(2,1)}, f32[8,128]{1,0:T(8,128)S(1)}) custom-call(s32[1]{0:T(128)} %constant.3.clone.1.at_ref, bf16[256,2048]{1,0:T(8,128)(2,1)S(1)} %copy-done.4, bf16[256,2048]{1,0:T(8,128)(2,1)S(1)} %copy-done, bf16[256,2048]{1,0:T(8,128)(2,1)S(1)} %copy-done.1, ...), custom_call_target="tpu_custom_call" | custom-call | flops 1000 | bytes 1000 | tf_op jit(solution)/shard_map/pack_filter_product/pallas_call | solution.py:73
  43.8 5.3 %all-to-all-start = ((bf16[16,2,64,256]{3,2,1,0:T(8,128)(2,1)}), bf16[16,2,64,256]{3,2,1,0:T(8,128)(2,1)S(1)}, u32[]{:S(2)}, u32[]{:S(2)}) async-start(bf16[16,2,64,256]{3,2,1,0:T(8,128)(2,1)} %get-tuple-element.70), calls=%async_computation | async-start | bytes 2097152 | tf_op jit(solution)/shard_map/all_to_all | solution.py:438
  49.1 0.8 fusion
  49.9 0.1 broadcast_in_dim.9.skip_ref
  50.0 10.3 %long_conv.2 = (bf16[4,64,256]{2,1,0:T(8,128)(2,1)S(1)}, bf16[4,64,256]{2,1,0:T(8,128)(2,1)S(1)}, bf16[4,64,256]{2,1,0:T(8,128)(2,1)S(1)}, bf16[4,64,256]{2,1,0:T(8,128)(2,1)S(1)}, f32[8,128]{1,0:T(8,128)S(1)}) custom-call(s32[1]{0:T(128)} %bitcast.at_ref, f32[64,128]{1,0:T(8,128)S(1)} %broadcast_in_dim.9.skip_ref, ...), custom_call_target="tpu_custom_call" | custom-call | flops 1000 | bytes 1000 | tf_op jit(solution)/shard_map/long_conv/pallas_call | solution.py:304
  60.3 11.7 %all-to-all-done.refs_0_ = bf16[16,2,64,256]{3,2,1,0:T(8,128)(2,1)S(1)} async-done(((bf16[16,2,64,256]{3,2,1,0:T(8,128)(2,1)}), bf16[16,2,64,256]{3,2,1,0:T(8,128)(2,1)S(1)}, u32[]{:S(2)}, u32[]{:S(2)}) %all-to-all-start) | async-done | bytes 1048608 | tf_op jit(solution)/shard_map/all_to_all | solution.py:438
  72.1 3.2 %collective-permute-start.13 = (bf16[4,64,256]{2,1,0:T(8,128)(2,1)S(1)}, bf16[4,64,256]{2,1,0:T(8,128)(2,1)S(1)}, u32[]{:S(2)}, u32[]{:S(2)}) collective-permute-start(bf16[4,64,256]{2,1,0:T(8,128)(2,1)S(1)} %get-tuple-element.72), channel_id=1, source_target_pairs={{0,8},{2,10},{4,12},{6,14},{8,0},{10,2},{12,4},{14,6},{16,24},{18,... | collective-permute-start | bytes 393224 | tf_op jit(solution)/shard_map/ppermute | solution.py:113
  75.3 1.9 %collective-permute-start.14 = (bf16[4,64,256]{2,1,0:T(8,128)(2,1)S(1)}, bf16[4,64,256]{2,1,0:T(8,128)(2,1)S(1)}, u32[]{:S(2)}, u32[]{:S(2)}) collective-permute-start(bf16[4,64,256]{2,1,0:T(8,128)(2,1)S(1)} %get-tuple-element.73), channel_id=1, source_target_pairs={{0,16},{2,18},{4,20},{6,22},{8,24},{10,26},{12,28},{14,30},{16,0},... | collective-permute-start | bytes 393224 | tf_op jit(solution)/shard_map/ppermute | solution.py:113
  77.1 1.5 %collective-permute-start.15 = (bf16[4,64,256]{2,1,0:T(8,128)(2,1)S(1)}, bf16[4,64,256]{2,1,0:T(8,128)(2,1)S(1)}, u32[]{:S(2)}, u32[]{:S(2)}) collective-permute-start(bf16[4,64,256]{2,1,0:T(8,128)(2,1)S(1)} %get-tuple-element.74), channel_id=1, source_target_pairs={{0,24},{2,26},{4,28},{6,30},{8,16},{10,18},{12,20},{14,22},{16,8},... | collective-permute-start | bytes 393224 | tf_op jit(solution)/shard_map/ppermute | solution.py:113
  78.6 0.1 broadcast_in_dim.20.skip_ref
  78.7 11.1 %long_conv.3 = (bf16[16,64,256]{2,1,0:T(8,128)(2,1)}, f32[8,128]{1,0:T(8,128)S(1)}) custom-call(s32[1]{0:T(128)} %constant.3.clone.1.at_ref, f32[64,128]{1,0:T(8,128)S(1)} %broadcast_in_dim.20.skip_ref, f32[8,128]{1,0:T(8,128)S(1)} %get-tuple-element.75.later_ref, bf16[16,2,64,256]{3,2,1,0:T(8,128)(2,1)S(1)} %all-to-all-done.refs_0_), custom_call_target="tpu_custom_call" | custom-call | flops 4294967296 | bytes 3145728 | tf_op jit(solution)/shard_map/long_conv/pallas_call | solution.py:304
  89.8 0.0 collective-permute-done.13.refs_1_
  89.8 0.0 collective-permute-done.14.refs_2_
  89.8 0.0 collective-permute-done.15.refs_3_
  89.8 4.9 %all-to-all-start.1 = ((bf16[16,64,256]{2,1,0:T(8,128)(2,1)}), bf16[16,64,256]{2,1,0:T(8,128)(2,1)}, u32[]{:S(2)}, u32[]{:S(2)}) async-start(bf16[16,64,256]{2,1,0:T(8,128)(2,1)} %get-tuple-element.79), calls=%async_computation.1 | async-start | bytes 1048576 | tf_op jit(solution)/shard_map/all_to_all | solution.py:438
  94.8 0.4 collective-permute-start.16
  95.2 1.7 %collective-permute-start.17 = (bf16[4,64,256]{2,1,0:T(8,128)(2,1)S(1)}, bf16[4,64,256]{2,1,0:T(8,128)(2,1)S(1)}, u32[]{:S(2)}, u32[]{:S(2)}) collective-permute-start(bf16[4,64,256]{2,1,0:T(8,128)(2,1)S(1)} %get-tuple-element.87), channel_id=1, source_target_pairs={{0,4},{2,6},{4,0},{6,2},{8,12},{10,14},{12,8},{14,10},{16,20},{18,... | collective-permute-start | bytes 393224 | tf_op jit(solution)/shard_map/ppermute | solution.py:113
  96.9 0.0 collective-permute-start.18
  96.9 0.0 collective-permute-done.16.refs_1_
  96.9 8.5 %collective-permute-done.17.refs_2_ = bf16[4,64,256]{2,1,0:T(8,128)(2,1)S(1)} collective-permute-done((bf16[4,64,256]{2,1,0:T(8,128)(2,1)S(1)}, bf16[4,64,256]{2,1,0:T(8,128)(2,1)S(1)}, u32[]{:S(2)}, u32[]{:S(2)}) %collective-permute-start.17) | collective-permute-done | bytes 131104 | tf_op jit(solution)/shard_map/ppermute | solution.py:113
  105.4 2.1 %collective-permute-done.18.refs_3_ = bf16[4,64,256]{2,1,0:T(8,128)(2,1)S(1)} collective-permute-done((bf16[4,64,256]{2,1,0:T(8,128)(2,1)S(1)}, bf16[4,64,256]{2,1,0:T(8,128)(2,1)S(1)}, u32[]{:S(2)}, u32[]{:S(2)}) %collective-permute-start.18) | collective-permute-done | bytes 131104 | tf_op jit(solution)/shard_map/ppermute | solution.py:113
  107.5 0.9 gated_squares.2
  108.4 0.0 copy-start.8
  108.4 0.8 all-to-all-done.1.refs_0_
  109.3 1.9 %gated_squares.3 = (f32[256,2048]{1,0:T(8,128)S(1)}, f32[8,256]{1,0:T(8,128)S(1)}) custom-call(s32[1]{0:T(128)} %constant.3.clone.1.at_ref, bf16[256,2048]{1,0:T(8,128)(2,1)S(1)} %copy-done.2, bf16[48,2048]{1,0:T(8,128)(2,1)S(1)} %collective-permute-done.refs_2_.refs_3_.halo_ref, f32[3,2048]{1,0:T(4,128)S(1)} %copy-done.7, ...), custom_call_target="tpu_custom_call", output_to_operand_aliasing={{0}: (6, {})} | custom-call | flops 1000 | bytes 1000 | tf_op jit(solution)/shard_map/gated_squares/pallas_call | solution.py:371
  111.2 1.5 %collective-permute-start.19 = (f32[8,256]{1,0:T(8,128)S(1)}, f32[8,256]{1,0:T(8,128)S(1)}, u32[]{:S(2)}, u32[]{:S(2)}) collective-permute-start(f32[8,256]{1,0:T(8,128)S(1)} %get-tuple-element.92.refs_0_), channel_id=1, source_target_pairs={{0,1},{1,0},{2,3},{3,2},{4,5},{5,4},{6,7},{7,6},{8,9},{9,8},{10,11... | collective-permute-start | bytes 24584 | tf_op jit(solution)/shard_map/ppermute | solution.py:477
  112.8 2.2 %collective-permute-done.19.refs_1_ = f32[8,256]{1,0:T(8,128)S(1)} collective-permute-done((f32[8,256]{1,0:T(8,128)S(1)}, f32[8,256]{1,0:T(8,128)S(1)}, u32[]{:S(2)}, u32[]{:S(2)}) %collective-permute-start.19) | collective-permute-done | bytes 8224 | tf_op jit(solution)/shard_map/ppermute | solution.py:477
  114.9 0.0 copy-done.8
  114.9 1.9 %normed.1 = bf16[256,2048]{1,0:T(8,128)(2,1)} custom-call(f32[256,2048]{1,0:T(8,128)S(1)} %get-tuple-element.91.gated_ref, f32[1,2048]{1,0:T(1,128)S(1)} %bitcast.2, f32[8,256]{1,0:T(8,128)S(1)} %get-tuple-element.92.refs_0_, f32[8,256]{1,0:T(8,128)S(1)} %collective-permute-done.19.refs_1_), custom_call_target="tpu_custom_call" | custom-call | flops 1000 | bytes 1000 | tf_op jit(solution)/shard_map/normed/pallas_call | solution.py:415
  (13 shorter events, 0.1 us)
Async XLA Ops:
  0.0 1.2 %copy-start.3 = (bf16[256,2048]{1,0:T(8,128)(2,1)S(1)}, bf16[256,2048]{1,0:T(8,128)(2,1)}, u32[]{:S(2)}) copy-start(bf16[256,2048]{1,0:T(8,128)(2,1)} %refs_0_.7) | copy-start | bytes 3145732
  2.2 14.3 %copy-start = (bf16[256,2048]{1,0:T(8,128)(2,1)S(1)}, bf16[256,2048]{1,0:T(8,128)(2,1)}, u32[]{:S(2)}) copy-start(bf16[256,2048]{1,0:T(8,128)(2,1)} %refs_1_.5) | copy-start | bytes 3145732
  2.2 14.3 %copy-start.1 = (bf16[256,2048]{1,0:T(8,128)(2,1)S(1)}, bf16[256,2048]{1,0:T(8,128)(2,1)}, u32[]{:S(2)}) copy-start(bf16[256,2048]{1,0:T(8,128)(2,1)} %refs_2_.3) | copy-start | bytes 3145732
  2.2 14.3 %copy-start.5 = (f32[3,2048]{1,0:T(4,128)S(1)}, f32[3,2048]{1,0:T(4,128)}, u32[]{:S(2)}) copy-start(f32[3,2048]{1,0:T(4,128)} %refs_4_.3) | copy-start | bytes 73732
  2.2 14.3 %copy-start.6 = (f32[3,2048]{1,0:T(4,128)S(1)}, f32[3,2048]{1,0:T(4,128)}, u32[]{:S(2)}) copy-start(f32[3,2048]{1,0:T(4,128)} %refs_5_.1) | copy-start | bytes 73732
  2.2 7.0 %collective-permute-start.1 = (bf16[4,1,64,256]{3,2,1,0:T(8,128)(2,1)S(1)}, bf16[4,1,64,256]{3,2,1,0:T(8,128)(2,1)S(1)}, u32[]{:S(2)}, u32[]{:S(2)}) collective-permute-start(bf16[4,1,64,256]{3,2,1,0:T(8,128)(2,1)S(1)} %get-tuple-element.50), channel_id=1, source_target_pairs={{0,2},{2,0},{4,6},{6,4},{8,10},{10,8},{12,14},{14,12},{16,18},{18,... | collective-permute-start | bytes 393224 | tf_op jit(solution)/shard_map/ppermute | solution.py:113
  2.7 6.9 %collective-permute-start.2 = (bf16[4,1,64,256]{3,2,1,0:T(8,128)(2,1)S(1)}, bf16[4,1,64,256]{3,2,1,0:T(8,128)(2,1)S(1)}, u32[]{:S(2)}, u32[]{:S(2)}) collective-permute-start(bf16[4,1,64,256]{3,2,1,0:T(8,128)(2,1)S(1)} %get-tuple-element.51), channel_id=1, source_target_pairs={{0,4},{2,6},{4,0},{6,2},{8,12},{10,14},{12,8},{14,10},{16,20},{18,... | collective-permute-start | bytes 393224 | tf_op jit(solution)/shard_map/ppermute | solution.py:113
  5.3 6.6 %collective-permute-start.3 = (bf16[4,1,64,256]{3,2,1,0:T(8,128)(2,1)S(1)}, bf16[4,1,64,256]{3,2,1,0:T(8,128)(2,1)S(1)}, u32[]{:S(2)}, u32[]{:S(2)}) collective-permute-start(bf16[4,1,64,256]{3,2,1,0:T(8,128)(2,1)S(1)} %get-tuple-element.52), channel_id=1, source_target_pairs={{0,6},{2,4},{4,2},{6,0},{8,14},{10,12},{12,10},{14,8},{16,22},{18,... | collective-permute-start | bytes 393224 | tf_op jit(solution)/shard_map/ppermute | solution.py:113
  7.0 34.5 %copy-start.4 = (bf16[256,2048]{1,0:T(8,128)(2,1)S(1)}, bf16[256,2048]{1,0:T(8,128)(2,1)}, u32[]{:S(2)}) copy-start(bf16[256,2048]{1,0:T(8,128)(2,1)} %refs_0_.7) | copy-start | bytes 3145732
  7.0 9.5 %collective-permute-start = (bf16[48,2048]{1,0:T(8,128)(2,1)}, bf16[48,2048]{1,0:T(8,128)(2,1)S(1)}, u32[]{:S(2)}, u32[]{:S(2)}) collective-permute-start(bf16[48,2048]{1,0:T(8,128)(2,1)} %tails.1), channel_id=1, source_target_pairs={{0,2},{2,4},{4,6},{6,8},{8,10},{10,12},{12,14},{14,16},{16,18},{18... | collective-permute-start | bytes 589832 | tf_op jit(solution)/shard_map/ppermute | solution.py:32
  12.0 7.8 %collective-permute-start.4 = (bf16[4,1,64,256]{3,2,1,0:T(8,128)(2,1)S(1)}, bf16[4,1,64,256]{3,2,1,0:T(8,128)(2,1)S(1)}, u32[]{:S(2)}, u32[]{:S(2)}) collective-permute-start(bf16[4,1,64,256]{3,2,1,0:T(8,128)(2,1)S(1)} %get-tuple-element.53), channel_id=1, source_target_pairs={{0,8},{2,10},{4,12},{6,14},{8,0},{10,2},{12,4},{14,6},{16,24},{18,... | collective-permute-start | bytes 393224 | tf_op jit(solution)/shard_map/ppermute | solution.py:113
  13.7 12.9 %collective-permute-start.8 = (bf16[4,1,64,256]{3,2,1,0:T(8,128)(2,1)S(1)}, bf16[4,1,64,256]{3,2,1,0:T(8,128)(2,1)S(1)}, u32[]{:S(2)}, u32[]{:S(2)}) collective-permute-start(bf16[4,1,64,256]{3,2,1,0:T(8,128)(2,1)S(1)} %get-tuple-element.58), channel_id=1, source_target_pairs={{0,16},{2,18},{4,20},{6,22},{8,24},{10,26},{12,28},{14,30},{16,0},... | collective-permute-start | bytes 393224 | tf_op jit(solution)/shard_map/ppermute | solution.py:113
  16.3 10.3 %collective-permute-start.9 = (bf16[4,1,64,256]{3,2,1,0:T(8,128)(2,1)S(1)}, bf16[4,1,64,256]{3,2,1,0:T(8,128)(2,1)S(1)}, u32[]{:S(2)}, u32[]{:S(2)}) collective-permute-start(bf16[4,1,64,256]{3,2,1,0:T(8,128)(2,1)S(1)} %get-tuple-element.59), channel_id=1, source_target_pairs={{0,24},{2,26},{4,28},{6,30},{8,16},{10,18},{12,20},{14,22},{16,8},... | collective-permute-start | bytes 393224 | tf_op jit(solution)/shard_map/ppermute | solution.py:113
  18.2 8.4 %collective-permute-start.5 = (bf16[4,1,64,256]{3,2,1,0:T(8,128)(2,1)S(1)}, bf16[4,1,64,256]{3,2,1,0:T(8,128)(2,1)S(1)}, u32[]{:S(2)}, u32[]{:S(2)}) collective-permute-start(bf16[4,1,64,256]{3,2,1,0:T(8,128)(2,1)S(1)} %get-tuple-element.55), channel_id=1, source_target_pairs={{0,2},{2,0},{4,6},{6,4},{8,10},{10,8},{12,14},{14,12},{16,18},{18,... | collective-permute-start | bytes 393224 | tf_op jit(solution)/shard_map/ppermute | solution.py:113
  18.2 8.4 %collective-permute-start.6 = (bf16[4,1,64,256]{3,2,1,0:T(8,128)(2,1)S(1)}, bf16[4,1,64,256]{3,2,1,0:T(8,128)(2,1)S(1)}, u32[]{:S(2)}, u32[]{:S(2)}) collective-permute-start(bf16[4,1,64,256]{3,2,1,0:T(8,128)(2,1)S(1)} %get-tuple-element.56), channel_id=1, source_target_pairs={{0,4},{2,6},{4,0},{6,2},{8,12},{10,14},{12,8},{14,10},{16,20},{18,... | collective-permute-start | bytes 393224 | tf_op jit(solution)/shard_map/ppermute | solution.py:113
  19.8 6.8 %collective-permute-start.7 = (bf16[4,1,64,256]{3,2,1,0:T(8,128)(2,1)S(1)}, bf16[4,1,64,256]{3,2,1,0:T(8,128)(2,1)S(1)}, u32[]{:S(2)}, u32[]{:S(2)}) collective-permute-start(bf16[4,1,64,256]{3,2,1,0:T(8,128)(2,1)S(1)} %get-tuple-element.57), channel_id=1, source_target_pairs={{0,6},{2,4},{4,2},{6,0},{8,14},{10,12},{12,10},{14,8},{16,22},{18,... | collective-permute-start | bytes 393224 | tf_op jit(solution)/shard_map/ppermute | solution.py:113
  26.7 6.8 %collective-permute-start.10 = (bf16[4,1,64,256]{3,2,1,0:T(8,128)(2,1)S(1)}, bf16[4,1,64,256]{3,2,1,0:T(8,128)(2,1)S(1)}, u32[]{:S(2)}, u32[]{:S(2)}) collective-permute-start(bf16[4,1,64,256]{3,2,1,0:T(8,128)(2,1)S(1)} %get-tuple-element.60), channel_id=1, source_target_pairs={{0,8},{2,10},{4,12},{6,14},{8,0},{10,2},{12,4},{14,6},{16,24},{18,... | collective-permute-start | bytes 393224 | tf_op jit(solution)/shard_map/ppermute | solution.py:113
  29.1 12.3 %collective-permute-start.11 = (bf16[4,1,64,256]{3,2,1,0:T(8,128)(2,1)S(1)}, bf16[4,1,64,256]{3,2,1,0:T(8,128)(2,1)S(1)}, u32[]{:S(2)}, u32[]{:S(2)}) collective-permute-start(bf16[4,1,64,256]{3,2,1,0:T(8,128)(2,1)S(1)} %get-tuple-element.61), channel_id=1, source_target_pairs={{0,16},{2,18},{4,20},{6,22},{8,24},{10,26},{12,28},{14,30},{16,0},... | collective-permute-start | bytes 393224 | tf_op jit(solution)/shard_map/ppermute | solution.py:113
  30.9 10.6 %collective-permute-start.12 = (bf16[4,1,64,256]{3,2,1,0:T(8,128)(2,1)S(1)}, bf16[4,1,64,256]{3,2,1,0:T(8,128)(2,1)S(1)}, u32[]{:S(2)}, u32[]{:S(2)}) collective-permute-start(bf16[4,1,64,256]{3,2,1,0:T(8,128)(2,1)S(1)} %get-tuple-element.62), channel_id=1, source_target_pairs={{0,24},{2,26},{4,28},{6,30},{8,16},{10,18},{12,20},{14,22},{16,8},... | collective-permute-start | bytes 393224 | tf_op jit(solution)/shard_map/ppermute | solution.py:113
  43.8 28.3 %all-to-all-start = ((bf16[16,2,64,256]{3,2,1,0:T(8,128)(2,1)}), bf16[16,2,64,256]{3,2,1,0:T(8,128)(2,1)S(1)}, u32[]{:S(2)}, u32[]{:S(2)}) async-start(bf16[16,2,64,256]{3,2,1,0:T(8,128)(2,1)} %get-tuple-element.70), calls=%async_computation | async-start | bytes 2097152 | tf_op jit(solution)/shard_map/all_to_all | solution.py:438
  72.1 17.7 %collective-permute-start.13 = (bf16[4,64,256]{2,1,0:T(8,128)(2,1)S(1)}, bf16[4,64,256]{2,1,0:T(8,128)(2,1)S(1)}, u32[]{:S(2)}, u32[]{:S(2)}) collective-permute-start(bf16[4,64,256]{2,1,0:T(8,128)(2,1)S(1)} %get-tuple-element.72), channel_id=1, source_target_pairs={{0,8},{2,10},{4,12},{6,14},{8,0},{10,2},{12,4},{14,6},{16,24},{18,... | collective-permute-start | bytes 393224 | tf_op jit(solution)/shard_map/ppermute | solution.py:113
  75.3 14.5 %collective-permute-start.14 = (bf16[4,64,256]{2,1,0:T(8,128)(2,1)S(1)}, bf16[4,64,256]{2,1,0:T(8,128)(2,1)S(1)}, u32[]{:S(2)}, u32[]{:S(2)}) collective-permute-start(bf16[4,64,256]{2,1,0:T(8,128)(2,1)S(1)} %get-tuple-element.73), channel_id=1, source_target_pairs={{0,16},{2,18},{4,20},{6,22},{8,24},{10,26},{12,28},{14,30},{16,0},... | collective-permute-start | bytes 393224 | tf_op jit(solution)/shard_map/ppermute | solution.py:113
  77.1 12.7 %collective-permute-start.15 = (bf16[4,64,256]{2,1,0:T(8,128)(2,1)S(1)}, bf16[4,64,256]{2,1,0:T(8,128)(2,1)S(1)}, u32[]{:S(2)}, u32[]{:S(2)}) collective-permute-start(bf16[4,64,256]{2,1,0:T(8,128)(2,1)S(1)} %get-tuple-element.74), channel_id=1, source_target_pairs={{0,24},{2,26},{4,28},{6,30},{8,16},{10,18},{12,20},{14,22},{16,8},... | collective-permute-start | bytes 393224 | tf_op jit(solution)/shard_map/ppermute | solution.py:113
  78.7 28.8 %copy-start.7 = (f32[3,2048]{1,0:T(4,128)S(1)}, f32[3,2048]{1,0:T(4,128)}, u32[]{:S(2)}) copy-start(f32[3,2048]{1,0:T(4,128)} %taps_ref.3) | copy-start | bytes 73732
  89.8 17.7 %copy-start.2 = (bf16[256,2048]{1,0:T(8,128)(2,1)S(1)}, bf16[256,2048]{1,0:T(8,128)(2,1)}, u32[]{:S(2)}) copy-start(bf16[256,2048]{1,0:T(8,128)(2,1)} %gate_ref.3) | copy-start | bytes 3145732
  89.8 19.4 %all-to-all-start.1 = ((bf16[16,64,256]{2,1,0:T(8,128)(2,1)}), bf16[16,64,256]{2,1,0:T(8,128)(2,1)}, u32[]{:S(2)}, u32[]{:S(2)}) async-start(bf16[16,64,256]{2,1,0:T(8,128)(2,1)} %get-tuple-element.79), calls=%async_computation.1 | async-start | bytes 1048576 | tf_op jit(solution)/shard_map/all_to_all | solution.py:438
  94.8 2.1 %collective-permute-start.16 = (bf16[4,64,256]{2,1,0:T(8,128)(2,1)S(1)}, bf16[4,64,256]{2,1,0:T(8,128)(2,1)S(1)}, u32[]{:S(2)}, u32[]{:S(2)}) collective-permute-start(bf16[4,64,256]{2,1,0:T(8,128)(2,1)S(1)} %get-tuple-element.86), channel_id=1, source_target_pairs={{0,2},{2,0},{4,6},{6,4},{8,10},{10,8},{12,14},{14,12},{16,18},{18,... | collective-permute-start | bytes 393224 | tf_op jit(solution)/shard_map/ppermute | solution.py:113
  95.2 10.2 %collective-permute-start.17 = (bf16[4,64,256]{2,1,0:T(8,128)(2,1)S(1)}, bf16[4,64,256]{2,1,0:T(8,128)(2,1)S(1)}, u32[]{:S(2)}, u32[]{:S(2)}) collective-permute-start(bf16[4,64,256]{2,1,0:T(8,128)(2,1)S(1)} %get-tuple-element.87), channel_id=1, source_target_pairs={{0,4},{2,6},{4,0},{6,2},{8,12},{10,14},{12,8},{14,10},{16,20},{18,... | collective-permute-start | bytes 393224 | tf_op jit(solution)/shard_map/ppermute | solution.py:113
  96.9 10.6 %collective-permute-start.18 = (bf16[4,64,256]{2,1,0:T(8,128)(2,1)S(1)}, bf16[4,64,256]{2,1,0:T(8,128)(2,1)S(1)}, u32[]{:S(2)}, u32[]{:S(2)}) collective-permute-start(bf16[4,64,256]{2,1,0:T(8,128)(2,1)S(1)} %get-tuple-element.88), channel_id=1, source_target_pairs={{0,6},{2,4},{4,2},{6,0},{8,14},{10,12},{12,10},{14,8},{16,22},{18,... | collective-permute-start | bytes 393224 | tf_op jit(solution)/shard_map/ppermute | solution.py:113
  108.4 6.5 %copy-start.8 = (f32[2048]{0:T(1024)S(1)}, f32[2048]{0:T(1024)}, u32[]{:S(2)}) copy-start(f32[2048]{0:T(1024)} %param.17) | copy-start | bytes 24580
  111.2 3.7 %collective-permute-start.19 = (f32[8,256]{1,0:T(8,128)S(1)}, f32[8,256]{1,0:T(8,128)S(1)}, u32[]{:S(2)}, u32[]{:S(2)}) collective-permute-start(f32[8,256]{1,0:T(8,128)S(1)} %get-tuple-element.92.refs_0_), channel_id=1, source_target_pairs={{0,1},{1,0},{2,3},{3,2},{4,5},{5,4},{6,7},{7,6},{8,9},{9,8},{10,11... | collective-permute-start | bytes 24584 | tf_op jit(solution)/shard_map/ppermute | solution.py:477

commit v3 on v2

--- a/solution.py
+++ b/solution.py
@@ -46,6 +46,7 @@
     refs, outs, done_ref, held = list(refs[:arrays]), refs[arrays + waits : -2], refs[-2], refs[-1]
     done_ref[...] = jnp.zeros_like(done_ref)
     _, _, narrow, tok = held.shape
+    near = outs[0].shape[0]
     count = WIDE // narrow
     step = pl.program_id(0)
     for at, want in enumerate(wants):
@@ -60,16 +61,16 @@
 
     @pl.when(step == pl.num_programs(0) - 1)
     def _():
-        for i, out_ref in enumerate(outs):
-            for j in range(out_ref.shape[0]):
-                out_ref[j] = held[at_ref[0] ^ (len(outs) * j + i)]
+        for j, out_ref in enumerate(outs):
+            for i in range(near):
+                out_ref[i] = held[at_ref[0] ^ (near * j + i)]
 
 
 def packed(wants, arrays, later, part, near, position):
     start, narrow, blocks = part
     tok = arrays[0].shape[0]
     first = start // WIDE
-    shape = (blocks // near, len(wants), narrow, tok)
+    shape = (near, len(wants), narrow, tok)
     return pl.pallas_call(
         functools.partial(pack_kernel, wants, len(later)),
         grid_spec=pltpu.PrefetchScalarGridSpec(
@@ -80,11 +81,11 @@
                 for array in arrays
             ]
             + [corner(array) for array in later],
-            out_specs=[pl.BlockSpec(shape, lambda i, at: (0, 0, 0, 0))] * near
+            out_specs=[pl.BlockSpec(shape, lambda i, at: (0, 0, 0, 0))] * (blocks // near)
             + [pl.BlockSpec(DONE.shape, lambda i, at: (0, 0))],
             scratch_shapes=[pltpu.VMEM((blocks,) + shape[1:], BF16)],
         ),
-        out_shape=[jax.ShapeDtypeStruct(shape, BF16)] * near + [DONE],
+        out_shape=[jax.ShapeDtypeStruct(shape, BF16)] * (blocks // near) + [DONE],
         compiler_params=pltpu.CompilerParams(vmem_limit_bytes=VMEM_BYTES),
         cost_estimate=BRIEF,
         name="pack_" + "_".join(wants),
@@ -119,34 +120,31 @@
     return [lines[0]] + [came[j] for j in range(1, len(lines))]
 
 
-def plane_first(parts):
-    return [parts[0]] + [swapped(parts[i], i) for i in range(1, NEAR)]
-
-
-def regroup_kernel(count, *refs):
-    for i, out_ref in enumerate(refs[-count:]):
+def regroup_kernel(*refs):
+    outs = refs[-NEAR:]
+    for i, out_ref in enumerate(outs):
         for j in range(out_ref.shape[0]):
             out_ref[j] = refs[j][i]
 
 
 def regroup(lines, later):
     whole = lambda array: pl.BlockSpec(array.shape, lambda i: (0,) * len(array.shape))
-    count = lines[0].shape[0]
-    out_shape = [jax.ShapeDtypeStruct((len(lines),) + lines[0].shape[1:], BF16)] * count
-    return pl.pallas_call(
-        functools.partial(regroup_kernel, count),
+    out_shape = [jax.ShapeDtypeStruct((len(lines),) + lines[0].shape[1:], BF16)] * NEAR
+    return pl.pallas_call(
+        regroup_kernel,
         grid=(1,),
-        in_specs=[whole(line) for line in lines] + [corner(array) for array in later],
+        in_specs=[whole(line) for line in lines] + [corner(later)],
         out_specs=[whole(array) for array in out_shape],
         out_shape=out_shape,
         compiler_params=pltpu.CompilerParams(vmem_limit_bytes=VMEM_BYTES),
         cost_estimate=BRIEF,
         name="regroup",
-    )(*lines, *later)
+    )(*lines, later)
 
 
 def swap_near(lines, later):
-    return plane_first(regroup(lines, later))
+    parts = regroup(lines, later)
+    return [parts[0]] + [swapped(parts[i], i) for i in range(1, NEAR)]
 
 
 def delayed(rows, by):
@@ -192,12 +190,12 @@
     turns = blocks // 2
     units = lanes // 16
 
-    for j, (filt_ref, prod_ref) in enumerate(zip(filt_refs, prod_refs)):
-        for i in range(filt_ref.shape[0]):
-            block = at_ref[0] ^ (filt_ref.shape[0] * j + i)
+    for i, (filt_ref, prod_ref) in enumerate(zip(filt_refs, prod_refs)):
+        for j in range(filt_ref.shape[0]):
+            block = at_ref[0] ^ (len(filt_refs) * j + i)
             lags = pl.ds(pl.multiple_of(block * tok, tok), tok)
-            filt[:, lags] = filt_ref[i, 0].astype(F32)
-            prod[block] = prod_ref[i, int(merged)].astype(F32)
+            filt[:, lags] = filt_ref[j, 0].astype(F32)
+            prod[block] = prod_ref[j, int(merged)].astype(F32)
     base[:, :, :LANES] = jnp.zeros((2, GROUP * FINE, LANES), BF16)
 
     def pairs_of(row, side):
@@ -452,22 +450,23 @@
         return jnp.broadcast_to(skip[:, None], (narrow, LANES))
 
     halo = passed_along(tails((key_in, value_in, gate_in)), "seq", 1)
-    *lines, _ = pack(("filter",), starts[0], NEAR, position, [])
-    filters = swap_far(regroup(plane_first(lines), []))
-    *product, _ = pack(("product",), starts[0], NEAR, position, [])
-    product = plane_first(product)
-    products = swap_far(regroup(product, filters[1:]))
-    second, done = pack(("filter", "product"), starts[1], 1, natural, filters[1:2] + products[1:])
+    *lines, ended = pack(("filter",), starts[0], NEAR, position, [])
+    lines = swap_far(lines)
+    *product, _ = pack(("product",), starts[0], NEAR, position, [ended])
+    came = swap_far(product)
+    filters = swap_near(lines, came[2])
+    products = swap_near(came, lines[2])
+    later = [filters[2], products[2]]
+    second, done = pack(("filter", "product"), starts[1], blocks, natural, later)
     second = exchange(second)
     *lines, ended = long_conv(filters + products, skip_of(starts[0]), done, blocks, NEAR, position)
-    lines, second = lax.optimization_barrier((lines, second))
     lines = swap_far(lines)
     cost = pl.CostEstimate(
         flops=2 * width * tok * tok * blocks, bytes_accessed=6 * tok * width, transcendentals=0
     )
     last, done = long_conv([second], skip_of(starts[1]), ended, blocks, blocks, natural, cost)
     lines, last, done = lax.optimization_barrier((lines, last, done))
-    first = swap_near(lines, [done])
+    first = swap_near(lines, done)
     last = exchange(last)
     gated = gated_of(gate_in, halo, gate_short, first, starts[0], None, position)
     gated = gated_of(gate_in, halo, gate_short, [last], starts[1], gated, natural)

time: 117 us -> 120 us (1.026)
  starting transfers between devices: 37 us -> 40.9 us
  waiting for transfers between devices: 44.5 us -> 42.6 us
  local copies, waits for them, and re-layouts: 2.18 us -> 3.89 us
  Pallas kernels: 33 us -> 31.6 us
    all_to_all x2, waiting for transfers between devices: 12.6 us -> 0.84 us  [local(): lax.all_to_all(rows, 'seq', split_axis=0, concat_axis=0, tiled=True)]
    ppermute x18, waiting for transfers between devices: 29.7 us -> 39.6 us  [swapped(): return lax.ppermute(rows, 'seq', [(i, i ^ by) for i in range(size)])]
    ppermute x18, starting transfers between devices: 23.1 us -> 26.1 us  [swapped(): return lax.ppermute(rows, 'seq', [(i, i ^ by) for i in range(size)])]
    unnamed x18 -> x42, local copies, waits for them, and re-layouts: 1.26 us -> 2.97 us
    pallas_call x3, Pallas kernels: 5.01 us -> 3.49 us  [packed(): pl.pallas_call(functools.partial(pack_kernel, wants, len(later)), grid_sp...]
  transfers between devices with their start and end apart: 22 -> 22, of which waited for: 10 -> 10; matrix products, arithmetic and copies ran while one was open for 1% -> 1% of each run, Pallas kernels for 22% -> 21%
where the time goes in v3:
time: 120 us; the launch traced here: 119 us
  waiting for transfers between devices  42.6 us (36%)
  starting transfers between devices  40.9 us (34%)
  Pallas kernels  31.6 us (26%)
  local copies, waits for them, and re-layouts  3.89 us (3%)
    ppermute x18, waiting for transfers between devices, swapped(): return lax.ppermute(rows, 'seq', [(i, i ^ by) for i in range(size)])  39.6 us
    ppermute x18, starting transfers between devices, swapped(): return lax.ppermute(rows, 'seq', [(i, i ^ by) for i in range(size)])  26.1 us
    pallas_call x2, Pallas kernels, long_conv(): pl.pallas_call(conv_kernel, grid_spec=pltpu.PrefetchScalarGridSpec(num_sc...  21.5 us
    all_to_all x2, starting transfers between devices, local(): lax.all_to_all(rows, 'seq', split_axis=0, concat_axis=0, tiled=True)  10.9 us
    pallas_call x3, Pallas kernels, packed(): pl.pallas_call(functools.partial(pack_kernel, wants, len(later)), grid_sp...  3.49 us
    unnamed x42, local copies, waits for them, and re-layouts  2.97 us
    pallas_call x2, Pallas kernels, gated_of(): pl.pallas_call(gated_kernel, grid_spec=pltpu.PrefetchScalarGridSpec(num_s...  2.9 us
  transfers between devices with their start and end apart: 22, of which 10 were waited for; matrix products, arithmetic and copies ran while one was open for 1% of the time, Pallas kernels for 21%

profile of v3, /device:TPU:0, one launch (start us, length us, event | category | flops | bytes accessed | tf_op | source)
XLA Modules:
  0.0 119.3 jit_solution(9007204867492795986)
XLA Ops:
  0.0 1.8 %tails.1 = bf16[48,2048]{1,0:T(8,128)(2,1)} custom-call(bf16[256,2048]{1,0:T(8,128)(2,1)} %refs_1_.5, bf16[256,2048]{1,0:T(8,128)(2,1)} %refs_2_.3, bf16[256,2048]{1,0:T(8,128)(2,1)} %gate_ref.3), custom_call_target="tpu_custom_call" | custom-call | tf_op jit(solution)/shard_map/tails/pallas_call | solution.py:102
  1.8 2.4 %collective-permute-start = (bf16[48,2048]{1,0:T(8,128)(2,1)}, bf16[48,2048]{1,0:T(8,128)(2,1)S(1)}, u32[]{:S(2)}, u32[]{:S(2)}) collective-permute-start(bf16[48,2048]{1,0:T(8,128)(2,1)} %tails.1), channel_id=1, source_target_pairs={{0,2},{2,4},{4,6},{6,8},{8,10},{10,12},{12,14},{14,16},{16,18},{18... | collective-permute-start | bytes 589832 | tf_op jit(solution)/shard_map/ppermute | solution.py:32
  4.2 0.4 pack_filter.1
  4.6 2.6 %collective-permute-start.1 = (bf16[4,1,64,256]{3,2,1,0:T(8,128)(2,1)S(1)}, bf16[4,1,64,256]{3,2,1,0:T(8,128)(2,1)S(1)}, u32[]{:S(2)}, u32[]{:S(2)}) collective-permute-start(bf16[4,1,64,256]{3,2,1,0:T(8,128)(2,1)S(1)} %get-tuple-element.46), channel_id=1, source_target_pairs={{0,8},{2,10},{4,12},{6,14},{8,0},{10,2},{12,4},{14,6},{16,24},{18,... | collective-permute-start | bytes 393224 | tf_op jit(solution)/shard_map/ppermute | solution.py:114
  7.2 2.6 %collective-permute-start.2 = (bf16[4,1,64,256]{3,2,1,0:T(8,128)(2,1)S(1)}, bf16[4,1,64,256]{3,2,1,0:T(8,128)(2,1)S(1)}, u32[]{:S(2)}, u32[]{:S(2)}) collective-permute-start(bf16[4,1,64,256]{3,2,1,0:T(8,128)(2,1)S(1)} %get-tuple-element.47), channel_id=1, source_target_pairs={{0,16},{2,18},{4,20},{6,22},{8,24},{10,26},{12,28},{14,30},{16,0},... | collective-permute-start | bytes 393224 | tf_op jit(solution)/shard_map/ppermute | solution.py:114
  9.8 0.0 collective-permute-start.3
  9.8 0.0 collective-permute-done.refs_2_.refs_3_.halo_ref
  9.9 1.7 %pack_product.1 = (bf16[4,1,64,256]{3,2,1,0:T(8,128)(2,1)S(1)}, bf16[4,1,64,256]{3,2,1,0:T(8,128)(2,1)S(1)}, bf16[4,1,64,256]{3,2,1,0:T(8,128)(2,1)S(1)}, bf16[4,1,64,256]{3,2,1,0:T(8,128)(2,1)S(1)}, f32[8,128]{1,0:T(8,128)}) custom-call(s32[1]{0:T(128)} %bitcast.at_ref, bf16[256,2048]{1,0:T(8,128)(2,1)S(1)} %copy-done.1, bf16[256,2048]{1,0:T(8,128)(2,1)S(1)} %copy-done.2, ...), custom_call_target="tpu_custom_call" | custom-call | flops 1000 | bytes 1000 | tf_op jit(solution)/shard_map/pack_product/pallas_call | solution.py:74
  11.6 4.1 %collective-permute-start.4 = (bf16[4,1,64,256]{3,2,1,0:T(8,128)(2,1)S(1)}, bf16[4,1,64,256]{3,2,1,0:T(8,128)(2,1)S(1)}, u32[]{:S(2)}, u32[]{:S(2)}) collective-permute-start(bf16[4,1,64,256]{3,2,1,0:T(8,128)(2,1)S(1)} %get-tuple-element.50), channel_id=1, source_target_pairs={{0,16},{2,18},{4,20},{6,22},{8,24},{10,26},{12,28},{14,30},{16,0},... | collective-permute-start | bytes 393224 | tf_op jit(solution)/shard_map/ppermute | solution.py:114
  15.7 4.9 %collective-permute-start.6 = (bf16[4,1,64,256]{3,2,1,0:T(8,128)(2,1)S(1)}, bf16[4,1,64,256]{3,2,1,0:T(8,128)(2,1)S(1)}, u32[]{:S(2)}, u32[]{:S(2)}) collective-permute-start(bf16[4,1,64,256]{3,2,1,0:T(8,128)(2,1)S(1)} %get-tuple-element.53), channel_id=1, source_target_pairs={{0,8},{2,10},{4,12},{6,14},{8,0},{10,2},{12,4},{14,6},{16,24},{18,... | collective-permute-start | bytes 393224 | tf_op jit(solution)/shard_map/ppermute | solution.py:114
  20.5 0.0 collective-permute-done.1.refs_1_
  20.5 0.0 collective-permute-start.7
  20.5 0.7 collective-permute-done.2.refs_2_.refs_4_
  21.3 0.0 collective-permute-done.3.refs_3_
  21.3 9.8 %collective-permute-done.4.refs_4_.refs_2_ = bf16[4,1,64,256]{3,2,1,0:T(8,128)(2,1)S(1)} collective-permute-done((bf16[4,1,64,256]{3,2,1,0:T(8,128)(2,1)S(1)}, bf16[4,1,64,256]{3,2,1,0:T(8,128)(2,1)S(1)}, u32[]{:S(2)}, u32[]{:S(2)}) %collective-permute-start.4) | collective-permute-done | bytes 131104 | tf_op jit(solution)/shard_map/ppermute | solution.py:114
  31.2 1.6 %collective-permute-start.5 = (bf16[4,1,64,256]{3,2,1,0:T(8,128)(2,1)S(1)}, bf16[4,1,64,256]{3,2,1,0:T(8,128)(2,1)S(1)}, u32[]{:S(2)}, u32[]{:S(2)}) collective-permute-start(bf16[4,1,64,256]{3,2,1,0:T(8,128)(2,1)S(1)} %get-tuple-element.51), channel_id=1, source_target_pairs={{0,4},{2,6},{4,0},{6,2},{8,12},{10,14},{12,8},{14,10},{16,20},{18,... | collective-permute-start | bytes 393224 | tf_op jit(solution)/shard_map/ppermute | solution.py:114
  32.8 0.0 collective-permute-done.6.refs_1_
  32.8 0.0 collective-permute-done.7.refs_3_
  32.8 0.0 copy-done.15
  32.9 0.6 copy-done.12
  33.5 0.6 copy-done.17
  34.2 0.6 copy-done.19
  34.8 0.6 collective-permute-start.8
  35.4 1.6 %collective-permute-done.5.refs_6_.refs_2_ = bf16[4,1,64,256]{3,2,1,0:T(8,128)(2,1)S(1)} collective-permute-done((bf16[4,1,64,256]{3,2,1,0:T(8,128)(2,1)S(1)}, bf16[4,1,64,256]{3,2,1,0:T(8,128)(2,1)S(1)}, u32[]{:S(2)}, u32[]{:S(2)}) %collective-permute-start.5) | collective-permute-done | bytes 131104 | tf_op jit(solution)/shard_map/ppermute | solution.py:114
  37.0 3.3 %collective-permute-done.8.refs_7_.refs_6_ = bf16[4,1,64,256]{3,2,1,0:T(8,128)(2,1)S(1)} collective-permute-done((bf16[4,1,64,256]{3,2,1,0:T(8,128)(2,1)S(1)}, bf16[4,1,64,256]{3,2,1,0:T(8,128)(2,1)S(1)}, u32[]{:S(2)}, u32[]{:S(2)}) %collective-permute-start.8) | collective-permute-done | bytes 131104 | tf_op jit(solution)/shard_map/ppermute | solution.py:114
  40.3 1.3 %pack_filter_product.1 = (bf16[16,2,64,256]{3,2,1,0:T(8,128)(2,1)S(1)}, f32[8,128]{1,0:T(8,128)S(1)}) custom-call(s32[1]{0:T(128)} %constant.3.clone.1.at_ref, bf16[256,2048]{1,0:T(8,128)(2,1)S(1)} %copy-done.3, bf16[256,2048]{1,0:T(8,128)(2,1)S(1)} %copy-done.1, bf16[256,2048]{1,0:T(8,128)(2,1)S(1)} %copy-done.2, ...), custom_call_target="tpu_custom_call" | custom-call | flops 1000 | bytes 1000 | tf_op jit(solution)/shard_map/pack_filter_product/pallas_call | solution.py:74
  41.7 0.0 copy-start.4
  41.7 1.0 copy-done.4
  42.6 5.5 %all-to-all-start = ((bf16[16,2,64,256]{3,2,1,0:T(8,128)(2,1)}), bf16[16,2,64,256]{3,2,1,0:T(8,128)(2,1)S(1)}, u32[]{:S(2)}, u32[]{:S(2)}) async-start(bf16[16,2,64,256]{3,2,1,0:T(8,128)(2,1)} %copy-done.4), calls=%async_computation | async-start | bytes 2097152 | tf_op jit(solution)/shard_map/all_to_all | solution.py:436
  48.2 0.4 collective-permute-start.9
  48.6 1.6 %collective-permute-start.10 = (bf16[4,1,64,256]{3,2,1,0:T(8,128)(2,1)}, bf16[4,1,64,256]{3,2,1,0:T(8,128)(2,1)S(1)}, u32[]{:S(2)}, u32[]{:S(2)}) collective-permute-start(bf16[4,1,64,256]{3,2,1,0:T(8,128)(2,1)} %copy-done.15), channel_id=1, source_target_pairs={{0,6},{2,4},{4,2},{6,0},{8,14},{10,12},{12,10},{14,8},{16,22},{18,... | collective-permute-start | bytes 393224 | tf_op jit(solution)/shard_map/ppermute | solution.py:114
  50.2 0.2 collective-permute-start.11
  50.4 0.1 collective-permute-start.12
  50.5 0.8 fusion
  51.3 0.0 collective-permute-done.9.refs_1_
  51.3 9.1 %collective-permute-done.10.refs_3_ = bf16[4,1,64,256]{3,2,1,0:T(8,128)(2,1)S(1)} collective-permute-done((bf16[4,1,64,256]{3,2,1,0:T(8,128)(2,1)}, bf16[4,1,64,256]{3,2,1,0:T(8,128)(2,1)S(1)}, u32[]{:S(2)}, u32[]{:S(2)}) %collective-permute-start.10) | collective-permute-done | bytes 131104 | tf_op jit(solution)/shard_map/ppermute | solution.py:114
  60.3 0.0 collective-permute-done.11.refs_5_
  60.3 4.5 %collective-permute-done.12.refs_7_ = bf16[4,1,64,256]{3,2,1,0:T(8,128)(2,1)S(1)} collective-permute-done((bf16[4,1,64,256]{3,2,1,0:T(8,128)(2,1)S(1)}, bf16[4,1,64,256]{3,2,1,0:T(8,128)(2,1)S(1)}, u32[]{:S(2)}, u32[]{:S(2)}) %collective-permute-start.12) | collective-permute-done | bytes 131104 | tf_op jit(solution)/shard_map/ppermute | solution.py:114
  64.9 0.1 broadcast_in_dim.9.skip_ref
  64.9 0.0 copy-done.13
  64.9 10.3 %long_conv.2 = (bf16[4,64,256]{2,1,0:T(8,128)(2,1)S(1)}, bf16[4,64,256]{2,1,0:T(8,128)(2,1)S(1)}, bf16[4,64,256]{2,1,0:T(8,128)(2,1)S(1)}, bf16[4,64,256]{2,1,0:T(8,128)(2,1)S(1)}, f32[8,128]{1,0:T(8,128)S(1)}) custom-call(s32[1]{0:T(128)} %bitcast.at_ref, f32[64,128]{1,0:T(8,128)S(1)} %broadcast_in_dim.9.skip_ref, ...), custom_call_target="tpu_custom_call" | custom-call | flops 1000 | bytes 1000 | tf_op jit(solution)/shard_map/long_conv/pallas_call | solution.py:302
  75.3 0.1 collective-permute-start.13
  75.4 5.2 %collective-permute-start.14 = (bf16[4,64,256]{2,1,0:T(8,128)(2,1)S(1)}, bf16[4,64,256]{2,1,0:T(8,128)(2,1)S(1)}, u32[]{:S(2)}, u32[]{:S(2)}) collective-permute-start(bf16[4,64,256]{2,1,0:T(8,128)(2,1)S(1)} %get-tuple-element.65), channel_id=1, source_target_pairs={{0,16},{2,18},{4,20},{6,22},{8,24},{10,26},{12,28},{14,30},{16,0},... | collective-permute-start | bytes 393224 | tf_op jit(solution)/shard_map/ppermute | solution.py:114
  80.6 0.0 collective-permute-start.15
  80.6 0.0 all-to-all-done.refs_0_
  80.6 0.1 broadcast_in_dim.20.skip_ref
  80.7 11.1 %long_conv.3 = (bf16[16,64,256]{2,1,0:T(8,128)(2,1)}, f32[8,128]{1,0:T(8,128)S(1)}) custom-call(s32[1]{0:T(128)} %constant.3.clone.1.at_ref, f32[64,128]{1,0:T(8,128)S(1)} %broadcast_in_dim.20.skip_ref, f32[8,128]{1,0:T(8,128)S(1)} %get-tuple-element.67.later_ref, bf16[16,2,64,256]{3,2,1,0:T(8,128)(2,1)S(1)} %all-to-all-done.refs_0_), custom_call_target="tpu_custom_call" | custom-call | flops 4294967296 | bytes 3145728 | tf_op jit(solution)/shard_map/long_conv/pallas_call | solution.py:302
  91.8 0.0 collective-permute-done.13.refs_1_
  91.8 0.0 collective-permute-done.14.refs_2_
  91.8 0.0 collective-permute-done.15.refs_3_
  91.8 5.4 %all-to-all-start.1 = ((bf16[16,64,256]{2,1,0:T(8,128)(2,1)}), bf16[16,64,256]{2,1,0:T(8,128)(2,1)}, u32[]{:S(2)}, u32[]{:S(2)}) async-start(bf16[16,64,256]{2,1,0:T(8,128)(2,1)} %get-tuple-element.71), calls=%async_computation.1 | async-start | bytes 1048576 | tf_op jit(solution)/shard_map/all_to_all | solution.py:436
  97.3 0.4 collective-permute-start.16
  97.7 1.7 %collective-permute-start.17 = (bf16[4,64,256]{2,1,0:T(8,128)(2,1)S(1)}, bf16[4,64,256]{2,1,0:T(8,128)(2,1)S(1)}, u32[]{:S(2)}, u32[]{:S(2)}) collective-permute-start(bf16[4,64,256]{2,1,0:T(8,128)(2,1)S(1)} %get-tuple-element.79), channel_id=1, source_target_pairs={{0,4},{2,6},{4,0},{6,2},{8,12},{10,14},{12,8},{14,10},{16,20},{18,... | collective-permute-start | bytes 393224 | tf_op jit(solution)/shard_map/ppermute | solution.py:114
  99.4 0.0 collective-permute-start.18
  99.4 0.0 collective-permute-done.16.refs_1_
  99.4 8.5 %collective-permute-done.17.refs_2_ = bf16[4,64,256]{2,1,0:T(8,128)(2,1)S(1)} collective-permute-done((bf16[4,64,256]{2,1,0:T(8,128)(2,1)S(1)}, bf16[4,64,256]{2,1,0:T(8,128)(2,1)S(1)}, u32[]{:S(2)}, u32[]{:S(2)}) %collective-permute-start.17) | collective-permute-done | bytes 131104 | tf_op jit(solution)/shard_map/ppermute | solution.py:114
  107.8 2.1 %collective-permute-done.18.refs_3_ = bf16[4,64,256]{2,1,0:T(8,128)(2,1)S(1)} collective-permute-done((bf16[4,64,256]{2,1,0:T(8,128)(2,1)S(1)}, bf16[4,64,256]{2,1,0:T(8,128)(2,1)S(1)}, u32[]{:S(2)}, u32[]{:S(2)}) %collective-permute-start.18) | collective-permute-done | bytes 131104 | tf_op jit(solution)/shard_map/ppermute | solution.py:114
  109.9 0.9 gated_squares.2
  110.9 0.0 copy-start.14
  110.9 0.8 all-to-all-done.1.refs_0_
  111.7 1.9 %gated_squares.3 = (f32[256,2048]{1,0:T(8,128)S(1)}, f32[8,256]{1,0:T(8,128)S(1)}) custom-call(s32[1]{0:T(128)} %constant.3.clone.1.at_ref, bf16[256,2048]{1,0:T(8,128)(2,1)S(1)} %copy-done, bf16[48,2048]{1,0:T(8,128)(2,1)S(1)} %collective-permute-done.refs_2_.refs_3_.halo_ref, f32[3,2048]{1,0:T(4,128)S(1)} %copy-done.7, ...), custom_call_target="tpu_custom_call", output_to_operand_aliasing={{0}: (6, {})} | custom-call | flops 1000 | bytes 1000 | tf_op jit(solution)/shard_map/gated_squares/pallas_call | solution.py:369
  113.7 1.5 %collective-permute-start.19 = (f32[8,256]{1,0:T(8,128)S(1)}, f32[8,256]{1,0:T(8,128)S(1)}, u32[]{:S(2)}, u32[]{:S(2)}) collective-permute-start(f32[8,256]{1,0:T(8,128)S(1)} %get-tuple-element.84.refs_0_), channel_id=1, source_target_pairs={{0,1},{1,0},{2,3},{3,2},{4,5},{5,4},{6,7},{7,6},{8,9},{9,8},{10,11... | collective-permute-start | bytes 24584 | tf_op jit(solution)/shard_map/ppermute | solution.py:476
  115.2 2.2 %collective-permute-done.19.refs_1_ = f32[8,256]{1,0:T(8,128)S(1)} collective-permute-done((f32[8,256]{1,0:T(8,128)S(1)}, f32[8,256]{1,0:T(8,128)S(1)}, u32[]{:S(2)}, u32[]{:S(2)}) %collective-permute-start.19) | collective-permute-done | bytes 8224 | tf_op jit(solution)/shard_map/ppermute | solution.py:476
  117.4 1.9 %normed.1 = bf16[256,2048]{1,0:T(8,128)(2,1)} custom-call(f32[256,2048]{1,0:T(8,128)S(1)} %get-tuple-element.83.gated_ref, f32[1,2048]{1,0:T(1,128)S(1)} %bitcast.2, f32[8,256]{1,0:T(8,128)S(1)} %get-tuple-element.84.refs_0_, f32[8,256]{1,0:T(8,128)S(1)} %collective-permute-done.19.refs_1_), custom_call_target="tpu_custom_call" | custom-call | flops 1000 | bytes 1000 | tf_op jit(solution)/shard_map/normed/pallas_call | solution.py:413
  (37 shorter events, 0.2 us)
Async XLA Ops:
  0.0 9.8 %copy-start.2 = (bf16[256,2048]{1,0:T(8,128)(2,1)S(1)}, bf16[256,2048]{1,0:T(8,128)(2,1)}, u32[]{:S(2)}) copy-start(bf16[256,2048]{1,0:T(8,128)(2,1)} %refs_2_.3) | copy-start | bytes 3145732
  0.0 9.8 %copy-start.1 = (bf16[256,2048]{1,0:T(8,128)(2,1)S(1)}, bf16[256,2048]{1,0:T(8,128)(2,1)}, u32[]{:S(2)}) copy-start(bf16[256,2048]{1,0:T(8,128)(2,1)} %refs_1_.5) | copy-start | bytes 3145732
  0.0 4.2 %copy-start.3 = (bf16[256,2048]{1,0:T(8,128)(2,1)S(1)}, bf16[256,2048]{1,0:T(8,128)(2,1)}, u32[]{:S(2)}) copy-start(bf16[256,2048]{1,0:T(8,128)(2,1)} %refs_0_.7) | copy-start | bytes 3145732
  0.0 9.8 %copy-start.9 = (f32[3,2048]{1,0:T(4,128)S(1)}, f32[3,2048]{1,0:T(4,128)}, u32[]{:S(2)}) copy-start(f32[3,2048]{1,0:T(4,128)} %refs_5_.1) | copy-start | bytes 73732
  0.0 9.8 %copy-start.8 = (f32[3,2048]{1,0:T(4,128)S(1)}, f32[3,2048]{1,0:T(4,128)}, u32[]{:S(2)}) copy-start(f32[3,2048]{1,0:T(4,128)} %refs_4_.3) | copy-start | bytes 73732
  1.8 8.0 %collective-permute-start = (bf16[48,2048]{1,0:T(8,128)(2,1)}, bf16[48,2048]{1,0:T(8,128)(2,1)S(1)}, u32[]{:S(2)}, u32[]{:S(2)}) collective-permute-start(bf16[48,2048]{1,0:T(8,128)(2,1)} %tails.1), channel_id=1, source_target_pairs={{0,2},{2,4},{4,6},{6,8},{8,10},{10,12},{12,14},{14,16},{16,18},{18... | collective-permute-start | bytes 589832 | tf_op jit(solution)/shard_map/ppermute | solution.py:32
  4.6 15.9 %collective-permute-start.1 = (bf16[4,1,64,256]{3,2,1,0:T(8,128)(2,1)S(1)}, bf16[4,1,64,256]{3,2,1,0:T(8,128)(2,1)S(1)}, u32[]{:S(2)}, u32[]{:S(2)}) collective-permute-start(bf16[4,1,64,256]{3,2,1,0:T(8,128)(2,1)S(1)} %get-tuple-element.46), channel_id=1, source_target_pairs={{0,8},{2,10},{4,12},{6,14},{8,0},{10,2},{12,4},{14,6},{16,24},{18,... | collective-permute-start | bytes 393224 | tf_op jit(solution)/shard_map/ppermute | solution.py:114
  7.2 14.1 %collective-permute-start.2 = (bf16[4,1,64,256]{3,2,1,0:T(8,128)(2,1)S(1)}, bf16[4,1,64,256]{3,2,1,0:T(8,128)(2,1)S(1)}, u32[]{:S(2)}, u32[]{:S(2)}) collective-permute-start(bf16[4,1,64,256]{3,2,1,0:T(8,128)(2,1)S(1)} %get-tuple-element.47), channel_id=1, source_target_pairs={{0,16},{2,18},{4,20},{6,22},{8,24},{10,26},{12,28},{14,30},{16,0},... | collective-permute-start | bytes 393224 | tf_op jit(solution)/shard_map/ppermute | solution.py:114
  9.8 11.5 %collective-permute-start.3 = (bf16[4,1,64,256]{3,2,1,0:T(8,128)(2,1)S(1)}, bf16[4,1,64,256]{3,2,1,0:T(8,128)(2,1)S(1)}, u32[]{:S(2)}, u32[]{:S(2)}) collective-permute-start(bf16[4,1,64,256]{3,2,1,0:T(8,128)(2,1)S(1)} %get-tuple-element.48), channel_id=1, source_target_pairs={{0,24},{2,26},{4,28},{6,30},{8,16},{10,18},{12,20},{14,22},{16,8},... | collective-permute-start | bytes 393224 | tf_op jit(solution)/shard_map/ppermute | solution.py:114
  11.6 19.5 %collective-permute-start.4 = (bf16[4,1,64,256]{3,2,1,0:T(8,128)(2,1)S(1)}, bf16[4,1,64,256]{3,2,1,0:T(8,128)(2,1)S(1)}, u32[]{:S(2)}, u32[]{:S(2)}) collective-permute-start(bf16[4,1,64,256]{3,2,1,0:T(8,128)(2,1)S(1)} %get-tuple-element.50), channel_id=1, source_target_pairs={{0,16},{2,18},{4,20},{6,22},{8,24},{10,26},{12,28},{14,30},{16,0},... | collective-permute-start | bytes 393224 | tf_op jit(solution)/shard_map/ppermute | solution.py:114
  15.7 17.1 %collective-permute-start.6 = (bf16[4,1,64,256]{3,2,1,0:T(8,128)(2,1)S(1)}, bf16[4,1,64,256]{3,2,1,0:T(8,128)(2,1)S(1)}, u32[]{:S(2)}, u32[]{:S(2)}) collective-permute-start(bf16[4,1,64,256]{3,2,1,0:T(8,128)(2,1)S(1)} %get-tuple-element.53), channel_id=1, source_target_pairs={{0,8},{2,10},{4,12},{6,14},{8,0},{10,2},{12,4},{14,6},{16,24},{18,... | collective-permute-start | bytes 393224 | tf_op jit(solution)/shard_map/ppermute | solution.py:114
  20.5 12.3 %collective-permute-start.7 = (bf16[4,1,64,256]{3,2,1,0:T(8,128)(2,1)S(1)}, bf16[4,1,64,256]{3,2,1,0:T(8,128)(2,1)S(1)}, u32[]{:S(2)}, u32[]{:S(2)}) collective-permute-start(bf16[4,1,64,256]{3,2,1,0:T(8,128)(2,1)S(1)} %get-tuple-element.54), channel_id=1, source_target_pairs={{0,24},{2,26},{4,28},{6,30},{8,16},{10,18},{12,20},{14,22},{16,8},... | collective-permute-start | bytes 393224 | tf_op jit(solution)/shard_map/ppermute | solution.py:114
  31.1 1.7 %copy-start.15 = (bf16[4,1,64,256]{3,2,1,0:T(8,128)(2,1)}, bf16[4,1,64,256]{3,2,1,0:T(8,128)(2,1)S(1)}, u32[]{:S(2)}) copy-start(bf16[4,1,64,256]{3,2,1,0:T(8,128)(2,1)S(1)} %get-tuple-element.59) | copy-start | bytes 393220
  31.2 1.6 %copy-start.16 = (bf16[4,1,64,256]{3,2,1,0:T(8,128)(2,1)}, bf16[4,1,64,256]{3,2,1,0:T(8,128)(2,1)S(1)}, u32[]{:S(2)}) copy-start(bf16[4,1,64,256]{3,2,1,0:T(8,128)(2,1)S(1)} %get-tuple-element.58) | copy-start | bytes 393220
  31.2 5.9 %copy-start.10 = (bf16[4,1,64,256]{3,2,1,0:T(8,128)(2,1)}, bf16[4,1,64,256]{3,2,1,0:T(8,128)(2,1)S(1)}, u32[]{:S(2)}) copy-start(bf16[4,1,64,256]{3,2,1,0:T(8,128)(2,1)S(1)} %get-tuple-element.57.refs_0_) | copy-start | bytes 393220
  31.2 5.9 %collective-permute-start.5 = (bf16[4,1,64,256]{3,2,1,0:T(8,128)(2,1)S(1)}, bf16[4,1,64,256]{3,2,1,0:T(8,128)(2,1)S(1)}, u32[]{:S(2)}, u32[]{:S(2)}) collective-permute-start(bf16[4,1,64,256]{3,2,1,0:T(8,128)(2,1)S(1)} %get-tuple-element.51), channel_id=1, source_target_pairs={{0,4},{2,6},{4,0},{6,2},{8,12},{10,14},{12,8},{14,10},{16,20},{18,... | collective-permute-start | bytes 393224 | tf_op jit(solution)/shard_map/ppermute | solution.py:114
  32.9 0.7 copy-start.12
  33.5 0.6 copy-start.17
  34.2 0.6 copy-start.19
  34.8 5.5 %collective-permute-start.8 = (bf16[4,1,64,256]{3,2,1,0:T(8,128)(2,1)S(1)}, bf16[4,1,64,256]{3,2,1,0:T(8,128)(2,1)S(1)}, u32[]{:S(2)}, u32[]{:S(2)}) collective-permute-start(bf16[4,1,64,256]{3,2,1,0:T(8,128)(2,1)S(1)} %get-tuple-element.55), channel_id=1, source_target_pairs={{0,4},{2,6},{4,0},{6,2},{8,12},{10,14},{12,8},{14,10},{16,20},{18,... | collective-permute-start | bytes 393224 | tf_op jit(solution)/shard_map/ppermute | solution.py:114
  40.3 1.4 %copy-start.5 = (bf16[4,1,64,256]{3,2,1,0:T(8,128)(2,1)}, bf16[4,1,64,256]{3,2,1,0:T(8,128)(2,1)S(1)}, u32[]{:S(2)}) copy-start(bf16[4,1,64,256]{3,2,1,0:T(8,128)(2,1)S(1)} %collective-permute-done.8.refs_7_.refs_6_) | copy-start | bytes 393220
  41.7 1.0 copy-start.4
  42.6 7.6 %copy-start.20 = (bf16[4,1,64,256]{3,2,1,0:T(8,128)(2,1)S(1)}, bf16[4,1,64,256]{3,2,1,0:T(8,128)(2,1)}, u32[]{:S(2)}) copy-start(bf16[4,1,64,256]{3,2,1,0:T(8,128)(2,1)} %copy-done.19) | copy-start | bytes 393220
  42.6 7.7 %copy-start.18 = (bf16[4,1,64,256]{3,2,1,0:T(8,128)(2,1)S(1)}, bf16[4,1,64,256]{3,2,1,0:T(8,128)(2,1)}, u32[]{:S(2)}) copy-start(bf16[4,1,64,256]{3,2,1,0:T(8,128)(2,1)} %copy-done.17) | copy-start | bytes 393220
  42.6 22.3 %copy-start.11 = (bf16[4,1,64,256]{3,2,1,0:T(8,128)(2,1)S(1)}, bf16[4,1,64,256]{3,2,1,0:T(8,128)(2,1)}, u32[]{:S(2)}) copy-start(bf16[4,1,64,256]{3,2,1,0:T(8,128)(2,1)} %copy-done.10) | copy-start | bytes 393220
  42.6 22.3 %copy-start.13 = (bf16[4,1,64,256]{3,2,1,0:T(8,128)(2,1)S(1)}, bf16[4,1,64,256]{3,2,1,0:T(8,128)(2,1)}, u32[]{:S(2)}) copy-start(bf16[4,1,64,256]{3,2,1,0:T(8,128)(2,1)} %copy-done.12) | copy-start | bytes 393220
  42.6 22.3 %copy-start.6 = (bf16[4,1,64,256]{3,2,1,0:T(8,128)(2,1)S(1)}, bf16[4,1,64,256]{3,2,1,0:T(8,128)(2,1)}, u32[]{:S(2)}) copy-start(bf16[4,1,64,256]{3,2,1,0:T(8,128)(2,1)} %copy-done.5) | copy-start | bytes 393220
  42.6 37.9 %all-to-all-start = ((bf16[16,2,64,256]{3,2,1,0:T(8,128)(2,1)}), bf16[16,2,64,256]{3,2,1,0:T(8,128)(2,1)S(1)}, u32[]{:S(2)}, u32[]{:S(2)}) async-start(bf16[16,2,64,256]{3,2,1,0:T(8,128)(2,1)} %copy-done.4), calls=%async_computation | async-start | bytes 2097152 | tf_op jit(solution)/shard_map/all_to_all | solution.py:436
  48.2 3.1 %collective-permute-start.9 = (bf16[4,1,64,256]{3,2,1,0:T(8,128)(2,1)}, bf16[4,1,64,256]{3,2,1,0:T(8,128)(2,1)S(1)}, u32[]{:S(2)}, u32[]{:S(2)}) collective-permute-start(bf16[4,1,64,256]{3,2,1,0:T(8,128)(2,1)} %copy-done.16), channel_id=1, source_target_pairs={{0,2},{2,0},{4,6},{6,4},{8,10},{10,8},{12,14},{14,12},{16,18},{18,... | collective-permute-start | bytes 393224 | tf_op jit(solution)/shard_map/ppermute | solution.py:114
  48.6 11.8 %collective-permute-start.10 = (bf16[4,1,64,256]{3,2,1,0:T(8,128)(2,1)}, bf16[4,1,64,256]{3,2,1,0:T(8,128)(2,1)S(1)}, u32[]{:S(2)}, u32[]{:S(2)}) collective-permute-start(bf16[4,1,64,256]{3,2,1,0:T(8,128)(2,1)} %copy-done.15), channel_id=1, source_target_pairs={{0,6},{2,4},{4,2},{6,0},{8,14},{10,12},{12,10},{14,8},{16,22},{18,... | collective-permute-start | bytes 393224 | tf_op jit(solution)/shard_map/ppermute | solution.py:114
  50.2 10.1 %collective-permute-start.11 = (bf16[4,1,64,256]{3,2,1,0:T(8,128)(2,1)S(1)}, bf16[4,1,64,256]{3,2,1,0:T(8,128)(2,1)S(1)}, u32[]{:S(2)}, u32[]{:S(2)}) collective-permute-start(bf16[4,1,64,256]{3,2,1,0:T(8,128)(2,1)S(1)} %copy-done.20), channel_id=1, source_target_pairs={{0,2},{2,0},{4,6},{6,4},{8,10},{10,8},{12,14},{14,12},{16,18},{18,... | collective-permute-start | bytes 393224 | tf_op jit(solution)/shard_map/ppermute | solution.py:114
  50.4 14.5 %collective-permute-start.12 = (bf16[4,1,64,256]{3,2,1,0:T(8,128)(2,1)S(1)}, bf16[4,1,64,256]{3,2,1,0:T(8,128)(2,1)S(1)}, u32[]{:S(2)}, u32[]{:S(2)}) collective-permute-start(bf16[4,1,64,256]{3,2,1,0:T(8,128)(2,1)S(1)} %copy-done.18), channel_id=1, source_target_pairs={{0,6},{2,4},{4,2},{6,0},{8,14},{10,12},{12,10},{14,8},{16,22},{18,... | collective-permute-start | bytes 393224 | tf_op jit(solution)/shard_map/ppermute | solution.py:114
  75.3 16.5 %collective-permute-start.13 = (bf16[4,64,256]{2,1,0:T(8,128)(2,1)S(1)}, bf16[4,64,256]{2,1,0:T(8,128)(2,1)S(1)}, u32[]{:S(2)}, u32[]{:S(2)}) collective-permute-start(bf16[4,64,256]{2,1,0:T(8,128)(2,1)S(1)} %get-tuple-element.64), channel_id=1, source_target_pairs={{0,8},{2,10},{4,12},{6,14},{8,0},{10,2},{12,4},{14,6},{16,24},{18,... | collective-permute-start | bytes 393224 | tf_op jit(solution)/shard_map/ppermute | solution.py:114
  75.4 16.5 %collective-permute-start.14 = (bf16[4,64,256]{2,1,0:T(8,128)(2,1)S(1)}, bf16[4,64,256]{2,1,0:T(8,128)(2,1)S(1)}, u32[]{:S(2)}, u32[]{:S(2)}) collective-permute-start(bf16[4,64,256]{2,1,0:T(8,128)(2,1)S(1)} %get-tuple-element.65), channel_id=1, source_target_pairs={{0,16},{2,18},{4,20},{6,22},{8,24},{10,26},{12,28},{14,30},{16,0},... | collective-permute-start | bytes 393224 | tf_op jit(solution)/shard_map/ppermute | solution.py:114
  80.6 11.2 %collective-permute-start.15 = (bf16[4,64,256]{2,1,0:T(8,128)(2,1)S(1)}, bf16[4,64,256]{2,1,0:T(8,128)(2,1)S(1)}, u32[]{:S(2)}, u32[]{:S(2)}) collective-permute-start(bf16[4,64,256]{2,1,0:T(8,128)(2,1)S(1)} %get-tuple-element.66), channel_id=1, source_target_pairs={{0,24},{2,26},{4,28},{6,30},{8,16},{10,18},{12,20},{14,22},{16,8},... | collective-permute-start | bytes 393224 | tf_op jit(solution)/shard_map/ppermute | solution.py:114
  80.7 29.3 %copy-start.7 = (f32[3,2048]{1,0:T(4,128)S(1)}, f32[3,2048]{1,0:T(4,128)}, u32[]{:S(2)}) copy-start(f32[3,2048]{1,0:T(4,128)} %taps_ref.3) | copy-start | bytes 73732
  91.8 18.1 %copy-start = (bf16[256,2048]{1,0:T(8,128)(2,1)S(1)}, bf16[256,2048]{1,0:T(8,128)(2,1)}, u32[]{:S(2)}) copy-start(bf16[256,2048]{1,0:T(8,128)(2,1)} %gate_ref.3) | copy-start | bytes 3145732
  91.8 19.9 %all-to-all-start.1 = ((bf16[16,64,256]{2,1,0:T(8,128)(2,1)}), bf16[16,64,256]{2,1,0:T(8,128)(2,1)}, u32[]{:S(2)}, u32[]{:S(2)}) async-start(bf16[16,64,256]{2,1,0:T(8,128)(2,1)} %get-tuple-element.71), calls=%async_computation.1 | async-start | bytes 1048576 | tf_op jit(solution)/shard_map/all_to_all | solution.py:436
  97.3 2.1 %collective-permute-start.16 = (bf16[4,64,256]{2,1,0:T(8,128)(2,1)S(1)}, bf16[4,64,256]{2,1,0:T(8,128)(2,1)S(1)}, u32[]{:S(2)}, u32[]{:S(2)}) collective-permute-start(bf16[4,64,256]{2,1,0:T(8,128)(2,1)S(1)} %get-tuple-element.78), channel_id=1, source_target_pairs={{0,2},{2,0},{4,6},{6,4},{8,10},{10,8},{12,14},{14,12},{16,18},{18,... | collective-permute-start | bytes 393224 | tf_op jit(solution)/shard_map/ppermute | solution.py:114
  97.7 10.2 %collective-permute-start.17 = (bf16[4,64,256]{2,1,0:T(8,128)(2,1)S(1)}, bf16[4,64,256]{2,1,0:T(8,128)(2,1)S(1)}, u32[]{:S(2)}, u32[]{:S(2)}) collective-permute-start(bf16[4,64,256]{2,1,0:T(8,128)(2,1)S(1)} %get-tuple-element.79), channel_id=1, source_target_pairs={{0,4},{2,6},{4,0},{6,2},{8,12},{10,14},{12,8},{14,10},{16,20},{18,... | collective-permute-start | bytes 393224 | tf_op jit(solution)/shard_map/ppermute | solution.py:114
  99.4 10.6 %collective-permute-start.18 = (bf16[4,64,256]{2,1,0:T(8,128)(2,1)S(1)}, bf16[4,64,256]{2,1,0:T(8,128)(2,1)S(1)}, u32[]{:S(2)}, u32[]{:S(2)}) collective-permute-start(bf16[4,64,256]{2,1,0:T(8,128)(2,1)S(1)} %get-tuple-element.80), channel_id=1, source_target_pairs={{0,6},{2,4},{4,2},{6,0},{8,14},{10,12},{12,10},{14,8},{16,22},{18,... | collective-permute-start | bytes 393224 | tf_op jit(solution)/shard_map/ppermute | solution.py:114
  110.9 6.5 %copy-start.14 = (f32[2048]{0:T(1024)S(1)}, f32[2048]{0:T(1024)}, u32[]{:S(2)}) copy-start(f32[2048]{0:T(1024)} %param.17) | copy-start | bytes 24580
  113.7 3.7 %collective-permute-start.19 = (f32[8,256]{1,0:T(8,128)S(1)}, f32[8,256]{1,0:T(8,128)S(1)}, u32[]{:S(2)}, u32[]{:S(2)}) collective-permute-start(f32[8,256]{1,0:T(8,128)S(1)} %get-tuple-element.84.refs_0_), channel_id=1, source_target_pairs={{0,1},{1,0},{2,3},{3,2},{4,5},{5,4},{6,7},{7,6},{8,9},{9,8},{10,11... | collective-permute-start | bytes 24584 | tf_op jit(solution)/shard_map/ppermute | solution.py:476
